TPU v7x, 256 devices: a whole 4x4x8 slice. The times are simulated.
256 devices in a mesh: gx: 8 (over z_hi, core), gy: 32 (over x, z_lo, y).
Axes of the slice: x: 4, y: 4, z: 8 (z_hi: 4, z_lo: 2; z = z_hi * 2 + z_lo), core: 2. Of those that a mesh axis runs over, the one named last changes fastest.
Arguments:
- volume: float32 [192, 1024, 128], P('gx', 'gy'), may hold values from -12 to 12
Outputs:
- throat: float32 [192, 1024, 128], P('gx', 'gy')
All inputs are finite; a program needn't handle non-finite values.
Results may differ from a plain program's by a relative error of at most 0.0003.
Values sent between devices are 32-bit elements; how exact they have to be, the bound alone decides.
No kernel may reach another device: no remote copies, remote signals or barrier semaphores. Data moves between devices by JAX's collectives and lax.ppermute only.
A program may use at most 64 MiB of HBM per device.

v0:
```python
import jax
import jax.numpy as jnp
import ml_dtypes
import numpy as np
from jax import lax
from jax.experimental import pallas as pl
from jax.experimental.pallas import tpu as pltpu
from jax.sharding import PartitionSpec as P

scale_list = (8.0, 4.0, 2.0, 1.0)
radius_list = (24, 12, 6, 3)
x_axes = ("zh", "core")
y_axes = ("x", "zl", "y")
rim = 24
tile_x, tile_y, depth = 24, 32, 128
wide_y = tile_y + 2 * rim
x_span = ((0, 80), (12, 48), (12, 48), (20, 32))
rows = tile_x * tile_y
z_rows = 96
score_rows = 192
mib = 1024 * 1024


def taps(scale, radius):
    t = np.arange(-radius, radius + 1).astype(np.float64)
    bell = np.exp(-t * t / (2.0 * scale * scale))
    w0 = bell / bell.sum()
    w1 = -t / (scale * scale) * w0
    w2 = (t * t / scale**4 - 1.0 / (scale * scale)) * w0
    return w0, w1, w2


def band(weights, radius, n_out, n_in, offset):
    lag = np.arange(n_out)[:, None] + offset - np.arange(n_in)[None, :]
    return np.where(np.abs(lag) <= radius, weights[np.clip(lag + radius, 0, 2 * radius)], 0.0)


def split(matrix):
    hi = matrix.astype(np.float32).astype(ml_dtypes.bfloat16)
    lo = (matrix - hi.astype(np.float64)).astype(np.float32).astype(ml_dtypes.bfloat16)
    return hi, lo


def constants():
    y_parts, x_parts, z_parts = [], [], []
    for scale, radius, (first, count) in zip(scale_list, radius_list, x_span):
        w = taps(scale, radius)
        y_parts += [band(v, radius, tile_y, wide_y, rim) for v in w]
        xb = np.concatenate([band(v, radius, tile_x, count, rim - first) for v in w])
        hi, lo = split(xb)
        x_parts.append(np.concatenate([hi, hi, lo], axis=1))
        for v in w:
            hi, lo = split(band(v * scale * scale, radius, depth, depth, 0).T)
            z_parts.append(
                np.concatenate(
                    [np.concatenate([hi, lo], axis=1), np.concatenate([hi, 0 * lo], axis=1)]
                )
            )
    hi, lo = split(np.concatenate(y_parts))
    y_all = np.concatenate([hi, hi, lo, np.zeros((hi.shape[0], 16), hi.dtype)], axis=1)
    return y_all, x_parts, np.stack(z_parts)


def halves(value):
    hi = value.astype(jnp.bfloat16)
    lo = (value - hi.astype(jnp.float32)).astype(jnp.bfloat16)
    return hi, lo


def dot(a, b):
    return jnp.dot(a, b, preferred_element_type=jnp.float32)


def filter_kernel(core_ref, *refs):
    sources, refs = refs[:8], refs[8:]
    wy, wx8, wx4, wx2, wx1, wz, stats_out, peaks, f8, f4, f2, f1, mixed, stats = refs[:14]
    held, in_sems, out_sems = refs[14:22], refs[22], refs[23]
    mid, pair, far, mid_lo, mid_hi, pair_y, far_lo, far_hi = held
    loads = [
        pltpu.make_async_copy(a, b, in_sems.at[i]) for i, (a, b) in enumerate(zip(sources, held))
    ]
    for i in (0, 3, 4, 1, 5, 2, 6, 7):
        loads[i].start()
    fields = (f8, f4, f2, f1)
    x_bands = (wx8, wx4, wx2, wx1)
    core = core_ref[0]
    f8[pl.ds(72 * 96, 8 * 96), :] = jnp.zeros((8 * 96, depth), jnp.float32)
    zeros16 = jnp.zeros((16, 2 * depth), jnp.bfloat16)

    def y_step(parts, plane, out_plane, levels):
        low, centre, high = parts(plane)
        both = jnp.concatenate([low, centre, high], axis=1)
        both = jnp.concatenate([both[0], both[1]], axis=1)
        hi, lo = halves(both)
        data = jnp.concatenate([hi, lo, hi, zeros16], axis=0)
        out = dot(wy[0 : 96 * levels, :], data)
        for level in range(levels):
            block = out[96 * level : 96 * level + 96]
            for k in range(2):
                at = pl.multiple_of((out_plane + k - x_span[level][0]) * 96, 96)
                fields[level][pl.ds(at, 96), :] = block[:, depth * k : depth * (k + 1)]

    def mid_parts(plane):
        at = pl.ds(plane, 2)
        return mid_lo[at], mid[at], mid_hi[at]

    def pair_parts(plane):
        at = pl.ds(plane, 2)
        return pair_y[at, 0:rim], pair[at], pair_y[at, rim : 2 * rim]

    def far_parts(plane):
        at = pl.ds(plane, 2)
        return far_lo[at], far[at], far_hi[at]

    def mid_body(i, carry):
        y_step(mid_parts, 2 * i, rim + 2 * i, 4)
        return carry

    for i in (0, 3, 4):
        loads[i].wait()
    lax.fori_loop(0, 12, mid_body, 0, unroll=2)

    sides = ((pair_parts, core, (1, 5)), (far_parts, 1 - core, (2, 6, 7)))
    for parts, before, needed in sides:
        for i in needed:
            loads[i].wait()
        for start, stop, levels in ((0, 2, 4), (2, 6, 3), (6, 12, 1)):

            def side_body(j, carry, parts=parts, before=before, levels=levels):
                i = j + before * (11 - 2 * j)
                y_step(parts, 2 * i, 2 * i + 48 * (1 - before), levels)
                return carry

            lax.fori_loop(start, stop, side_body, 0, unroll=2)

    peak_rows, stores = [], []
    for level in range(4):
        field, x_band = fields[level], x_bands[level]
        count = x_span[level][1]

        def x_body(yp, carry, field=field, x_band=x_band, count=count):
            at = pl.ds(pl.multiple_of(48 * yp, 48), 48)
            for f, first, outs in ((0, 0, 3), (1, 3, 2), (2, 5, 1)):
                pieces = [
                    field[pl.ds(32 * f + 2 * yp + k, count, stride=96), :] for k in range(2)
                ]
                hi, lo = halves(jnp.concatenate(pieces, axis=1))
                data = jnp.concatenate([hi, lo, hi], axis=0)
                out = dot(x_band[0 : 24 * outs, :], data)
                for k in range(outs):
                    u = out[24 * k : 24 * k + 24]
                    u = jnp.concatenate([u[:, :depth], u[:, depth:]], axis=0)
                    hi, lo = halves(u)
                    mixed[first + k, at, 0:depth] = hi
                    mixed[first + k, at, depth : 2 * depth] = lo
            return carry

        lax.fori_loop(0, tile_y // 2, x_body, 0, unroll=2)

        def z_body(c, best, level=level):
            at = pl.ds(pl.multiple_of(c * z_rows, z_rows), z_rows)

            def z_pass(order, chosen):
                data = jnp.concatenate([mixed[p, at, :] for p in chosen], axis=0)
                out = dot(data, wz[3 * level + order])
                out = out[:, :depth] + out[:, depth:]
                return [out[z_rows * k : z_rows * (k + 1)] for k in range(len(chosen))]

            (zz,) = z_pass(2, (0,))
            yz, xz = z_pass(1, (3, 1))
            yy, xy, xx = z_pass(0, (5, 4, 2))
            sq = xy * xy + xz * xz + yz * yz
            stats[3 * level, at, :] = xx + yy + zz
            stats[3 * level + 1, at, :] = xx * yy + (xx + yy) * zz - sq
            energy = xx * xx + yy * yy + zz * zz + 2.0 * sq
            stats[3 * level + 2, at, :] = energy
            return jnp.maximum(best, jnp.max(energy.reshape(z_rows // 8, 8, depth), axis=0))

        best = lax.fori_loop(0, rows // z_rows, z_body, jnp.zeros((8, depth), jnp.float32), unroll=2)
        at = pl.ds(3 * level, 3)
        stores.append(pltpu.make_async_copy(stats.at[at], stats_out.at[at], out_sems.at[level]))
        stores[-1].start()
        peak_rows.append(jnp.broadcast_to(jnp.max(best), (1, depth)))
    peaks[...] = jnp.concatenate(peak_rows + peak_rows, axis=0)
    for store in stores:
        store.wait()


def score_kernel(stats, peaks, throat, flat):
    step = pl.program_id(0)
    for c in range(score_rows // 24):
        at = pl.ds(24 * c, 24)
        best = None
        for level in range(4):
            trace_sum = stats[3 * level, at, :]
            minors = stats[3 * level + 1, at, :]
            energy = stats[3 * level + 2, at, :]
            spread = 0.25 * peaks[pl.ds(level, 1), :] + 1e-06
            guard = energy + 0.1 * spread
            ratio = minors / guard
            score = (
                (1.0 - jnp.exp(energy * (-0.5 / spread)))
                * jnp.exp(-2.0 * ratio * ratio)
                / (1.0 + jnp.exp(4.0 * trace_sum * lax.rsqrt(guard)))
            )
            best = score if best is None else jnp.maximum(best, score)
        flat[pl.ds(pl.multiple_of(step * score_rows + 24 * c, 8), 24), :] = best

    @pl.when(step == rows // score_rows - 1)
    def _():
        for i in range(tile_x):
            throat[i] = flat[pl.ds(i, tile_y, stride=tile_x), :]


def hbm(n):
    return [pl.BlockSpec(memory_space=pl.ANY)] * n


def vmem(n):
    return [pl.BlockSpec(memory_space=pltpu.VMEM)] * n


def filter_call(core, pieces, interpret=False):
    y_all, x_parts, z_all = constants()
    return pl.pallas_call(
        filter_kernel,
        out_shape=(
            jax.ShapeDtypeStruct((12, rows, depth), jnp.float32),
            jax.ShapeDtypeStruct((8, depth), jnp.float32),
        ),
        in_specs=[pl.BlockSpec(memory_space=pltpu.SMEM)] + hbm(8) + vmem(6),
        out_specs=(*hbm(1), *vmem(1)),
        scratch_shapes=[pltpu.VMEM((count * 96, depth), jnp.float32) for _, count in x_span]
        + [
            pltpu.VMEM((6, rows, 2 * depth), jnp.bfloat16),
            pltpu.VMEM((12, rows, depth), jnp.float32),
        ]
        + [pltpu.VMEM(piece.shape, jnp.float32) for piece in pieces]
        + [pltpu.SemaphoreType.DMA((8,)), pltpu.SemaphoreType.DMA((4,))],
        compiler_params=pltpu.CompilerParams(vmem_limit_bytes=40 * mib),
        interpret=interpret,
    )(core, *pieces, jnp.asarray(y_all), *[jnp.asarray(v) for v in x_parts], jnp.asarray(z_all))


def score_call(stats, peaks, interpret=False):
    return pl.pallas_call(
        score_kernel,
        out_shape=jax.ShapeDtypeStruct((tile_x, tile_y, depth), jnp.float32),
        grid=(rows // score_rows,),
        in_specs=[
            pl.BlockSpec((12, score_rows, depth), lambda i: (0, i, 0)),
            pl.BlockSpec((8, depth), lambda i: (0, 0)),
        ],
        out_specs=pl.BlockSpec((tile_x, tile_y, depth), lambda i: (0, 0, 0)),
        scratch_shapes=[pltpu.VMEM((rows, depth), jnp.float32)],
        compiler_params=pltpu.CompilerParams(vmem_limit_bytes=24 * mib),
        interpret=interpret,
    )(stats, peaks)


def global_max(block):
    for axis, step in (
        ("core", 1), ("y", 1), ("y", 2), ("x", 1), ("x", 2), ("zl", 1), ("zh", 1), ("zh", 2),
    ):
        pairs = [(i, i ^ step) for i in range(lax.axis_size(axis))]
        block = jnp.maximum(block, lax.ppermute(block, axis, pairs))
    return block


def per_device(volume):
    n_x, n_y = lax.axis_size(x_axes), lax.axis_size(y_axes)
    pair_perm = [(i, i ^ 1) for i in range(n_x)]
    far_perm = [(i, i + 1) for i in range(1, n_x - 1, 2)]
    far_perm += [(j, i) for i, j in far_perm]
    up = [(i, i + 1) for i in range(n_y - 1)]
    down = [(j, i) for i, j in up]
    tail, head = slice(tile_y - rim, tile_y), slice(0, rim)

    far = lax.ppermute(volume, x_axes, far_perm)
    mid_lo = lax.ppermute(volume[:, tail], y_axes, up)
    mid_hi = lax.ppermute(volume[:, head], y_axes, down)
    pair = lax.ppermute(volume, x_axes, pair_perm)
    far_lo = lax.ppermute(far[:, tail], y_axes, up)
    far_hi = lax.ppermute(far[:, head], y_axes, down)
    pair_y = lax.ppermute(jnp.concatenate([mid_lo, mid_hi], axis=1), x_axes, pair_perm)

    core = lax.axis_index("core").reshape(1)
    pieces = (volume, pair, far, mid_lo, mid_hi, pair_y, far_lo, far_hi)
    stats, peaks = filter_call(core, pieces)
    return score_call(stats, global_max(peaks))


def solution(mesh):
    fine = jax.sharding.Mesh(
        mesh.devices.reshape(4, 2, 4, 2, 4), ("zh", "core", "x", "zl", "y")
    )
    spec = P(x_axes, y_axes, None)
    return jax.shard_map(
        per_device, mesh=fine, in_specs=(spec,), out_specs=spec, check_vma=False
    )
```

profile of v0, /device:TPU:6, one launch (start us, length us, event | category | flops | bytes accessed | tf_op | source)
XLA Modules:
  0.0 112.7 jit_solution(3984482063997095357)
XLA Ops:
  0.0 1.1 fusion.1
  1.1 6.5 %collective-permute-start.3 = (f32[24,24,128]{2,1,0:T(8,128)S(1)}, f32[24,24,128]{2,1,0:T(8,128)S(1)}, u32[]{:S(2)}, u32[]{:S(2)}) collective-permute-start(f32[24,24,128]{2,1,0:T(8,128)S(1)} %get-tuple-element.11), channel_id=1, source_target_pairs={{1,0},{2,1},{3,2},{4,3},{5,4},{6,5},{7,6},{8,7},{9,8},{10,9},{11,1... | collective-permute-start | bytes 884744 | tf_op jit(solution)/shard_map/ppermute | solution.py:281
  7.6 1.9 %collective-permute-start.2 = (f32[24,24,128]{2,1,0:T(8,128)S(1)}, f32[24,24,128]{2,1,0:T(8,128)S(1)}, u32[]{:S(2)}, u32[]{:S(2)}) collective-permute-start(f32[24,24,128]{2,1,0:T(8,128)S(1)} %get-tuple-element.12), channel_id=1, source_target_pairs={{0,1},{1,2},{2,3},{3,4},{4,5},{5,6},{6,7},{7,8},{8,9},{9,10},{10,1... | collective-permute-start | bytes 884744 | tf_op jit(solution)/shard_map/ppermute | solution.py:280
  9.6 0.7 collective-permute-start.1
  10.3 3.6 %collective-permute-done.3.refs_4_ = f32[24,24,128]{2,1,0:T(8,128)S(1)} collective-permute-done((f32[24,24,128]{2,1,0:T(8,128)S(1)}, f32[24,24,128]{2,1,0:T(8,128)S(1)}, u32[]{:S(2)}, u32[]{:S(2)}) %collective-permute-start.3) | collective-permute-done | bytes 294944 | tf_op jit(solution)/shard_map/ppermute | solution.py:281
  13.9 11.3 %collective-permute-done.2.refs_3_ = f32[24,24,128]{2,1,0:T(8,128)S(1)} collective-permute-done((f32[24,24,128]{2,1,0:T(8,128)S(1)}, f32[24,24,128]{2,1,0:T(8,128)S(1)}, u32[]{:S(2)}, u32[]{:S(2)}) %collective-permute-start.2) | collective-permute-done | bytes 294944 | tf_op jit(solution)/shard_map/ppermute | solution.py:280
  25.9 0.8 fusion
  26.6 1.9 %collective-permute-start.6 = (f32[24,24,128]{2,1,0:T(8,128)}, f32[24,24,128]{2,1,0:T(8,128)S(1)}, u32[]{:S(2)}, u32[]{:S(2)}) collective-permute-start(f32[24,24,128]{2,1,0:T(8,128)} %get-tuple-element.9), channel_id=1, source_target_pairs={{1,0},{2,1},{3,2},{4,3},{5,4},{6,5},{7,6},{8,7},{9,8},{10,9},{11,1... | collective-permute-start | bytes 884744 | tf_op jit(solution)/shard_map/ppermute | solution.py:284
  28.5 3.9 %collective-permute-start.5 = (f32[24,24,128]{2,1,0:T(8,128)S(1)}, f32[24,24,128]{2,1,0:T(8,128)S(1)}, u32[]{:S(2)}, u32[]{:S(2)}) collective-permute-start(f32[24,24,128]{2,1,0:T(8,128)S(1)} %get-tuple-element.10), channel_id=1, source_target_pairs={{0,1},{1,2},{2,3},{3,4},{4,5},{5,6},{6,7},{7,8},{8,9},{9,10},{10,1... | collective-permute-start | bytes 884744 | tf_op jit(solution)/shard_map/ppermute | solution.py:283
  32.5 5.2 %collective-permute-done.6.refs_7_ = f32[24,24,128]{2,1,0:T(8,128)S(1)} collective-permute-done((f32[24,24,128]{2,1,0:T(8,128)}, f32[24,24,128]{2,1,0:T(8,128)S(1)}, u32[]{:S(2)}, u32[]{:S(2)}) %collective-permute-start.6) | collective-permute-done | bytes 294944 | tf_op jit(solution)/shard_map/ppermute | solution.py:284
  37.7 2.4 %collective-permute-done.5.refs_6_ = f32[24,24,128]{2,1,0:T(8,128)S(1)} collective-permute-done((f32[24,24,128]{2,1,0:T(8,128)S(1)}, f32[24,24,128]{2,1,0:T(8,128)S(1)}, u32[]{:S(2)}, u32[]{:S(2)}) %collective-permute-start.5) | collective-permute-done | bytes 294944 | tf_op jit(solution)/shard_map/ppermute | solution.py:283
  40.2 1.0 copy-done
  41.2 1.4 %copy-done.1 = bf16[12,256,256]{2,1,0:T(8,128)(2,1)S(1)} copy-done((bf16[12,256,256]{2,1,0:T(8,128)(2,1)S(1)}, bf16[12,256,256]{2,1,0:T(8,128)(2,1)}, u32[]{:S(2)}) %copy-start.1) | copy-done | bytes 1572888
  42.6 0.9 copy-done.2
  43.5 0.8 copy-done.3
  44.3 0.8 copy-done.4
  45.0 0.8 copy-done.5
  45.8 0.7 copy-done.6
  46.5 23.0 %shard_map.73 = (f32[12,768,128]{2,1,0:T(8,128)S(1)}, f32[8,128]{1,0:T(8,128)S(1)}) custom-call(s32[1]{0:T(128)} %bitcast.core_ref, f32[24,32,128]{2,1,0:T(8,128)S(1)} %copy-done, f32[24,32,128]{2,1,0:T(8,128)S(1)} %collective-permute-done.refs_1_, f32[24,32,128]{2,1,0:T(8,128)S(1)} %collective-permute-done.1.refs_2_, ...), custom_call_target="tpu_custom_call" | custom-call | tf_op jit(solution)/shard_map/pallas_call | solution.py:225
  69.6 5.3 %collective-permute-start.7 = (f32[8,128]{1,0:T(8,128)S(1)}, f32[8,128]{1,0:T(8,128)S(1)}, u32[]{:S(2)}, u32[]{:S(2)}) collective-permute-start(f32[8,128]{1,0:T(8,128)S(1)} %get-tuple-element.8), channel_id=1, source_target_pairs={{0,32},{32,0},{1,33},{33,1},{2,34},{34,2},{3,35},{35,3},{4,36},{36... | collective-permute-start | bytes 12296 | tf_op jit(solution)/shard_map/ppermute | solution.py:266
  74.9 0.8 collective-permute-done.7
  75.7 3.6 %collective-permute-done.8 = f32[8,128]{1,0:T(8,128)S(1)} collective-permute-done((f32[8,128]{1,0:T(8,128)S(1)}, f32[8,128]{1,0:T(8,128)S(1)}, u32[]{:S(2)}, u32[]{:S(2)}) %collective-permute-start.8) | collective-permute-done | bytes 4128 | tf_op jit(solution)/shard_map/ppermute | solution.py:266
  79.3 5.1 %collective-permute-done.9 = f32[8,128]{1,0:T(8,128)S(1)} collective-permute-done((f32[8,128]{1,0:T(8,128)S(1)}, f32[8,128]{1,0:T(8,128)S(1)}, u32[]{:S(2)}, u32[]{:S(2)}) %collective-permute-start.9) | collective-permute-done | bytes 4128 | tf_op jit(solution)/shard_map/ppermute | solution.py:266
  85.0 3.1 %collective-permute-done.10 = f32[8,128]{1,0:T(8,128)S(1)} collective-permute-done((f32[8,128]{1,0:T(8,128)S(1)}, f32[8,128]{1,0:T(8,128)S(1)}, u32[]{:S(2)}, u32[]{:S(2)}) %collective-permute-start.10) | collective-permute-done | bytes 4128 | tf_op jit(solution)/shard_map/ppermute | solution.py:266
  88.1 1.1 collective-permute-start.11
  89.2 4.0 %collective-permute-done.11 = f32[8,128]{1,0:T(8,128)S(1)} collective-permute-done((f32[8,128]{1,0:T(8,128)S(1)}, f32[8,128]{1,0:T(8,128)S(1)}, u32[]{:S(2)}, u32[]{:S(2)}) %collective-permute-start.11) | collective-permute-done | bytes 4128 | tf_op jit(solution)/shard_map/ppermute | solution.py:266
  93.2 3.6 %collective-permute-done.12 = f32[8,128]{1,0:T(8,128)S(1)} collective-permute-done((f32[8,128]{1,0:T(8,128)S(1)}, f32[8,128]{1,0:T(8,128)S(1)}, u32[]{:S(2)}, u32[]{:S(2)}) %collective-permute-start.12) | collective-permute-done | bytes 4128 | tf_op jit(solution)/shard_map/ppermute | solution.py:266
  96.8 4.2 %collective-permute-start.13 = (f32[8,128]{1,0:T(8,128)S(1)}, f32[8,128]{1,0:T(8,128)S(1)}, u32[]{:S(2)}, u32[]{:S(2)}) collective-permute-start(f32[8,128]{1,0:T(8,128)S(1)} %max.29), channel_id=1, source_target_pairs={{0,64},{64,0},{128,192},{192,128},{1,65},{65,1},{129,193},{193,129... | collective-permute-start | bytes 12296 | tf_op jit(solution)/shard_map/ppermute | solution.py:266
  101.0 1.6 %collective-permute-done.13 = f32[8,128]{1,0:T(8,128)S(1)} collective-permute-done((f32[8,128]{1,0:T(8,128)S(1)}, f32[8,128]{1,0:T(8,128)S(1)}, u32[]{:S(2)}, u32[]{:S(2)}) %collective-permute-start.13) | collective-permute-done | bytes 4128 | tf_op jit(solution)/shard_map/ppermute | solution.py:266
  102.6 4.0 %collective-permute-start.14 = (f32[8,128]{1,0:T(8,128)S(1)}, f32[8,128]{1,0:T(8,128)S(1)}, u32[]{:S(2)}, u32[]{:S(2)}) collective-permute-start(f32[8,128]{1,0:T(8,128)S(1)} %max.30), channel_id=1, source_target_pairs={{0,128},{64,192},{128,0},{192,64},{1,129},{65,193},{129,1},{193,65... | collective-permute-start | bytes 12296 | tf_op jit(solution)/shard_map/ppermute | solution.py:266
  106.7 3.5 %collective-permute-done.14 = f32[8,128]{1,0:T(8,128)S(1)} collective-permute-done((f32[8,128]{1,0:T(8,128)S(1)}, f32[8,128]{1,0:T(8,128)S(1)}, u32[]{:S(2)}, u32[]{:S(2)}) %collective-permute-start.14) | collective-permute-done | bytes 4128 | tf_op jit(solution)/shard_map/ppermute | solution.py:266
  110.2 2.5 %shard_map.74 = f32[24,32,128]{2,1,0:T(8,128)} custom-call(f32[12,768,128]{2,1,0:T(8,128)S(1)} %get-tuple-element.7.stats, f32[8,128]{1,0:T(8,128)S(1)} %max.31.peaks), custom_call_target="tpu_custom_call" | custom-call | tf_op jit(solution)/shard_map/pallas_call | solution.py:246
  (25 shorter events, 1.2 us)
Async XLA Ops:
  1.1 12.8 %collective-permute-start.3 = (f32[24,24,128]{2,1,0:T(8,128)S(1)}, f32[24,24,128]{2,1,0:T(8,128)S(1)}, u32[]{:S(2)}, u32[]{:S(2)}) collective-permute-start(f32[24,24,128]{2,1,0:T(8,128)S(1)} %get-tuple-element.11), channel_id=1, source_target_pairs={{1,0},{2,1},{3,2},{4,3},{5,4},{6,5},{7,6},{8,7},{9,8},{10,9},{11,1... | collective-permute-start | bytes 884744 | tf_op jit(solution)/shard_map/ppermute | solution.py:281
  7.6 17.6 %collective-permute-start.2 = (f32[24,24,128]{2,1,0:T(8,128)S(1)}, f32[24,24,128]{2,1,0:T(8,128)S(1)}, u32[]{:S(2)}, u32[]{:S(2)}) collective-permute-start(f32[24,24,128]{2,1,0:T(8,128)S(1)} %get-tuple-element.12), channel_id=1, source_target_pairs={{0,1},{1,2},{2,3},{3,4},{4,5},{5,6},{6,7},{7,8},{8,9},{9,10},{10,1... | collective-permute-start | bytes 884744 | tf_op jit(solution)/shard_map/ppermute | solution.py:280
  9.6 16.3 %collective-permute-start.1 = (f32[24,32,128]{2,1,0:T(8,128)}, f32[24,32,128]{2,1,0:T(8,128)S(1)}, u32[]{:S(2)}, u32[]{:S(2)}) collective-permute-start(f32[24,32,128]{2,1,0:T(8,128)} %refs_0_.1), channel_id=1, source_target_pairs={{32,64},{96,128},{160,192},{64,32},{128,96},{192,160},{33,65},{97,... | collective-permute-start | bytes 1179656 | tf_op jit(solution)/shard_map/ppermute | solution.py:279
  25.3 14.9 %collective-permute-start.4 = (f32[24,48,128]{2,1,0:T(8,128)S(1)}, f32[24,48,128]{2,1,0:T(8,128)S(1)}, u32[]{:S(2)}, u32[]{:S(2)}) collective-permute-start(f32[24,48,128]{2,1,0:T(8,128)S(1)} %pad_maximum_fusion), channel_id=1, source_target_pairs={{0,32},{32,0},{64,96},{96,64},{128,160},{160,128},{192,224},{224,1... | collective-permute-start | bytes 1769480 | tf_op jit(solution)/shard_map/ppermute | solution.py:285
  25.4 7.1 %collective-permute-start = (f32[24,32,128]{2,1,0:T(8,128)}, f32[24,32,128]{2,1,0:T(8,128)S(1)}, u32[]{:S(2)}, u32[]{:S(2)}) collective-permute-start(f32[24,32,128]{2,1,0:T(8,128)} %refs_0_.1), channel_id=1, source_target_pairs={{0,32},{32,0},{64,96},{96,64},{128,160},{160,128},{192,224},{224,1... | collective-permute-start | bytes 1179656 | tf_op jit(solution)/shard_map/ppermute | solution.py:282
  26.6 11.1 %collective-permute-start.6 = (f32[24,24,128]{2,1,0:T(8,128)}, f32[24,24,128]{2,1,0:T(8,128)S(1)}, u32[]{:S(2)}, u32[]{:S(2)}) collective-permute-start(f32[24,24,128]{2,1,0:T(8,128)} %get-tuple-element.9), channel_id=1, source_target_pairs={{1,0},{2,1},{3,2},{4,3},{5,4},{6,5},{7,6},{8,7},{9,8},{10,9},{11,1... | collective-permute-start | bytes 884744 | tf_op jit(solution)/shard_map/ppermute | solution.py:284
  28.5 11.6 %collective-permute-start.5 = (f32[24,24,128]{2,1,0:T(8,128)S(1)}, f32[24,24,128]{2,1,0:T(8,128)S(1)}, u32[]{:S(2)}, u32[]{:S(2)}) collective-permute-start(f32[24,24,128]{2,1,0:T(8,128)S(1)} %get-tuple-element.10), channel_id=1, source_target_pairs={{0,1},{1,2},{2,3},{3,4},{4,5},{5,6},{6,7},{7,8},{8,9},{9,10},{10,1... | collective-permute-start | bytes 884744 | tf_op jit(solution)/shard_map/ppermute | solution.py:283
  40.2 1.0 copy-start
  41.2 1.4 %copy-start.1 = (bf16[12,256,256]{2,1,0:T(8,128)(2,1)S(1)}, bf16[12,256,256]{2,1,0:T(8,128)(2,1)}, u32[]{:S(2)}) copy-start(bf16[12,256,256]{2,1,0:T(8,128)(2,1)} %constant.23.clone.refs_13_) | copy-start | bytes 4718596
  42.6 0.9 copy-start.2
  43.5 0.8 copy-start.3
  44.3 0.8 copy-start.4
  45.0 0.8 copy-start.5
  45.8 0.7 copy-start.6
  69.6 6.1 %collective-permute-start.7 = (f32[8,128]{1,0:T(8,128)S(1)}, f32[8,128]{1,0:T(8,128)S(1)}, u32[]{:S(2)}, u32[]{:S(2)}) collective-permute-start(f32[8,128]{1,0:T(8,128)S(1)} %get-tuple-element.8), channel_id=1, source_target_pairs={{0,32},{32,0},{1,33},{33,1},{2,34},{34,2},{3,35},{35,3},{4,36},{36... | collective-permute-start | bytes 12296 | tf_op jit(solution)/shard_map/ppermute | solution.py:266
  75.7 3.6 %collective-permute-start.8 = (f32[8,128]{1,0:T(8,128)S(1)}, f32[8,128]{1,0:T(8,128)S(1)}, u32[]{:S(2)}, u32[]{:S(2)}) collective-permute-start(f32[8,128]{1,0:T(8,128)S(1)} %max.24), channel_id=1, source_target_pairs={{0,1},{1,0},{2,3},{3,2},{4,5},{5,4},{6,7},{7,6},{8,9},{9,8},{10,11... | collective-permute-start | bytes 12296 | tf_op jit(solution)/shard_map/ppermute | solution.py:266
  79.3 5.1 %collective-permute-start.9 = (f32[8,128]{1,0:T(8,128)S(1)}, f32[8,128]{1,0:T(8,128)S(1)}, u32[]{:S(2)}, u32[]{:S(2)}) collective-permute-start(f32[8,128]{1,0:T(8,128)S(1)} %max.25), channel_id=1, source_target_pairs={{0,2},{1,3},{2,0},{3,1},{4,6},{5,7},{6,4},{7,5},{8,10},{9,11},{10,... | collective-permute-start | bytes 12296 | tf_op jit(solution)/shard_map/ppermute | solution.py:266
  84.4 3.6 %collective-permute-start.10 = (f32[8,128]{1,0:T(8,128)S(1)}, f32[8,128]{1,0:T(8,128)S(1)}, u32[]{:S(2)}, u32[]{:S(2)}) collective-permute-start(f32[8,128]{1,0:T(8,128)S(1)} %max.26), channel_id=1, source_target_pairs={{0,8},{8,0},{16,24},{24,16},{1,9},{9,1},{17,25},{25,17},{2,10},{10... | collective-permute-start | bytes 12296 | tf_op jit(solution)/shard_map/ppermute | solution.py:266
  88.1 5.1 %collective-permute-start.11 = (f32[8,128]{1,0:T(8,128)S(1)}, f32[8,128]{1,0:T(8,128)S(1)}, u32[]{:S(2)}, u32[]{:S(2)}) collective-permute-start(f32[8,128]{1,0:T(8,128)S(1)} %max.27), channel_id=1, source_target_pairs={{0,16},{8,24},{16,0},{24,8},{1,17},{9,25},{17,1},{25,9},{2,18},{10... | collective-permute-start | bytes 12296 | tf_op jit(solution)/shard_map/ppermute | solution.py:266
  93.2 3.6 %collective-permute-start.12 = (f32[8,128]{1,0:T(8,128)S(1)}, f32[8,128]{1,0:T(8,128)S(1)}, u32[]{:S(2)}, u32[]{:S(2)}) collective-permute-start(f32[8,128]{1,0:T(8,128)S(1)} %max.28), channel_id=1, source_target_pairs={{0,4},{4,0},{1,5},{5,1},{2,6},{6,2},{3,7},{7,3},{8,12},{12,8},{9,1... | collective-permute-start | bytes 12296 | tf_op jit(solution)/shard_map/ppermute | solution.py:266
  96.8 5.9 %collective-permute-start.13 = (f32[8,128]{1,0:T(8,128)S(1)}, f32[8,128]{1,0:T(8,128)S(1)}, u32[]{:S(2)}, u32[]{:S(2)}) collective-permute-start(f32[8,128]{1,0:T(8,128)S(1)} %max.29), channel_id=1, source_target_pairs={{0,64},{64,0},{128,192},{192,128},{1,65},{65,1},{129,193},{193,129... | collective-permute-start | bytes 12296 | tf_op jit(solution)/shard_map/ppermute | solution.py:266
  102.6 7.5 %collective-permute-start.14 = (f32[8,128]{1,0:T(8,128)S(1)}, f32[8,128]{1,0:T(8,128)S(1)}, u32[]{:S(2)}, u32[]{:S(2)}) collective-permute-start(f32[8,128]{1,0:T(8,128)S(1)} %max.30), channel_id=1, source_target_pairs={{0,128},{64,192},{128,0},{192,64},{1,129},{65,193},{129,1},{193,65... | collective-permute-start | bytes 12296 | tf_op jit(solution)/shard_map/ppermute | solution.py:266
where the time goes:
time: 113 us
  waiting for transfers between devices  48 us (42%)
  starting transfers between devices  30.8 us (27%)
  Pallas kernels  25.6 us (23%)
  local copies, waits for them, and re-layouts  8.2 us (7%)
    ppermute x8, waiting for transfers between devices, global_max(): block = jnp.maximum(block, lax.ppermute(block, axis, pairs))  25.3 us
    pallas_call x1, Pallas kernels, filter_call(): pl.pallas_call(filter_kernel, out_shape=(jax.ShapeDtypeStruct((12, rows,...  23 us
    ppermute x8, starting transfers between devices, global_max(): block = jnp.maximum(block, lax.ppermute(block, axis, pairs))  15.2 us
    ppermute x1, waiting for transfers between devices, per_device(): mid_lo = lax.ppermute(volume[:, tail], y_axes, up)  11.3 us
    ppermute x1, starting transfers between devices, per_device(): mid_hi = lax.ppermute(volume[:, head], y_axes, down)  6.54 us
    unnamed x14, local copies, waits for them, and re-layouts  6.35 us
    ppermute x1, waiting for transfers between devices, per_device(): far_hi = lax.ppermute(far[:, head], y_axes, down)  5.24 us
    ppermute x1, starting transfers between devices, per_device(): far_lo = lax.ppermute(far[:, tail], y_axes, up)  3.92 us
  transfers between devices with their start and end apart: 15, of which 12 were waited for; matrix products, arithmetic and copies ran while one was open for 1% of the time, Pallas kernels for 0%

commit v1 on v0

--- a/solution.py
+++ b/solution.py
@@ -16,7 +16,7 @@
 wide_y = tile_y + 2 * rim
 x_span = ((0, 80), (12, 48), (12, 48), (20, 32))
 rows = tile_x * tile_y
-z_rows = 96
+z_rows = 192
 score_rows = 192
 mib = 1024 * 1024
 
@@ -48,7 +48,9 @@
         y_parts += [band(v, radius, tile_y, wide_y, rim) for v in w]
         xb = np.concatenate([band(v, radius, tile_x, count, rim - first) for v in w])
         hi, lo = split(xb)
-        x_parts.append(np.concatenate([hi, hi, lo], axis=1))
+        x_part = np.zeros((72, 2 * depth), hi.dtype)
+        x_part[:, : 3 * count] = np.concatenate([hi, hi, lo], axis=1)
+        x_parts.append(x_part)
         for v in w:
             hi, lo = split(band(v * scale * scale, radius, depth, depth, 0).T)
             z_parts.append(
@@ -58,7 +60,7 @@
             )
     hi, lo = split(np.concatenate(y_parts))
     y_all = np.concatenate([hi, hi, lo, np.zeros((hi.shape[0], 16), hi.dtype)], axis=1)
-    return y_all, x_parts, np.stack(z_parts)
+    return y_all, np.stack(x_parts), np.stack(z_parts)
 
 
 def halves(value):
@@ -71,18 +73,17 @@
     return jnp.dot(a, b, preferred_element_type=jnp.float32)
 
 
-def filter_kernel(core_ref, *refs):
-    sources, refs = refs[:8], refs[8:]
-    wy, wx8, wx4, wx2, wx1, wz, stats_out, peaks, f8, f4, f2, f1, mixed, stats = refs[:14]
-    held, in_sems, out_sems = refs[14:22], refs[22], refs[23]
-    mid, pair, far, mid_lo, mid_hi, pair_y, far_lo, far_hi = held
+def filter_kernel(
+    core_ref, mid_hbm, wy_hbm, wx_hbm, wz_hbm, pair, far, mid_lo, mid_hi, pair_y, far_lo, far_hi,
+    stats_out, peaks, f8, f4, f2, f1, mixed, stats, mid, wy, wx, wz, in_sems, out_sems,
+):
     loads = [
-        pltpu.make_async_copy(a, b, in_sems.at[i]) for i, (a, b) in enumerate(zip(sources, held))
+        pltpu.make_async_copy(a, b, in_sems.at[i])
+        for i, (a, b) in enumerate(((mid_hbm, mid), (wy_hbm, wy), (wx_hbm, wx), (wz_hbm, wz)))
     ]
-    for i in (0, 3, 4, 1, 5, 2, 6, 7):
-        loads[i].start()
+    for load in loads:
+        load.start()
     fields = (f8, f4, f2, f1)
-    x_bands = (wx8, wx4, wx2, wx1)
     core = core_ref[0]
     f8[pl.ds(72 * 96, 8 * 96), :] = jnp.zeros((8 * 96, depth), jnp.float32)
     zeros16 = jnp.zeros((16, 2 * depth), jnp.bfloat16)
@@ -116,29 +117,30 @@
         y_step(mid_parts, 2 * i, rim + 2 * i, 4)
         return carry
 
-    for i in (0, 3, 4):
-        loads[i].wait()
-    lax.fori_loop(0, 12, mid_body, 0, unroll=2)
-
-    sides = ((pair_parts, core, (1, 5)), (far_parts, 1 - core, (2, 6, 7)))
-    for parts, before, needed in sides:
-        for i in needed:
-            loads[i].wait()
-        for start, stop, levels in ((0, 2, 4), (2, 6, 3), (6, 12, 1)):
+    loads[0].wait()
+    loads[1].wait()
+    lax.fori_loop(0, 12, mid_body, 0, unroll=4)
+
+    for parts, before in ((pair_parts, core), (far_parts, 1 - core)):
+        for start, stop, levels in ((0, 2, 4), (2, 6, 3), (6, 10, 1), (10, 12, 1)):
 
             def side_body(j, carry, parts=parts, before=before, levels=levels):
                 i = j + before * (11 - 2 * j)
                 y_step(parts, 2 * i, 2 * i + 48 * (1 - before), levels)
                 return carry
 
-            lax.fori_loop(start, stop, side_body, 0, unroll=2)
-
-    peak_rows, stores = [], []
+            lax.fori_loop(start, stop, side_body, 0, unroll=min(4, stop - start))
+
+    loads[2].wait()
+    loads[3].wait()
+    lane = lax.broadcasted_iota(jnp.int32, (1, depth), 1)
+    peak_row = jnp.zeros((1, depth), jnp.float32)
+    stores = []
     for level in range(4):
-        field, x_band = fields[level], x_bands[level]
+        field = fields[level]
         count = x_span[level][1]
 
-        def x_body(yp, carry, field=field, x_band=x_band, count=count):
+        def x_body(yp, carry, field=field, level=level, count=count):
             at = pl.ds(pl.multiple_of(48 * yp, 48), 48)
             for f, first, outs in ((0, 0, 3), (1, 3, 2), (2, 5, 1)):
                 pieces = [
@@ -146,7 +148,7 @@
                 ]
                 hi, lo = halves(jnp.concatenate(pieces, axis=1))
                 data = jnp.concatenate([hi, lo, hi], axis=0)
-                out = dot(x_band[0 : 24 * outs, :], data)
+                out = dot(wx[level, 0 : 24 * outs, 0 : 3 * count], data)
                 for k in range(outs):
                     u = out[24 * k : 24 * k + 24]
                     u = jnp.concatenate([u[:, :depth], u[:, depth:]], axis=0)
@@ -155,7 +157,7 @@
                     mixed[first + k, at, depth : 2 * depth] = lo
             return carry
 
-        lax.fori_loop(0, tile_y // 2, x_body, 0, unroll=2)
+        lax.fori_loop(0, tile_y // 2, x_body, 0, unroll=4)
 
         def z_body(c, best, level=level):
             at = pl.ds(pl.multiple_of(c * z_rows, z_rows), z_rows)
@@ -176,18 +178,19 @@
             stats[3 * level + 2, at, :] = energy
             return jnp.maximum(best, jnp.max(energy.reshape(z_rows // 8, 8, depth), axis=0))
 
-        best = lax.fori_loop(0, rows // z_rows, z_body, jnp.zeros((8, depth), jnp.float32), unroll=2)
+        best = lax.fori_loop(0, rows // z_rows, z_body, jnp.zeros((8, depth), jnp.float32))
         at = pl.ds(3 * level, 3)
         stores.append(pltpu.make_async_copy(stats.at[at], stats_out.at[at], out_sems.at[level]))
         stores[-1].start()
-        peak_rows.append(jnp.broadcast_to(jnp.max(best), (1, depth)))
-    peaks[...] = jnp.concatenate(peak_rows + peak_rows, axis=0)
+        peak_row = jnp.where(lane == level, jnp.max(best), peak_row)
+    peaks[...] = peak_row
     for store in stores:
         store.wait()
 
 
-def score_kernel(stats, peaks, throat, flat):
+def score_kernel(stats, all_peaks, throat, flat):
     step = pl.program_id(0)
+    peaks = jnp.max(all_peaks[...], axis=0, keepdims=True)
     for c in range(score_rows // 24):
         at = pl.ds(24 * c, 24)
         best = None
@@ -195,7 +198,7 @@
             trace_sum = stats[3 * level, at, :]
             minors = stats[3 * level + 1, at, :]
             energy = stats[3 * level + 2, at, :]
-            spread = 0.25 * peaks[pl.ds(level, 1), :] + 1e-06
+            spread = 0.25 * peaks[:, level : level + 1] + 1e-06
             guard = energy + 0.1 * spread
             ratio = minors / guard
             score = (
@@ -212,34 +215,34 @@
             throat[i] = flat[pl.ds(i, tile_y, stride=tile_x), :]
 
 
-def hbm(n):
-    return [pl.BlockSpec(memory_space=pl.ANY)] * n
-
-
 def vmem(n):
     return [pl.BlockSpec(memory_space=pltpu.VMEM)] * n
 
 
 def filter_call(core, pieces, interpret=False):
-    y_all, x_parts, z_all = constants()
+    weights = constants()
+    held = [pltpu.VMEM((tile_x, tile_y, depth), jnp.float32)]
+    held += [pltpu.VMEM(w.shape, jnp.bfloat16) for w in weights]
     return pl.pallas_call(
         filter_kernel,
         out_shape=(
             jax.ShapeDtypeStruct((12, rows, depth), jnp.float32),
-            jax.ShapeDtypeStruct((8, depth), jnp.float32),
+            jax.ShapeDtypeStruct((1, depth), jnp.float32),
         ),
-        in_specs=[pl.BlockSpec(memory_space=pltpu.SMEM)] + hbm(8) + vmem(6),
-        out_specs=(*hbm(1), *vmem(1)),
+        in_specs=[pl.BlockSpec(memory_space=pltpu.SMEM)]
+        + [pl.BlockSpec(memory_space=pltpu.HBM)] * 4
+        + vmem(7),
+        out_specs=(pl.BlockSpec(memory_space=pl.ANY), vmem(1)[0]),
         scratch_shapes=[pltpu.VMEM((count * 96, depth), jnp.float32) for _, count in x_span]
         + [
             pltpu.VMEM((6, rows, 2 * depth), jnp.bfloat16),
             pltpu.VMEM((12, rows, depth), jnp.float32),
         ]
-        + [pltpu.VMEM(piece.shape, jnp.float32) for piece in pieces]
-        + [pltpu.SemaphoreType.DMA((8,)), pltpu.SemaphoreType.DMA((4,))],
+        + held
+        + [pltpu.SemaphoreType.DMA((4,)), pltpu.SemaphoreType.DMA((4,))],
         compiler_params=pltpu.CompilerParams(vmem_limit_bytes=40 * mib),
         interpret=interpret,
-    )(core, *pieces, jnp.asarray(y_all), *[jnp.asarray(v) for v in x_parts], jnp.asarray(z_all))
+    )(core, pieces[0], *[jnp.asarray(w) for w in weights], *pieces[1:])
 
 
 def score_call(stats, peaks, interpret=False):
@@ -249,7 +252,7 @@
         grid=(rows // score_rows,),
         in_specs=[
             pl.BlockSpec((12, score_rows, depth), lambda i: (0, i, 0)),
-            pl.BlockSpec((8, depth), lambda i: (0, 0)),
+            pl.BlockSpec(peaks.shape, lambda i: (0, 0)),
         ],
         out_specs=pl.BlockSpec((tile_x, tile_y, depth), lambda i: (0, 0, 0)),
         scratch_shapes=[pltpu.VMEM((rows, depth), jnp.float32)],
@@ -258,13 +261,12 @@
     )(stats, peaks)
 
 
-def global_max(block):
-    for axis, step in (
-        ("core", 1), ("y", 1), ("y", 2), ("x", 1), ("x", 2), ("zl", 1), ("zh", 1), ("zh", 2),
-    ):
-        pairs = [(i, i ^ step) for i in range(lax.axis_size(axis))]
-        block = jnp.maximum(block, lax.ppermute(block, axis, pairs))
-    return block
+def all_peaks(row):
+    row = jnp.maximum(row, lax.ppermute(row, "core", [(0, 1), (1, 0)]))
+    axes = ("zh", "x", "zl", "y")
+    peers = lax.axis_size(axes)
+    spread = jnp.broadcast_to(row[None], (peers, 1, depth))
+    return lax.all_to_all(spread, axes, 0, 0, tiled=True).reshape(peers, depth)
 
 
 def per_device(volume):
@@ -277,9 +279,11 @@
     tail, head = slice(tile_y - rim, tile_y), slice(0, rim)
 
     far = lax.ppermute(volume, x_axes, far_perm)
-    mid_lo = lax.ppermute(volume[:, tail], y_axes, up)
-    mid_hi = lax.ppermute(volume[:, head], y_axes, down)
     pair = lax.ppermute(volume, x_axes, pair_perm)
+    own = volume
+    mid_lo = lax.ppermute(own[:, tail], y_axes, up)
+    mid_hi = lax.ppermute(own[:, head], y_axes, down)
+    far, mid_lo, mid_hi = lax.optimization_barrier((far, mid_lo, mid_hi))
     far_lo = lax.ppermute(far[:, tail], y_axes, up)
     far_hi = lax.ppermute(far[:, head], y_axes, down)
     pair_y = lax.ppermute(jnp.concatenate([mid_lo, mid_hi], axis=1), x_axes, pair_perm)
@@ -287,7 +291,7 @@
     core = lax.axis_index("core").reshape(1)
     pieces = (volume, pair, far, mid_lo, mid_hi, pair_y, far_lo, far_hi)
     stats, peaks = filter_call(core, pieces)
-    return score_call(stats, global_max(peaks))
+    return score_call(stats, all_peaks(peaks))
 
 
 def solution(mesh):

time: 113 us -> 92.2 us (0.82)
  the two profiles are of different devices: /device:TPU:6 before, /device:TPU:1 now
where the time goes in v1:
time: 92.2 us; the launch traced here: 91.8 us
  blocking collectives  33.3 us (36%)
  Pallas kernels  21.1 us (23%)
  starting transfers between devices  18.9 us (20%)
  waiting for transfers between devices  12.3 us (13%)
  local copies, waits for them, and re-layouts  6.13 us (7%)
    all_to_all x1, blocking collectives, all_peaks(): return lax.all_to_all(spread, axes, 0, 0, tiled=True).reshape(peers, depth)  33.3 us
    pallas_call x1, Pallas kernels, filter_call(): pl.pallas_call(filter_kernel, out_shape=(jax.ShapeDtypeStruct((12, rows,...  18.3 us
    ppermute x1, starting transfers between devices, per_device(): far = lax.ppermute(volume, x_axes, far_perm)  6.28 us
    ppermute x1, waiting for transfers between devices, per_device(): far_hi = lax.ppermute(far[:, head], y_axes, down)  5.5 us
    ppermute x1, starting transfers between devices, per_device(): far_lo = lax.ppermute(far[:, tail], y_axes, up)  4.47 us
    unnamed x8, local copies, waits for them, and re-layouts  4.24 us
    ppermute x1, starting transfers between devices, per_device(): mid_lo = lax.ppermute(own[:, tail], y_axes, up)  4 us
    ppermute x1, waiting for transfers between devices, per_device(): mid_hi = lax.ppermute(own[:, head], y_axes, down)  3.41 us
  transfers between devices with their start and end apart: 8, of which 5 were waited for; matrix products, arithmetic and copies ran while one was open for 2% of the time, Pallas kernels for 0%

profile of v1, /device:TPU:1, one launch (start us, length us, event | category | flops | bytes accessed | tf_op | source)
XLA Modules:
  0.0 91.8 jit_solution(8272360032644853636)
XLA Ops:
  0.0 6.3 %collective-permute-start.1 = (f32[24,32,128]{2,1,0:T(8,128)}, f32[24,32,128]{2,1,0:T(8,128)S(1)}, u32[]{:S(2)}, u32[]{:S(2)}) collective-permute-start(f32[24,32,128]{2,1,0:T(8,128)} %mid_hbm.1), channel_id=1, source_target_pairs={{32,64},{96,128},{160,192},{64,32},{128,96},{192,160},{33,65},{97,... | collective-permute-start | bytes 1179656 | tf_op jit(solution)/shard_map/ppermute | solution.py:281
  6.3 1.1 %fusion.1 = (f32[24,24,128]{2,1,0:T(8,128)S(1)}, f32[24,24,128]{2,1,0:T(8,128)S(1)}) fusion(f32[24,32,128]{2,1,0:T(8,128)} %mid_hbm.1), kind=kLoop, calls=%fused_computation.3 | loop fusion | bytes 1179648 | tf_op jit(solution)/shard_map/slice | solution.py:285
  7.4 1.3 %collective-permute-start.3 = (f32[24,24,128]{2,1,0:T(8,128)S(1)}, f32[24,24,128]{2,1,0:T(8,128)S(1)}, u32[]{:S(2)}, u32[]{:S(2)}) collective-permute-start(f32[24,24,128]{2,1,0:T(8,128)S(1)} %get-tuple-element.17), channel_id=1, source_target_pairs={{1,0},{2,1},{3,2},{4,3},{5,4},{6,5},{7,6},{8,7},{9,8},{10,9},{11,1... | collective-permute-start | bytes 884744 | tf_op jit(solution)/shard_map/ppermute | solution.py:285
  8.7 4.0 %collective-permute-start.2 = (f32[24,24,128]{2,1,0:T(8,128)S(1)}, f32[24,24,128]{2,1,0:T(8,128)S(1)}, u32[]{:S(2)}, u32[]{:S(2)}) collective-permute-start(f32[24,24,128]{2,1,0:T(8,128)S(1)} %get-tuple-element.18), channel_id=1, source_target_pairs={{0,1},{1,2},{2,3},{3,4},{4,5},{5,6},{6,7},{7,8},{8,9},{9,10},{10,1... | collective-permute-start | bytes 884744 | tf_op jit(solution)/shard_map/ppermute | solution.py:284
  12.7 3.4 %collective-permute-done.3.mid_hi = f32[24,24,128]{2,1,0:T(8,128)S(1)} collective-permute-done((f32[24,24,128]{2,1,0:T(8,128)S(1)}, f32[24,24,128]{2,1,0:T(8,128)S(1)}, u32[]{:S(2)}, u32[]{:S(2)}) %collective-permute-start.3) | collective-permute-done | bytes 294944 | tf_op jit(solution)/shard_map/ppermute | solution.py:285
  16.1 1.8 %collective-permute-done.2.mid_lo = f32[24,24,128]{2,1,0:T(8,128)S(1)} collective-permute-done((f32[24,24,128]{2,1,0:T(8,128)S(1)}, f32[24,24,128]{2,1,0:T(8,128)S(1)}, u32[]{:S(2)}, u32[]{:S(2)}) %collective-permute-start.2) | collective-permute-done | bytes 294944 | tf_op jit(solution)/shard_map/ppermute | solution.py:284
  17.9 0.0 collective-permute-done.1.far
  17.9 0.1 collective-permute-start.4
  18.0 0.5 collective-permute-start
  18.5 0.8 fusion
  19.3 1.3 %collective-permute-start.6 = (f32[24,24,128]{2,1,0:T(8,128)}, f32[24,24,128]{2,1,0:T(8,128)S(1)}, u32[]{:S(2)}, u32[]{:S(2)}) collective-permute-start(f32[24,24,128]{2,1,0:T(8,128)} %get-tuple-element.15), channel_id=1, source_target_pairs={{1,0},{2,1},{3,2},{4,3},{5,4},{6,5},{7,6},{8,7},{9,8},{10,9},{11,1... | collective-permute-start | bytes 884744 | tf_op jit(solution)/shard_map/ppermute | solution.py:288
  20.6 4.5 %collective-permute-start.5 = (f32[24,24,128]{2,1,0:T(8,128)S(1)}, f32[24,24,128]{2,1,0:T(8,128)S(1)}, u32[]{:S(2)}, u32[]{:S(2)}) collective-permute-start(f32[24,24,128]{2,1,0:T(8,128)S(1)} %get-tuple-element.16), channel_id=1, source_target_pairs={{0,1},{1,2},{2,3},{3,4},{4,5},{5,6},{6,7},{7,8},{8,9},{9,10},{10,1... | collective-permute-start | bytes 884744 | tf_op jit(solution)/shard_map/ppermute | solution.py:287
  25.0 0.0 collective-permute-done.pair
  25.1 5.5 %collective-permute-done.6.far_hi = f32[24,24,128]{2,1,0:T(8,128)S(1)} collective-permute-done((f32[24,24,128]{2,1,0:T(8,128)}, f32[24,24,128]{2,1,0:T(8,128)S(1)}, u32[]{:S(2)}, u32[]{:S(2)}) %collective-permute-start.6) | collective-permute-done | bytes 294944 | tf_op jit(solution)/shard_map/ppermute | solution.py:288
  30.6 0.8 collective-permute-done.5.far_lo
  31.4 0.0 collective-permute-done.4.pair_y
  31.4 0.0 copy-start
  31.4 1.0 %copy-done = f32[24,32,128]{2,1,0:T(8,128)S(1)} copy-done((f32[24,32,128]{2,1,0:T(8,128)S(1)}, f32[24,32,128]{2,1,0:T(8,128)}, u32[]{:S(2)}) %copy-start) | copy-done | bytes 393240
  32.4 0.0 copy-start.1
  32.4 1.4 %copy-done.1 = bf16[12,256,256]{2,1,0:T(8,128)(2,1)S(1)} copy-done((bf16[12,256,256]{2,1,0:T(8,128)(2,1)S(1)}, bf16[12,256,256]{2,1,0:T(8,128)(2,1)}, u32[]{:S(2)}) %copy-start.1) | copy-done | bytes 1572888
  33.8 0.0 copy-start.2
  33.8 0.9 %copy-done.2 = bf16[384,256]{1,0:T(8,128)(2,1)S(1)} copy-done((bf16[384,256]{1,0:T(8,128)(2,1)S(1)}, bf16[384,256]{1,0:T(8,128)(2,1)}, u32[]{:S(2)}) %copy-start.2) | copy-done | bytes 196632
  34.7 0.0 copy-start.3
  34.7 0.9 copy-done.3
  35.6 18.3 %shard_map.46 = (f32[12,768,128]{2,1,0:T(8,128)S(1)}, f32[1,128]{1,0:T(1,128)S(1)}) custom-call(s32[1]{0:T(128)} %bitcast.core_ref, f32[24,32,128]{2,1,0:T(8,128)S(1)} %copy-done, bf16[384,256]{1,0:T(8,128)(2,1)S(1)} %copy-done.2, bf16[4,72,256]{2,1,0:T(8,128)(2,1)S(1)} %copy-done.3, bf16[12,256,256]{2,1,0:T(8,128)(2,1)S(1)} %copy-done.1, ...), custom_call_target="tpu_custom_call" | custom-call | tf_op jit(solution)/shard_map/pallas_call | solution.py:226
  53.9 1.0 %collective-permute-start.7 = (f32[1,128]{1,0:T(1,128)S(1)}, f32[1,128]{1,0:T(1,128)S(1)}, u32[]{:S(2)}, u32[]{:S(2)}) collective-permute-start(f32[1,128]{1,0:T(1,128)S(1)} %get-tuple-element.14), channel_id=1, source_target_pairs={{0,32},{32,0},{1,33},{33,1},{2,34},{34,2},{3,35},{35,3},{4,36},{36... | collective-permute-start | bytes 1544 | tf_op jit(solution)/shard_map/ppermute | solution.py:265
  54.9 0.8 collective-permute-done.7
  55.7 33.3 %all_to_all.5 = f32[128,1,128]{2,1,0:T(1,128)S(1)} all-to-all(f32[128,1,128]{2,1,0:T(1,128)S(1)} %broadcast_in_dim.9), channel_id=1, replica_groups=mesh['zh'=4,'core'=2,'x'=4,'zl'=2,'y'=4] {'zh','x','zl','y'}, dimensions={0} | all-to-all | bytes 131072 | tf_op jit(solution)/shard_map/all_to_all | solution.py:269
  89.0 2.8 %shard_map.47 = f32[24,32,128]{2,1,0:T(8,128)} custom-call(f32[12,768,128]{2,1,0:T(8,128)S(1)} %get-tuple-element.13.stats, f32[128,128]{1,0:T(8,128)S(1)} %bitcast.4), custom_call_target="tpu_custom_call" | custom-call | tf_op jit(solution)/shard_map/pallas_call | solution.py:249
  (3 shorter events, 0.1 us)
Async XLA Ops:
  0.0 17.9 %collective-permute-start.1 = (f32[24,32,128]{2,1,0:T(8,128)}, f32[24,32,128]{2,1,0:T(8,128)S(1)}, u32[]{:S(2)}, u32[]{:S(2)}) collective-permute-start(f32[24,32,128]{2,1,0:T(8,128)} %mid_hbm.1), channel_id=1, source_target_pairs={{32,64},{96,128},{160,192},{64,32},{128,96},{192,160},{33,65},{97,... | collective-permute-start | bytes 1179656 | tf_op jit(solution)/shard_map/ppermute | solution.py:281
  7.4 8.7 %collective-permute-start.3 = (f32[24,24,128]{2,1,0:T(8,128)S(1)}, f32[24,24,128]{2,1,0:T(8,128)S(1)}, u32[]{:S(2)}, u32[]{:S(2)}) collective-permute-start(f32[24,24,128]{2,1,0:T(8,128)S(1)} %get-tuple-element.17), channel_id=1, source_target_pairs={{1,0},{2,1},{3,2},{4,3},{5,4},{6,5},{7,6},{8,7},{9,8},{10,9},{11,1... | collective-permute-start | bytes 884744 | tf_op jit(solution)/shard_map/ppermute | solution.py:285
  8.7 9.2 %collective-permute-start.2 = (f32[24,24,128]{2,1,0:T(8,128)S(1)}, f32[24,24,128]{2,1,0:T(8,128)S(1)}, u32[]{:S(2)}, u32[]{:S(2)}) collective-permute-start(f32[24,24,128]{2,1,0:T(8,128)S(1)} %get-tuple-element.18), channel_id=1, source_target_pairs={{0,1},{1,2},{2,3},{3,4},{4,5},{5,6},{6,7},{7,8},{8,9},{9,10},{10,1... | collective-permute-start | bytes 884744 | tf_op jit(solution)/shard_map/ppermute | solution.py:284
  17.9 13.4 %collective-permute-start.4 = (f32[24,48,128]{2,1,0:T(8,128)S(1)}, f32[24,48,128]{2,1,0:T(8,128)S(1)}, u32[]{:S(2)}, u32[]{:S(2)}) collective-permute-start(f32[24,48,128]{2,1,0:T(8,128)S(1)} %pad_maximum_fusion), channel_id=1, source_target_pairs={{0,32},{32,0},{64,96},{96,64},{128,160},{160,128},{192,224},{224,1... | collective-permute-start | bytes 1769480 | tf_op jit(solution)/shard_map/ppermute | solution.py:289
  18.0 7.0 %collective-permute-start = (f32[24,32,128]{2,1,0:T(8,128)}, f32[24,32,128]{2,1,0:T(8,128)S(1)}, u32[]{:S(2)}, u32[]{:S(2)}) collective-permute-start(f32[24,32,128]{2,1,0:T(8,128)} %mid_hbm.1), channel_id=1, source_target_pairs={{0,32},{32,0},{64,96},{96,64},{128,160},{160,128},{192,224},{224,1... | collective-permute-start | bytes 1179656 | tf_op jit(solution)/shard_map/ppermute | solution.py:282
  19.3 11.3 %collective-permute-start.6 = (f32[24,24,128]{2,1,0:T(8,128)}, f32[24,24,128]{2,1,0:T(8,128)S(1)}, u32[]{:S(2)}, u32[]{:S(2)}) collective-permute-start(f32[24,24,128]{2,1,0:T(8,128)} %get-tuple-element.15), channel_id=1, source_target_pairs={{1,0},{2,1},{3,2},{4,3},{5,4},{6,5},{7,6},{8,7},{9,8},{10,9},{11,1... | collective-permute-start | bytes 884744 | tf_op jit(solution)/shard_map/ppermute | solution.py:288
  20.6 10.8 %collective-permute-start.5 = (f32[24,24,128]{2,1,0:T(8,128)S(1)}, f32[24,24,128]{2,1,0:T(8,128)S(1)}, u32[]{:S(2)}, u32[]{:S(2)}) collective-permute-start(f32[24,24,128]{2,1,0:T(8,128)S(1)} %get-tuple-element.16), channel_id=1, source_target_pairs={{0,1},{1,2},{2,3},{3,4},{4,5},{5,6},{6,7},{7,8},{8,9},{9,10},{10,1... | collective-permute-start | bytes 884744 | tf_op jit(solution)/shard_map/ppermute | solution.py:287
  31.4 1.0 %copy-start = (f32[24,32,128]{2,1,0:T(8,128)S(1)}, f32[24,32,128]{2,1,0:T(8,128)}, u32[]{:S(2)}) copy-start(f32[24,32,128]{2,1,0:T(8,128)} %mid_hbm.1) | copy-start | bytes 1179652
  32.4 1.4 %copy-start.1 = (bf16[12,256,256]{2,1,0:T(8,128)(2,1)S(1)}, bf16[12,256,256]{2,1,0:T(8,128)(2,1)}, u32[]{:S(2)}) copy-start(bf16[12,256,256]{2,1,0:T(8,128)(2,1)} %constant.14.clone.wz_hbm) | copy-start | bytes 4718596
  33.8 0.9 %copy-start.2 = (bf16[384,256]{1,0:T(8,128)(2,1)S(1)}, bf16[384,256]{1,0:T(8,128)(2,1)}, u32[]{:S(2)}) copy-start(bf16[384,256]{1,0:T(8,128)(2,1)} %constant.12.clone.wy_hbm) | copy-start | bytes 589828
  34.7 0.9 copy-start.3
  53.9 1.8 %collective-permute-start.7 = (f32[1,128]{1,0:T(1,128)S(1)}, f32[1,128]{1,0:T(1,128)S(1)}, u32[]{:S(2)}, u32[]{:S(2)}) collective-permute-start(f32[1,128]{1,0:T(1,128)S(1)} %get-tuple-element.14), channel_id=1, source_target_pairs={{0,32},{32,0},{1,33},{33,1},{2,34},{34,2},{3,35},{35,3},{4,36},{36... | collective-permute-start | bytes 1544 | tf_op jit(solution)/shard_map/ppermute | solution.py:265

commit v2 on v1

v2 whole, which is shorter than its diff:
```python
import jax
import jax.numpy as jnp
import ml_dtypes
import numpy as np
from jax import lax
from jax.experimental import pallas as pl
from jax.experimental.pallas import tpu as pltpu
from jax.sharding import PartitionSpec as P

scale_list = (8.0, 4.0, 2.0, 1.0)
radius_list = (24, 12, 6, 3)
x_axes = ("zh", "core")
y_axes = ("x", "zl", "y")
rim = 24
tile_x, tile_y, depth = 24, 32, 128
wide_y = tile_y + 2 * rim
near = (24, 12, 12, 4)
planes = (80, 48, 48, 32)
rows = tile_x * tile_y
z_rows = 192
pitch = 104
mib = 1024 * 1024
log2_e = float(np.log2(np.e))


def taps(scale, radius):
    t = np.arange(-radius, radius + 1).astype(np.float64)
    bell = np.exp(-t * t / (2.0 * scale * scale))
    w0 = bell / bell.sum()
    w1 = -t / (scale * scale) * w0
    w2 = (t * t / scale**4 - 1.0 / (scale * scale)) * w0
    return w0, w1, w2


def band(weights, radius, out_places, in_places):
    lag = out_places[:, None] - in_places[None, :]
    return np.where(np.abs(lag) <= radius, weights[np.clip(lag + radius, 0, 2 * radius)], 0.0)


def split(matrix):
    hi = matrix.astype(np.float32).astype(ml_dtypes.bfloat16)
    lo = (matrix - hi.astype(np.float64)).astype(np.float32).astype(ml_dtypes.bfloat16)
    return hi, lo


def x_places(core, level):
    n = near[level]
    after, before = 2 * rim + np.arange(n), rim - n + np.arange(n)
    sides = [before, after] if core else [after, before]
    padding = np.full(planes[level] - rim - 2 * n, 1000)
    return np.concatenate([rim + np.arange(tile_x)] + sides + [padding])


def constants():
    y_parts, z_parts = [], []
    x_all = np.zeros((2, 4, 3 * tile_x, 2 * depth), ml_dtypes.bfloat16)
    y_places = np.arange(wide_y)
    for level, (scale, radius) in enumerate(zip(scale_list, radius_list)):
        w = taps(scale, radius)
        y_parts += [band(v, radius, rim + np.arange(tile_y), y_places) for v in w]
        for core in range(2):
            places = x_places(core, level)
            hi, lo = split(
                np.concatenate([band(v, radius, rim + np.arange(tile_x), places) for v in w])
            )
            x_all[core, level, :, : 3 * len(places)] = np.concatenate([hi, hi, lo], axis=1)
        for v in w:
            hi, lo = split(band(v * scale * scale, radius, np.arange(depth), np.arange(depth)).T)
            z_parts.append(
                np.concatenate(
                    [np.concatenate([hi, lo], axis=1), np.concatenate([hi, 0 * lo], axis=1)]
                )
            )
    hi, lo = split(np.concatenate(y_parts))
    y_all = np.concatenate([hi, hi, lo, np.zeros((hi.shape[0], 16), hi.dtype)], axis=1)
    return y_all, x_all, np.stack(z_parts)


def halves(value):
    hi = value.astype(jnp.bfloat16)
    lo = (value - hi.astype(jnp.float32)).astype(jnp.bfloat16)
    return hi, lo


def dot(a, b):
    return jnp.dot(a, b, preferred_element_type=jnp.float32)


def y_step(fields, wy, parts, slots):
    both = jnp.concatenate(parts, axis=1)
    both = jnp.concatenate([both[0], both[1]], axis=1)
    hi, lo = halves(both)
    zeros = jnp.zeros((16, 2 * depth), jnp.bfloat16)
    out = dot(wy[0 : 96 * len(slots), :], jnp.concatenate([hi, lo, hi, zeros], axis=0))
    for level, slot in enumerate(slots):
        for k in range(2):
            at = pl.multiple_of((slot + k) * pitch, 8)
            block = out[96 * level : 96 * level + 96, depth * k : depth * (k + 1)]
            fields[level][pl.ds(at, 96), :] = block


def side_steps(fields, wy, parts, before, base):
    for start, stop, levels in ((0, 2, 4), (2, 6, 3), (6, 10, 1), (10, 12, 1)):

        def body(j, carry, levels=levels):
            plane = 2 * (j + before * (11 - 2 * j))
            slots = [base[v] + plane - (rim - near[v]) * before for v in range(levels)]
            y_step(fields, wy, parts(plane), slots)
            return carry

        lax.fori_loop(start, stop, body, 0, unroll=min(4, stop - start))


def early_kernel(mid, wy, wx, wz, mid_lo, mid_hi, g8, g4, g2, g1):
    def mid_body(i, carry):
        at = pl.ds(2 * i, 2)
        y_step((g8, g4, g2, g1), wy, [mid_lo[at], mid[at], mid_hi[at]], [2 * i] * 4)
        return carry

    lax.fori_loop(0, tile_x // 2, mid_body, 0, unroll=4)


def late_kernel(
    core_ref, wy, wx, wz, far, far_lo, far_hi, pair, pair_lo, pair_hi, g8, g4, g2, g1,
    stats, peaks, f8, f4, f2, f1, mixed,
):
    own_fields, fields = (g8, g4, g2, g1), (f8, f4, f2, f1)
    core = core_ref[0]
    f8[pl.ds(2 * rim * pitch, 8 * pitch), :] = jnp.zeros((8 * pitch, depth), jnp.float32)

    def pair_parts(plane):
        at = pl.ds(plane, 2)
        return [pair_lo[at], pair[at], pair_hi[at]]

    def far_parts(plane):
        at = pl.ds(plane, 2)
        return [far_lo[at], far[at], far_hi[at]]

    side_steps(fields, wy, pair_parts, core, [0] * 4)
    side_steps(fields, wy, far_parts, 1 - core, near)

    lane = lax.broadcasted_iota(jnp.int32, (1, depth), 1)
    peak_row = jnp.zeros((1, depth), jnp.float32)
    for level in range(4):
        own, field = own_fields[level], fields[level]
        count = planes[level]

        def x_body(yp, carry, own=own, field=field, level=level, count=count):
            at = pl.ds(pl.multiple_of(48 * yp, 48), 48)
            for f, first, outs in ((0, 0, 3), (1, 3, 2), (2, 5, 1)):
                pieces = [
                    [
                        own[pl.ds(32 * f + 2 * yp + k, tile_x, stride=pitch), :],
                        field[pl.ds(32 * f + 2 * yp + k, count - tile_x, stride=pitch), :],
                    ]
                    for k in range(2)
                ]
                pieces = [jnp.concatenate(piece, axis=0) for piece in pieces]
                hi, lo = halves(jnp.concatenate(pieces, axis=1))
                data = jnp.concatenate([hi, lo, hi], axis=0)
                out = dot(wx[core, level, 0 : 24 * outs, 0 : 3 * count], data)
                for k in range(outs):
                    u = out[24 * k : 24 * k + 24]
                    u = jnp.concatenate([u[:, :depth], u[:, depth:]], axis=0)
                    hi, lo = halves(u)
                    mixed[first + k, at, 0:depth] = hi
                    mixed[first + k, at, depth : 2 * depth] = lo
            return carry

        lax.fori_loop(0, tile_y // 2, x_body, 0, unroll=4)

        def z_body(c, best, level=level):
            at = pl.ds(pl.multiple_of(c * z_rows, z_rows), z_rows)

            def z_pass(order, chosen):
                data = jnp.concatenate([mixed[p, at, :] for p in chosen], axis=0)
                out = dot(data, wz[3 * level + order])
                out = out[:, :depth] + out[:, depth:]
                return [out[z_rows * k : z_rows * (k + 1)] for k in range(len(chosen))]

            (zz,) = z_pass(2, (0,))
            yz, xz = z_pass(1, (3, 1))
            yy, xy, xx = z_pass(0, (5, 4, 2))
            sq = xy * xy + xz * xz + yz * yz
            stats[3 * level, at, :] = xx + yy + zz
            stats[3 * level + 1, at, :] = xx * yy + (xx + yy) * zz - sq
            energy = xx * xx + yy * yy + zz * zz + 2.0 * sq
            stats[3 * level + 2, at, :] = energy
            return jnp.maximum(best, jnp.max(energy.reshape(z_rows // 8, 8, depth), axis=0))

        best = lax.fori_loop(0, rows // z_rows, z_body, jnp.zeros((8, depth), jnp.float32), unroll=2)
        peak_row = jnp.where(lane == level, jnp.max(best), peak_row)
    peaks[...] = peak_row


def score_kernel(stats, all_peaks, throat, flat):
    peaks = jnp.max(all_peaks[...], axis=0, keepdims=True)
    spreads = [0.25 * peaks[:, level : level + 1] + 1e-06 for level in range(4)]

    def body(c, carry):
        at = pl.ds(pl.multiple_of(c * 24, 24), 24)
        best = None
        for level, spread in enumerate(spreads):
            trace_sum = stats[3 * level, at, :]
            minors = stats[3 * level + 1, at, :]
            energy = stats[3 * level + 2, at, :]
            guard = energy + 0.1 * spread
            root = lax.rsqrt(guard)
            ratio = minors * root * root
            score = (
                (1.0 - jnp.exp2(energy * (-0.5 * log2_e / spread)))
                * jnp.exp2(ratio * ratio * (-2.0 * log2_e))
                * (1.0 - jnp.tanh(2.0 * trace_sum * root))
            )
            best = score if best is None else jnp.maximum(best, score)
        flat[at, :] = 0.5 * best
        return carry

    lax.fori_loop(0, rows // 24, body, 0, unroll=4)
    for i in range(tile_x):
        throat[i] = flat[pl.ds(i, tile_y, stride=tile_x), :]


def vmem(n):
    return [pl.BlockSpec(memory_space=pltpu.VMEM)] * n


def early_call(volume, mid_lo, mid_hi, weights, interpret=False):
    return pl.pallas_call(
        early_kernel,
        out_shape=[jax.ShapeDtypeStruct((tile_x * pitch, depth), jnp.float32)] * 4,
        in_specs=vmem(6),
        out_specs=vmem(4),
        compiler_params=pltpu.CompilerParams(vmem_limit_bytes=16 * mib),
        interpret=interpret,
    )(volume, *weights, mid_lo, mid_hi)


def late_call(core, weights, pieces, early, interpret=False):
    return pl.pallas_call(
        late_kernel,
        out_shape=(
            jax.ShapeDtypeStruct((12, rows, depth), jnp.float32),
            jax.ShapeDtypeStruct((1, depth), jnp.float32),
        ),
        in_specs=[pl.BlockSpec(memory_space=pltpu.SMEM)] + vmem(13),
        out_specs=tuple(vmem(2)),
        scratch_shapes=[
            pltpu.VMEM(((count - tile_x) * pitch, depth), jnp.float32) for count in planes
        ]
        + [pltpu.VMEM((6, rows, 2 * depth), jnp.bfloat16)],
        compiler_params=pltpu.CompilerParams(vmem_limit_bytes=24 * mib),
        interpret=interpret,
    )(core, *weights, *pieces, *early)


def score_call(stats, peaks, interpret=False):
    return pl.pallas_call(
        score_kernel,
        out_shape=jax.ShapeDtypeStruct((tile_x, tile_y, depth), jnp.float32),
        in_specs=vmem(2),
        out_specs=vmem(1)[0],
        scratch_shapes=[pltpu.VMEM((rows, depth), jnp.float32)],
        compiler_params=pltpu.CompilerParams(vmem_limit_bytes=8 * mib),
        interpret=interpret,
    )(stats, peaks)


def all_peaks(row):
    row = jnp.maximum(row, lax.ppermute(row, "core", [(0, 1), (1, 0)]))
    axes = ("zh", "x", "zl", "y")
    peers = lax.axis_size(axes)
    spread = jnp.broadcast_to(row[None], (peers, 1, depth))
    return lax.all_to_all(spread, axes, 0, 0, tiled=True).reshape(peers, depth)


def per_device(volume):
    n_x, n_y = lax.axis_size(x_axes), lax.axis_size(y_axes)
    pair_perm = [(i, i ^ 1) for i in range(n_x)]
    far_perm = [(i, i + 1) for i in range(1, n_x - 1, 2)]
    far_perm += [(j, i) for i, j in far_perm]
    up = [(i, i + 1) for i in range(n_y - 1)]
    down = [(j, i) for i, j in up]
    tail, head = slice(tile_y - rim, tile_y), slice(0, rim)

    core = lax.axis_index("core").reshape(1)
    volume, core = lax.optimization_barrier((volume, core))
    far = lax.ppermute(volume, x_axes, far_perm)
    mid_lo = lax.ppermute(volume[:, tail], y_axes, up)
    mid_hi = lax.ppermute(volume[:, head], y_axes, down)
    pair = lax.ppermute(volume, x_axes, pair_perm)
    far_lo, far_hi = far[:, tail], far[:, head]
    _, _, mid_lo, mid_hi = lax.optimization_barrier((far_lo, far_hi, mid_lo, mid_hi))
    far_lo = lax.ppermute(far_lo, y_axes, up)
    far_hi = lax.ppermute(far_hi, y_axes, down)
    weights = [jnp.asarray(w) for w in constants()]
    early = early_call(volume, mid_lo, mid_hi, weights)
    mid_lo, mid_hi, *early = lax.optimization_barrier((mid_lo, mid_hi, *early))
    pair_lo = lax.ppermute(mid_lo, x_axes, pair_perm)
    pair_hi = lax.ppermute(mid_hi, x_axes, pair_perm)
    pieces = (far, far_lo, far_hi, pair, pair_lo, pair_hi)
    stats, peaks = late_call(core, weights, pieces, early)
    return score_call(stats, all_peaks(peaks))


def solution(mesh):
    fine = jax.sharding.Mesh(
        mesh.devices.reshape(4, 2, 4, 2, 4), ("zh", "core", "x", "zl", "y")
    )
    spec = P(x_axes, y_axes, None)
    return jax.shard_map(
        per_device, mesh=fine, in_specs=(spec,), out_specs=spec, check_vma=False
    )
```

time: 92.2 us -> 71.8 us (0.78)
  Pallas kernels: 21.1 us -> 13.8 us
  waiting for transfers between devices: 12.3 us -> 6.45 us
  local copies, waits for them, and re-layouts: 6.13 us -> 2.12 us
  blocking collectives: 33.3 us -> 31.1 us
  starting transfers between devices: 18.9 us -> 17.8 us
    ppermute x5 -> x6, waiting for transfers between devices: 11.5 us -> 1.98 us  [the longest x1 1.76 us: per_device(): far_lo = lax.ppermute(far_lo, y_axes, up)]
    pallas_call x1 -> x2, Pallas kernels: 18.3 us -> 11.4 us  [the longest x1 10.3 us: late_call(): pl.pallas_call(late_kernel, out_shape=(jax.ShapeDtypeStruct((12, rows, de...]
    ppermute x1, waiting for transfers between devices: 0.01 us -> 3.35 us  [per_device(): far = lax.ppermute(volume, x_axes, far_perm)]
    unnamed x8 -> x10, local copies, waits for them, and re-layouts: 4.24 us -> 0.94 us
    all_to_all x1, blocking collectives: 33.3 us -> 31.1 us  [all_peaks(): return lax.all_to_all(spread, axes, 0, 0, tiled=True).reshape(peers, depth)]
    ppermute x5 -> x6, starting transfers between devices: 11.1 us -> 11.2 us  [the longest x1 4 us: per_device(): mid_lo = lax.ppermute(volume[:, tail], y_axes, up)]
  transfers between devices with their start and end apart: 8 -> 9, of which waited for: 5 -> 4; matrix products, arithmetic and copies ran while one was open for 2% -> 2% of each run, Pallas kernels for 0% -> 2%
where the time goes in v2:
time: 71.8 us; the launch traced here: 71.5 us
  blocking collectives  31.1 us (43%)
  starting transfers between devices  17.8 us (25%)
  Pallas kernels  13.8 us (19%)
  waiting for transfers between devices  6.45 us (9%)
  local copies, waits for them, and re-layouts  2.12 us (3%)
    all_to_all x1, blocking collectives, all_peaks(): return lax.all_to_all(spread, axes, 0, 0, tiled=True).reshape(peers, depth)  31.1 us
    pallas_call x1, Pallas kernels, late_call(): pl.pallas_call(late_kernel, out_shape=(jax.ShapeDtypeStruct((12, rows, de...  10.3 us
    ppermute x1, starting transfers between devices, per_device(): far = lax.ppermute(volume, x_axes, far_perm)  6.42 us
    ppermute x1, starting transfers between devices, per_device(): mid_lo = lax.ppermute(volume[:, tail], y_axes, up)  4 us
    ppermute x1, starting transfers between devices, per_device(): far_lo = lax.ppermute(far_lo, y_axes, up)  4 us
    ppermute x1, waiting for transfers between devices, per_device(): far = lax.ppermute(volume, x_axes, far_perm)  3.35 us
    pallas_call x1, Pallas kernels, score_call(): pl.pallas_call(score_kernel, out_shape=jax.ShapeDtypeStruct((tile_x, tile...  2.41 us
    ppermute x1, waiting for transfers between devices, per_device(): far_lo = lax.ppermute(far_lo, y_axes, up)  1.76 us
  transfers between devices with their start and end apart: 9, of which 4 were waited for; matrix products, arithmetic and copies ran while one was open for 2% of the time, Pallas kernels for 2%

profile of v2, /device:TPU:1, one launch (start us, length us, event | category | flops | bytes accessed | tf_op | source)
XLA Modules:
  0.0 71.5 jit_solution(14541736165695765587)
XLA Ops:
  0.0 0.0 copy-start
  0.0 0.0 copy-start.2
  0.0 0.0 copy-start.1
  0.0 6.4 %collective-permute-start = (f32[24,32,128]{2,1,0:T(8,128)}, f32[24,32,128]{2,1,0:T(8,128)S(1)}, u32[]{:S(2)}, u32[]{:S(2)}) collective-permute-start(f32[24,32,128]{2,1,0:T(8,128)} %mid), channel_id=1, source_target_pairs={{32,64},{96,128},{160,192},{64,32},{128,96},{192,160},{33,65},{97,... | collective-permute-start | bytes 1179656 | tf_op jit(solution)/shard_map/ppermute | solution.py:288
  6.4 1.1 %fusion = (f32[24,24,128]{2,1,0:T(8,128)S(1)}, f32[24,24,128]{2,1,0:T(8,128)S(1)}) fusion(f32[24,32,128]{2,1,0:T(8,128)} %mid), kind=kLoop, calls=%fused_computation.1 | loop fusion | bytes 1179648 | tf_op jit(solution)/shard_map/slice | solution.py:290
  7.5 1.3 %collective-permute-start.5 = (f32[24,24,128]{2,1,0:T(8,128)S(1)}, f32[24,24,128]{2,1,0:T(8,128)S(1)}, u32[]{:S(2)}, u32[]{:S(2)}) collective-permute-start(f32[24,24,128]{2,1,0:T(8,128)S(1)} %get-tuple-element.37), channel_id=1, source_target_pairs={{1,0},{2,1},{3,2},{4,3},{5,4},{6,5},{7,6},{8,7},{9,8},{10,9},{11,1... | collective-permute-start | bytes 884744 | tf_op jit(solution)/shard_map/ppermute | solution.py:290
  8.8 4.0 %collective-permute-start.4 = (f32[24,24,128]{2,1,0:T(8,128)S(1)}, f32[24,24,128]{2,1,0:T(8,128)S(1)}, u32[]{:S(2)}, u32[]{:S(2)}) collective-permute-start(f32[24,24,128]{2,1,0:T(8,128)S(1)} %get-tuple-element.38), channel_id=1, source_target_pairs={{0,1},{1,2},{2,3},{3,4},{4,5},{5,6},{6,7},{7,8},{8,9},{9,10},{10,1... | collective-permute-start | bytes 884744 | tf_op jit(solution)/shard_map/ppermute | solution.py:289
  12.9 0.1 collective-permute-start.3
  13.0 3.4 %collective-permute-done.far = f32[24,32,128]{2,1,0:T(8,128)S(1)} collective-permute-done((f32[24,32,128]{2,1,0:T(8,128)}, f32[24,32,128]{2,1,0:T(8,128)S(1)}, u32[]{:S(2)}, u32[]{:S(2)}) %collective-permute-start) | collective-permute-done | bytes 393248 | tf_op jit(solution)/shard_map/ppermute | solution.py:288
  16.4 1.3 %collective-permute-start.2 = (f32[24,24,128]{2,1,0:T(8,128)S(1)}, f32[24,24,128]{2,1,0:T(8,128)S(1)}, u32[]{:S(2)}, u32[]{:S(2)}) collective-permute-start(f32[24,24,128]{2,1,0:T(8,128)S(1)} %get-tuple-element.39), channel_id=1, source_target_pairs={{1,0},{2,1},{3,2},{4,3},{5,4},{6,5},{7,6},{8,7},{9,8},{10,9},{11,1... | collective-permute-start | bytes 884744 | tf_op jit(solution)/shard_map/ppermute | solution.py:295
  17.7 4.0 %collective-permute-start.1 = (f32[24,24,128]{2,1,0:T(8,128)S(1)}, f32[24,24,128]{2,1,0:T(8,128)S(1)}, u32[]{:S(2)}, u32[]{:S(2)}) collective-permute-start(f32[24,24,128]{2,1,0:T(8,128)S(1)} %get-tuple-element.40), channel_id=1, source_target_pairs={{0,1},{1,2},{2,3},{3,4},{4,5},{5,6},{6,7},{7,8},{8,9},{9,10},{10,1... | collective-permute-start | bytes 884744 | tf_op jit(solution)/shard_map/ppermute | solution.py:294
  21.7 0.0 collective-permute-done.5.mid_hi
  21.7 0.0 collective-permute-done.4.mid_lo
  21.7 0.0 copy-done
  21.7 0.0 copy-done.2
  21.7 0.0 copy-done.1
  21.7 0.0 copy-start.3
  21.7 0.9 %copy-done.3 = bf16[384,256]{1,0:T(8,128)(2,1)S(1)} copy-done((bf16[384,256]{1,0:T(8,128)(2,1)S(1)}, bf16[384,256]{1,0:T(8,128)(2,1)}, u32[]{:S(2)}) %copy-start.3) | copy-done | bytes 196632
  22.7 1.1 %shard_map.46 = (f32[2496,128]{1,0:T(8,128)S(1)}, f32[2496,128]{1,0:T(8,128)S(1)}, f32[2496,128]{1,0:T(8,128)S(1)}, f32[2496,128]{1,0:T(8,128)S(1)}) custom-call(f32[24,32,128]{2,1,0:T(8,128)S(1)} %copy-done.1, bf16[384,256]{1,0:T(8,128)(2,1)S(1)} %copy-done.3, bf16[2,4,72,256]{3,2,1,0:T(8,128)(2,1)S(1)} %copy-done.2, bf16[12,256,256]{2,1,0:T(8,128)(2,1)S(1)} %copy-done, ...), custom_call_target="tpu_custom_call" | custom-call | tf_op jit(solution)/shard_map/pallas_call | solution.py:229
  23.8 0.1 collective-permute-start.6
  23.9 0.5 collective-permute-start.7
  24.4 0.0 collective-permute-done.3.pair
  24.4 0.2 collective-permute-done.2.far_hi
  24.6 1.8 %collective-permute-done.1.far_lo = f32[24,24,128]{2,1,0:T(8,128)S(1)} collective-permute-done((f32[24,24,128]{2,1,0:T(8,128)S(1)}, f32[24,24,128]{2,1,0:T(8,128)S(1)}, u32[]{:S(2)}, u32[]{:S(2)}) %collective-permute-start.1) | collective-permute-done | bytes 294944 | tf_op jit(solution)/shard_map/ppermute | solution.py:294
  26.3 0.0 collective-permute-done.6.pair_lo
  26.4 0.0 collective-permute-done.7.pair_hi
  26.4 0.0 copy-done.4
  26.4 10.3 %shard_map.47 = (f32[12,768,128]{2,1,0:T(8,128)S(1)}, f32[1,128]{1,0:T(1,128)S(1)}) custom-call(s32[1]{0:T(128)} %bitcast.core_ref, bf16[384,256]{1,0:T(8,128)(2,1)S(1)} %copy-done.4, bf16[2,4,72,256]{3,2,1,0:T(8,128)(2,1)S(1)} %copy-done.2, bf16[12,256,256]{2,1,0:T(8,128)(2,1)S(1)} %copy-done, f32[24,32,128]{2,1,0:T(8,128)S(1)} %collective-permute-done.far, ...), custom_call_target="tpu_custom_call" | custom-call | tf_op jit(solution)/shard_map/pallas_call | solution.py:240
  36.7 0.1 collective-permute-start.8
  36.8 1.1 %collective-permute-done.8 = f32[1,128]{1,0:T(1,128)S(1)} collective-permute-done((f32[1,128]{1,0:T(1,128)S(1)}, f32[1,128]{1,0:T(1,128)S(1)}, u32[]{:S(2)}, u32[]{:S(2)}) %collective-permute-start.8) | collective-permute-done | bytes 544 | tf_op jit(solution)/shard_map/ppermute | solution.py:270
  37.9 31.1 %all_to_all.5 = f32[128,1,128]{2,1,0:T(1,128)S(1)} all-to-all(f32[128,1,128]{2,1,0:T(1,128)S(1)} %broadcast_in_dim.9), channel_id=1, replica_groups=mesh['zh'=4,'core'=2,'x'=4,'zl'=2,'y'=4] {'zh','x','zl','y'}, dimensions={0} | all-to-all | bytes 131072 | tf_op jit(solution)/shard_map/all_to_all | solution.py:274
  69.1 2.4 %shard_map.48 = f32[24,32,128]{2,1,0:T(8,128)} custom-call(f32[12,768,128]{2,1,0:T(8,128)S(1)} %get-tuple-element.35.stats, f32[128,128]{1,0:T(8,128)S(1)} %bitcast.4), custom_call_target="tpu_custom_call" | custom-call | tf_op jit(solution)/shard_map/pallas_call | solution.py:258
  (4 shorter events, 0.1 us)
Async XLA Ops:
  0.0 21.7 %copy-start = (bf16[12,256,256]{2,1,0:T(8,128)(2,1)S(1)}, bf16[12,256,256]{2,1,0:T(8,128)(2,1)}, u32[]{:S(2)}) copy-start(bf16[12,256,256]{2,1,0:T(8,128)(2,1)} %constant.14.clone.wz) | copy-start | bytes 4718596
  0.0 21.7 %copy-start.2 = (bf16[2,4,72,256]{3,2,1,0:T(8,128)(2,1)S(1)}, bf16[2,4,72,256]{3,2,1,0:T(8,128)(2,1)}, u32[]{:S(2)}) copy-start(bf16[2,4,72,256]{3,2,1,0:T(8,128)(2,1)} %constant.13.clone.wx) | copy-start | bytes 884740
  0.0 21.7 %copy-start.1 = (f32[24,32,128]{2,1,0:T(8,128)S(1)}, f32[24,32,128]{2,1,0:T(8,128)}, u32[]{:S(2)}) copy-start(f32[24,32,128]{2,1,0:T(8,128)} %mid) | copy-start | bytes 1179652
  0.0 16.3 %collective-permute-start = (f32[24,32,128]{2,1,0:T(8,128)}, f32[24,32,128]{2,1,0:T(8,128)S(1)}, u32[]{:S(2)}, u32[]{:S(2)}) collective-permute-start(f32[24,32,128]{2,1,0:T(8,128)} %mid), channel_id=1, source_target_pairs={{32,64},{96,128},{160,192},{64,32},{128,96},{192,160},{33,65},{97,... | collective-permute-start | bytes 1179656 | tf_op jit(solution)/shard_map/ppermute | solution.py:288
  7.5 14.1 %collective-permute-start.5 = (f32[24,24,128]{2,1,0:T(8,128)S(1)}, f32[24,24,128]{2,1,0:T(8,128)S(1)}, u32[]{:S(2)}, u32[]{:S(2)}) collective-permute-start(f32[24,24,128]{2,1,0:T(8,128)S(1)} %get-tuple-element.37), channel_id=1, source_target_pairs={{1,0},{2,1},{3,2},{4,3},{5,4},{6,5},{7,6},{8,7},{9,8},{10,9},{11,1... | collective-permute-start | bytes 884744 | tf_op jit(solution)/shard_map/ppermute | solution.py:290
  8.8 12.8 %collective-permute-start.4 = (f32[24,24,128]{2,1,0:T(8,128)S(1)}, f32[24,24,128]{2,1,0:T(8,128)S(1)}, u32[]{:S(2)}, u32[]{:S(2)}) collective-permute-start(f32[24,24,128]{2,1,0:T(8,128)S(1)} %get-tuple-element.38), channel_id=1, source_target_pairs={{0,1},{1,2},{2,3},{3,4},{4,5},{5,6},{6,7},{7,8},{8,9},{9,10},{10,1... | collective-permute-start | bytes 884744 | tf_op jit(solution)/shard_map/ppermute | solution.py:289
  12.9 11.5 %collective-permute-start.3 = (f32[24,32,128]{2,1,0:T(8,128)}, f32[24,32,128]{2,1,0:T(8,128)S(1)}, u32[]{:S(2)}, u32[]{:S(2)}) collective-permute-start(f32[24,32,128]{2,1,0:T(8,128)} %mid), channel_id=1, source_target_pairs={{0,32},{32,0},{64,96},{96,64},{128,160},{160,128},{192,224},{224,1... | collective-permute-start | bytes 1179656 | tf_op jit(solution)/shard_map/ppermute | solution.py:291
  16.4 8.2 %collective-permute-start.2 = (f32[24,24,128]{2,1,0:T(8,128)S(1)}, f32[24,24,128]{2,1,0:T(8,128)S(1)}, u32[]{:S(2)}, u32[]{:S(2)}) collective-permute-start(f32[24,24,128]{2,1,0:T(8,128)S(1)} %get-tuple-element.39), channel_id=1, source_target_pairs={{1,0},{2,1},{3,2},{4,3},{5,4},{6,5},{7,6},{8,7},{9,8},{10,9},{11,1... | collective-permute-start | bytes 884744 | tf_op jit(solution)/shard_map/ppermute | solution.py:295
  17.7 8.7 %collective-permute-start.1 = (f32[24,24,128]{2,1,0:T(8,128)S(1)}, f32[24,24,128]{2,1,0:T(8,128)S(1)}, u32[]{:S(2)}, u32[]{:S(2)}) collective-permute-start(f32[24,24,128]{2,1,0:T(8,128)S(1)} %get-tuple-element.40), channel_id=1, source_target_pairs={{0,1},{1,2},{2,3},{3,4},{4,5},{5,6},{6,7},{7,8},{8,9},{9,10},{10,1... | collective-permute-start | bytes 884744 | tf_op jit(solution)/shard_map/ppermute | solution.py:294
  21.7 0.9 %copy-start.3 = (bf16[384,256]{1,0:T(8,128)(2,1)S(1)}, bf16[384,256]{1,0:T(8,128)(2,1)}, u32[]{:S(2)}) copy-start(bf16[384,256]{1,0:T(8,128)(2,1)} %constant.12.clone.wy) | copy-start | bytes 589828
  22.7 3.7 %copy-start.4 = (bf16[384,256]{1,0:T(8,128)(2,1)S(1)}, bf16[384,256]{1,0:T(8,128)(2,1)}, u32[]{:S(2)}) copy-start(bf16[384,256]{1,0:T(8,128)(2,1)} %constant.12.clone.wy) | copy-start | bytes 589828
  23.8 2.6 %collective-permute-start.6 = (f32[24,24,128]{2,1,0:T(8,128)S(1)}, f32[24,24,128]{2,1,0:T(8,128)S(1)}, u32[]{:S(2)}, u32[]{:S(2)}) collective-permute-start(f32[24,24,128]{2,1,0:T(8,128)S(1)} %collective-permute-done.4.mid_lo), channel_id=1, source_target_pairs={{0,32},{32,0},{64,96},{96,64},{128,160},{160,128},{192,224},{224,1... | collective-permute-start | bytes 884744 | tf_op jit(solution)/shard_map/ppermute | solution.py:299
  23.9 2.5 %collective-permute-start.7 = (f32[24,24,128]{2,1,0:T(8,128)S(1)}, f32[24,24,128]{2,1,0:T(8,128)S(1)}, u32[]{:S(2)}, u32[]{:S(2)}) collective-permute-start(f32[24,24,128]{2,1,0:T(8,128)S(1)} %collective-permute-done.5.mid_hi), channel_id=1, source_target_pairs={{0,32},{32,0},{64,96},{96,64},{128,160},{160,128},{192,224},{224,1... | collective-permute-start | bytes 884744 | tf_op jit(solution)/shard_map/ppermute | solution.py:300
  36.7 1.2 %collective-permute-start.8 = (f32[1,128]{1,0:T(1,128)S(1)}, f32[1,128]{1,0:T(1,128)S(1)}, u32[]{:S(2)}, u32[]{:S(2)}) collective-permute-start(f32[1,128]{1,0:T(1,128)S(1)} %get-tuple-element.36), channel_id=1, source_target_pairs={{0,32},{32,0},{1,33},{33,1},{2,34},{34,2},{3,35},{35,3},{4,36},{36... | collective-permute-start | bytes 1544 | tf_op jit(solution)/shard_map/ppermute | solution.py:270

commit v3 on v2

--- a/solution.py
+++ b/solution.py
@@ -111,30 +111,38 @@
         lax.fori_loop(start, stop, body, 0, unroll=min(4, stop - start))
 
 
-def early_kernel(mid, wy, wx, wz, mid_lo, mid_hi, g8, g4, g2, g1):
+def with_rims(upward, tile, mine, other):
+    above = upward == 1
+    return [jnp.where(above, other, mine), tile, jnp.where(above, mine, other)]
+
+
+def early_kernel(place, mid, wy, wx, wz, got, passed, g8, g4, g2, g1):
+    upward = place[1]
+
     def mid_body(i, carry):
-        at = pl.ds(2 * i, 2)
-        y_step((g8, g4, g2, g1), wy, [mid_lo[at], mid[at], mid_hi[at]], [2 * i] * 4)
+        at, after = pl.ds(2 * i, 2), pl.ds(2 * i + tile_x, 2)
+        parts = with_rims(upward, mid[at], got[at], passed[after])
+        y_step((g8, g4, g2, g1), wy, parts, [2 * i] * 4)
         return carry
 
     lax.fori_loop(0, tile_x // 2, mid_body, 0, unroll=4)
 
 
 def late_kernel(
-    core_ref, wy, wx, wz, far, far_lo, far_hi, pair, pair_lo, pair_hi, g8, g4, g2, g1,
+    place, wy, wx, wz, far, far_got, far_passed, pair, got, passed, g8, g4, g2, g1,
     stats, peaks, f8, f4, f2, f1, mixed,
 ):
     own_fields, fields = (g8, g4, g2, g1), (f8, f4, f2, f1)
-    core = core_ref[0]
+    core, upward = place[0], place[1]
     f8[pl.ds(2 * rim * pitch, 8 * pitch), :] = jnp.zeros((8 * pitch, depth), jnp.float32)
 
     def pair_parts(plane):
-        at = pl.ds(plane, 2)
-        return [pair_lo[at], pair[at], pair_hi[at]]
+        at, after = pl.ds(plane, 2), pl.ds(plane + tile_x, 2)
+        return with_rims(upward, pair[at], got[after], passed[at])
 
     def far_parts(plane):
         at = pl.ds(plane, 2)
-        return [far_lo[at], far[at], far_hi[at]]
+        return with_rims(upward, far[at], far_got[at], far_passed[at])
 
     side_steps(fields, wy, pair_parts, core, [0] * 4)
     side_steps(fields, wy, far_parts, 1 - core, near)
@@ -225,18 +233,18 @@
     return [pl.BlockSpec(memory_space=pltpu.VMEM)] * n
 
 
-def early_call(volume, mid_lo, mid_hi, weights, interpret=False):
+def early_call(place, volume, got, passed, weights, interpret=False):
     return pl.pallas_call(
         early_kernel,
         out_shape=[jax.ShapeDtypeStruct((tile_x * pitch, depth), jnp.float32)] * 4,
-        in_specs=vmem(6),
+        in_specs=[pl.BlockSpec(memory_space=pltpu.SMEM)] + vmem(6),
         out_specs=vmem(4),
         compiler_params=pltpu.CompilerParams(vmem_limit_bytes=16 * mib),
         interpret=interpret,
-    )(volume, *weights, mid_lo, mid_hi)
-
-
-def late_call(core, weights, pieces, early, interpret=False):
+    )(place, volume, *weights, got, passed)
+
+
+def late_call(place, weights, pieces, early, interpret=False):
     return pl.pallas_call(
         late_kernel,
         out_shape=(
@@ -251,7 +259,7 @@
         + [pltpu.VMEM((6, rows, 2 * depth), jnp.bfloat16)],
         compiler_params=pltpu.CompilerParams(vmem_limit_bytes=24 * mib),
         interpret=interpret,
-    )(core, *weights, *pieces, *early)
+    )(place, *weights, *pieces, *early)
 
 
 def score_call(stats, peaks, interpret=False):
@@ -279,27 +287,38 @@
     pair_perm = [(i, i ^ 1) for i in range(n_x)]
     far_perm = [(i, i + 1) for i in range(1, n_x - 1, 2)]
     far_perm += [(j, i) for i, j in far_perm]
-    up = [(i, i + 1) for i in range(n_y - 1)]
-    down = [(j, i) for i, j in up]
-    tail, head = slice(tile_y - rim, tile_y), slice(0, rim)
-
-    core = lax.axis_index("core").reshape(1)
-    volume, core = lax.optimization_barrier((volume, core))
+    trade = [(i, i ^ 1) for i in range(n_y)]
+    trade += [(n_y + i, n_y + i + 1) for i in range(1, n_y - 1, 2)]
+    trade += [(n_y + i + 1, n_y + i) for i in range(1, n_y - 1, 2)]
+
+    core = lax.axis_index("core")
+    upward = 1 - (core ^ (lax.axis_index("y") & 1))
+    place = jnp.stack([core, upward]).astype(jnp.int32)
+    volume, place, above, below = lax.optimization_barrier(
+        (volume, place, upward == 1, upward == 0)
+    )
+
+    def edges(tile, towards):
+        return jnp.where(towards, tile[:, tile_y - rim :], tile[:, :rim])
+
+    def swap(value):
+        return lax.ppermute(value, x_axes, pair_perm)
+
     far = lax.ppermute(volume, x_axes, far_perm)
-    mid_lo = lax.ppermute(volume[:, tail], y_axes, up)
-    mid_hi = lax.ppermute(volume[:, head], y_axes, down)
-    pair = lax.ppermute(volume, x_axes, pair_perm)
-    far_lo, far_hi = far[:, tail], far[:, head]
-    _, _, mid_lo, mid_hi = lax.optimization_barrier((far_lo, far_hi, mid_lo, mid_hi))
-    far_lo = lax.ppermute(far_lo, y_axes, up)
-    far_hi = lax.ppermute(far_hi, y_axes, down)
+    pair = swap(volume)
+    rims = jnp.concatenate([edges(volume, above), edges(pair, above)], axis=0)
+    got = lax.ppermute(rims, ("core",) + y_axes, trade)
+    _, far = lax.optimization_barrier((rims, far))
+    far_rims = jnp.concatenate([edges(far, above), swap(edges(far, below))], axis=0)
+    _, got = lax.optimization_barrier((far_rims, got))
+    far_got = lax.ppermute(far_rims, ("core",) + y_axes, trade)
+    passed = swap(got)
     weights = [jnp.asarray(w) for w in constants()]
-    early = early_call(volume, mid_lo, mid_hi, weights)
-    mid_lo, mid_hi, *early = lax.optimization_barrier((mid_lo, mid_hi, *early))
-    pair_lo = lax.ppermute(mid_lo, x_axes, pair_perm)
-    pair_hi = lax.ppermute(mid_hi, x_axes, pair_perm)
-    pieces = (far, far_lo, far_hi, pair, pair_lo, pair_hi)
-    stats, peaks = late_call(core, weights, pieces, early)
+    early = early_call(place, volume, got, passed, weights)
+    *early, far_got = lax.optimization_barrier((*early, far_got))
+    far_passed = swap(far_got[tile_x:])
+    pieces = (far, far_got, far_passed, pair, got, passed)
+    stats, peaks = late_call(place, weights, pieces, early)
     return score_call(stats, all_peaks(peaks))
 
 

time: 71.8 us -> 76.6 us (1.067)
  waiting for transfers between devices: 6.45 us -> 13.9 us
  blocking collectives: 31.1 us -> 28.7 us
  local copies, waits for them, and re-layouts: 2.12 us -> 0.09 us
  other arithmetic: 0.01 us -> 1.32 us
  Pallas kernels: 13.8 us -> 14.9 us
    ppermute x1, waiting for transfers between devices: 3.35 us -> 9.14 us  [per_device(): far = lax.ppermute(volume, x_axes, far_perm)]
    ppermute x1, starting transfers between devices: 6.42 us -> 3.09 us  [per_device(): far = lax.ppermute(volume, x_axes, far_perm)]
    ppermute x7 -> x6, starting transfers between devices: 11.3 us -> 13.7 us  [the longest x4 12.2 us: swap(): return lax.ppermute(value, x_axes, pair_perm)]
    all_to_all x1, blocking collectives: 31.1 us -> 28.7 us  [all_peaks(): return lax.all_to_all(spread, axes, 0, 0, tiled=True).reshape(peers, depth)]
    ppermute x7 -> x6, waiting for transfers between devices: 1.99 us -> 3.96 us  [the longest x4 3.95 us: swap(): return lax.ppermute(value, x_axes, pair_perm)]
    select_n x0 -> x3, other arithmetic: none -> 1.16 us  [edges(): return jnp.where(towards, tile[:, tile_y - rim:], tile[:, :rim])]
    slice x2 -> x1, local copies, waits for them, and re-layouts: 1.14 us -> 0.02 us  [per_device(): far_passed = swap(far_got[tile_x:])]
    unnamed x10 -> x8, local copies, waits for them, and re-layouts: 0.94 us -> 0.03 us
  transfers between devices with their start and end apart: 9 -> 8, of which waited for: 4 -> 5; matrix products, arithmetic and copies ran while one was open for 2% -> 2% of each run, Pallas kernels for 2% -> 2%
where the time goes in v3:
time: 76.6 us; the launch traced here: 76.4 us
  blocking collectives  28.7 us (37%)
  starting transfers between devices  17.3 us (23%)
  Pallas kernels  14.9 us (19%)
  waiting for transfers between devices  13.9 us (18%)
  other arithmetic  1.32 us (2%)
    all_to_all x1, blocking collectives, all_peaks(): return lax.all_to_all(spread, axes, 0, 0, tiled=True).reshape(peers, depth)  28.7 us
    ppermute x4, starting transfers between devices, swap(): return lax.ppermute(value, x_axes, pair_perm)  12.2 us
    pallas_call x1, Pallas kernels, late_call(): pl.pallas_call(late_kernel, out_shape=(jax.ShapeDtypeStruct((12, rows, de...  10.8 us
    ppermute x1, waiting for transfers between devices, per_device(): far = lax.ppermute(volume, x_axes, far_perm)  9.14 us
    ppermute x4, waiting for transfers between devices, swap(): return lax.ppermute(value, x_axes, pair_perm)  3.95 us
    ppermute x1, starting transfers between devices, per_device(): far = lax.ppermute(volume, x_axes, far_perm)  3.09 us
    pallas_call x1, Pallas kernels, score_call(): pl.pallas_call(score_kernel, out_shape=jax.ShapeDtypeStruct((tile_x, tile...  2.41 us
    pallas_call x1, Pallas kernels, early_call(): pl.pallas_call(early_kernel, out_shape=[jax.ShapeDtypeStruct((tile_x * pi...  1.68 us
  transfers between devices with their start and end apart: 8, of which 5 were waited for; matrix products, arithmetic and copies ran while one was open for 2% of the time, Pallas kernels for 2%

profile of v3, /device:TPU:1, one launch (start us, length us, event | category | flops | bytes accessed | tf_op | source)
XLA Modules:
  0.0 76.4 jit_solution(16958783925233165325)
XLA Ops:
  0.0 0.1 pad_add_fusion.place
  0.1 3.2 %collective-permute-start = (f32[24,32,128]{2,1,0:T(8,128)}, f32[24,32,128]{2,1,0:T(8,128)S(1)}, u32[]{:S(2)}, u32[]{:S(2)}) collective-permute-start(f32[24,32,128]{2,1,0:T(8,128)} %mid), channel_id=1, source_target_pairs={{0,32},{32,0},{64,96},{96,64},{128,160},{160,128},{192,224},{224,1... | collective-permute-start | bytes 1179656 | tf_op jit(solution)/shard_map/ppermute | solution.py:305
  3.3 3.1 %collective-permute-start.1 = (f32[24,32,128]{2,1,0:T(8,128)}, f32[24,32,128]{2,1,0:T(8,128)S(1)}, u32[]{:S(2)}, u32[]{:S(2)}) collective-permute-start(f32[24,32,128]{2,1,0:T(8,128)} %mid), channel_id=1, source_target_pairs={{32,64},{96,128},{160,192},{64,32},{128,96},{192,160},{33,65},{97,... | collective-permute-start | bytes 1179656 | tf_op jit(solution)/shard_map/ppermute | solution.py:307
  6.4 1.1 %slice_select_fusion.1 = f32[24,24,128]{2,1,0:T(8,128)S(1)} fusion(f32[24,32,128]{2,1,0:T(8,128)} %mid, pred[]{:T(512)S(6)} %eq.6), kind=kLoop, calls=%fused_computation.3 | loop fusion | flops 73728 | bytes 884737 | tf_op jit(solution)/shard_map/jit(_where)/select_n | solution.py:302
  7.5 0.0 collective-permute-done.pair
  7.6 0.0 copy-start.3
  7.6 0.0 copy-start
  7.6 0.0 copy-start.1
  7.6 0.0 copy-start.2
  7.7 0.8 %collective-permute-start.3 = (f32[48,24,128]{2,1,0:T(8,128)S(1)}, f32[48,24,128]{2,1,0:T(8,128)S(1)}, u32[]{:S(2)}, u32[]{:S(2)}) collective-permute-start(f32[48,24,128]{2,1,0:T(8,128)S(1)} %pad_maximum_fusion), channel_id=1, source_target_pairs={{0,1},{1,0},{2,3},{3,2},{4,5},{5,4},{6,7},{7,6},{8,9},{9,8},{10,11... | collective-permute-start | bytes 1769480 | tf_op jit(solution)/shard_map/ppermute | solution.py:310
  8.5 9.1 %collective-permute-done.1.far = f32[24,32,128]{2,1,0:T(8,128)S(1)} collective-permute-done((f32[24,32,128]{2,1,0:T(8,128)}, f32[24,32,128]{2,1,0:T(8,128)S(1)}, u32[]{:S(2)}, u32[]{:S(2)}) %collective-permute-start.1) | collective-permute-done | bytes 393248 | tf_op jit(solution)/shard_map/ppermute | solution.py:307
  17.7 0.1 collective-permute-start.2
  17.8 1.6 %collective-permute-done.2 = f32[24,24,128]{2,1,0:T(8,128)S(1)} collective-permute-done((f32[24,24,128]{2,1,0:T(8,128)S(1)}, f32[24,24,128]{2,1,0:T(8,128)S(1)}, u32[]{:S(2)}, u32[]{:S(2)}) %collective-permute-start.2) | collective-permute-done | bytes 294944 | tf_op jit(solution)/shard_map/ppermute | solution.py:305
  19.4 0.0 collective-permute-done.3.got
  19.4 0.2 collective-permute-start.4
  19.6 0.7 collective-permute-start.5
  20.3 1.2 %collective-permute-done.4.passed = f32[48,24,128]{2,1,0:T(8,128)S(1)} collective-permute-done((f32[48,24,128]{2,1,0:T(8,128)S(1)}, f32[48,24,128]{2,1,0:T(8,128)S(1)}, u32[]{:S(2)}, u32[]{:S(2)}) %collective-permute-start.4) | collective-permute-done | bytes 589856 | tf_op jit(solution)/shard_map/ppermute | solution.py:305
  21.5 0.0 copy-done.3
  21.5 0.0 copy-done
  21.5 0.0 copy-done.1
  21.5 0.0 copy-done.2
  21.5 1.7 %shard_map.46 = (f32[2496,128]{1,0:T(8,128)S(1)}, f32[2496,128]{1,0:T(8,128)S(1)}, f32[2496,128]{1,0:T(8,128)S(1)}, f32[2496,128]{1,0:T(8,128)S(1)}) custom-call(s32[2]{0:T(128)S(1)} %pad_add_fusion.place, f32[24,32,128]{2,1,0:T(8,128)S(1)} %copy-done.1, bf16[384,256]{1,0:T(8,128)(2,1)S(1)} %copy-done.3, bf16[2,4,72,256]{3,2,1,0:T(8,128)(2,1)S(1)} %copy-done.2, ...), custom_call_target="tpu_custom_call" | custom-call | tf_op jit(solution)/shard_map/pallas_call | solution.py:237
  23.2 0.0 collective-permute-done.5.far_got
  23.2 8.6 %collective-permute-start.6 = (f32[24,24,128]{2,1,0:T(8,128)S(1)}, f32[24,24,128]{2,1,0:T(8,128)S(1)}, u32[]{:S(2)}, u32[]{:S(2)}) collective-permute-start(f32[24,24,128]{2,1,0:T(8,128)S(1)} %slice.29), channel_id=1, source_target_pairs={{0,32},{32,0},{64,96},{96,64},{128,160},{160,128},{192,224},{224,1... | collective-permute-start | bytes 884744 | tf_op jit(solution)/shard_map/ppermute | solution.py:305
  31.9 1.2 %collective-permute-done.6.far_passed = f32[24,24,128]{2,1,0:T(8,128)S(1)} collective-permute-done((f32[24,24,128]{2,1,0:T(8,128)S(1)}, f32[24,24,128]{2,1,0:T(8,128)S(1)}, u32[]{:S(2)}, u32[]{:S(2)}) %collective-permute-start.6) | collective-permute-done | bytes 294944 | tf_op jit(solution)/shard_map/ppermute | solution.py:305
  33.1 10.8 %shard_map.47 = (f32[12,768,128]{2,1,0:T(8,128)S(1)}, f32[1,128]{1,0:T(1,128)S(1)}) custom-call(s32[2]{0:T(128)S(1)} %pad_add_fusion.place, bf16[384,256]{1,0:T(8,128)(2,1)S(1)} %copy-done.3, bf16[2,4,72,256]{3,2,1,0:T(8,128)(2,1)S(1)} %copy-done.2, bf16[12,256,256]{2,1,0:T(8,128)(2,1)S(1)} %copy-done, f32[24,32,128]{2,1,0:T(8,128)S(1)} %collective-permute-done.1.far, ...), custom_call_target="tpu_custom_call" | custom-call | tf_op jit(solution)/shard_map/pallas_call | solution.py:248
  43.9 0.5 collective-permute-start.7
  44.4 0.8 %collective-permute-done.7 = f32[1,128]{1,0:T(1,128)S(1)} collective-permute-done((f32[1,128]{1,0:T(1,128)S(1)}, f32[1,128]{1,0:T(1,128)S(1)}, u32[]{:S(2)}, u32[]{:S(2)}) %collective-permute-start.7) | collective-permute-done | bytes 544 | tf_op jit(solution)/shard_map/ppermute | solution.py:278
  45.3 28.7 %all_to_all.5 = f32[128,1,128]{2,1,0:T(1,128)S(1)} all-to-all(f32[128,1,128]{2,1,0:T(1,128)S(1)} %broadcast_in_dim.9), channel_id=1, replica_groups=mesh['zh'=4,'core'=2,'x'=4,'zl'=2,'y'=4] {'zh','x','zl','y'}, dimensions={0} | all-to-all | bytes 131072 | tf_op jit(solution)/shard_map/all_to_all | solution.py:282
  74.0 2.4 %shard_map.48 = f32[24,32,128]{2,1,0:T(8,128)} custom-call(f32[12,768,128]{2,1,0:T(8,128)S(1)} %get-tuple-element.37.stats, f32[128,128]{1,0:T(8,128)S(1)} %bitcast.5), custom_call_target="tpu_custom_call" | custom-call | tf_op jit(solution)/shard_map/pallas_call | solution.py:266
  (7 shorter events, 0.2 us)
Async XLA Ops:
  0.1 7.4 %collective-permute-start = (f32[24,32,128]{2,1,0:T(8,128)}, f32[24,32,128]{2,1,0:T(8,128)S(1)}, u32[]{:S(2)}, u32[]{:S(2)}) collective-permute-start(f32[24,32,128]{2,1,0:T(8,128)} %mid), channel_id=1, source_target_pairs={{0,32},{32,0},{64,96},{96,64},{128,160},{160,128},{192,224},{224,1... | collective-permute-start | bytes 1179656 | tf_op jit(solution)/shard_map/ppermute | solution.py:305
  3.3 14.3 %collective-permute-start.1 = (f32[24,32,128]{2,1,0:T(8,128)}, f32[24,32,128]{2,1,0:T(8,128)S(1)}, u32[]{:S(2)}, u32[]{:S(2)}) collective-permute-start(f32[24,32,128]{2,1,0:T(8,128)} %mid), channel_id=1, source_target_pairs={{32,64},{96,128},{160,192},{64,32},{128,96},{192,160},{33,65},{97,... | collective-permute-start | bytes 1179656 | tf_op jit(solution)/shard_map/ppermute | solution.py:307
  7.6 13.9 %copy-start.3 = (bf16[384,256]{1,0:T(8,128)(2,1)S(1)}, bf16[384,256]{1,0:T(8,128)(2,1)}, u32[]{:S(2)}) copy-start(bf16[384,256]{1,0:T(8,128)(2,1)} %constant.20.clone.wy) | copy-start | bytes 589828
  7.6 13.9 %copy-start = (bf16[12,256,256]{2,1,0:T(8,128)(2,1)S(1)}, bf16[12,256,256]{2,1,0:T(8,128)(2,1)}, u32[]{:S(2)}) copy-start(bf16[12,256,256]{2,1,0:T(8,128)(2,1)} %constant.22.clone.wz) | copy-start | bytes 4718596
  7.6 13.9 %copy-start.1 = (f32[24,32,128]{2,1,0:T(8,128)S(1)}, f32[24,32,128]{2,1,0:T(8,128)}, u32[]{:S(2)}) copy-start(f32[24,32,128]{2,1,0:T(8,128)} %mid) | copy-start | bytes 1179652
  7.6 13.9 %copy-start.2 = (bf16[2,4,72,256]{3,2,1,0:T(8,128)(2,1)S(1)}, bf16[2,4,72,256]{3,2,1,0:T(8,128)(2,1)}, u32[]{:S(2)}) copy-start(bf16[2,4,72,256]{3,2,1,0:T(8,128)(2,1)} %constant.21.clone.wx) | copy-start | bytes 884740
  7.7 11.7 %collective-permute-start.3 = (f32[48,24,128]{2,1,0:T(8,128)S(1)}, f32[48,24,128]{2,1,0:T(8,128)S(1)}, u32[]{:S(2)}, u32[]{:S(2)}) collective-permute-start(f32[48,24,128]{2,1,0:T(8,128)S(1)} %pad_maximum_fusion), channel_id=1, source_target_pairs={{0,1},{1,0},{2,3},{3,2},{4,5},{5,4},{6,7},{7,6},{8,9},{9,8},{10,11... | collective-permute-start | bytes 1769480 | tf_op jit(solution)/shard_map/ppermute | solution.py:310
  17.7 1.7 %collective-permute-start.2 = (f32[24,24,128]{2,1,0:T(8,128)S(1)}, f32[24,24,128]{2,1,0:T(8,128)S(1)}, u32[]{:S(2)}, u32[]{:S(2)}) collective-permute-start(f32[24,24,128]{2,1,0:T(8,128)S(1)} %get-tuple-element.40), channel_id=1, source_target_pairs={{0,32},{32,0},{64,96},{96,64},{128,160},{160,128},{192,224},{224,1... | collective-permute-start | bytes 884744 | tf_op jit(solution)/shard_map/ppermute | solution.py:305
  19.4 2.1 %collective-permute-start.4 = (f32[48,24,128]{2,1,0:T(8,128)S(1)}, f32[48,24,128]{2,1,0:T(8,128)S(1)}, u32[]{:S(2)}, u32[]{:S(2)}) collective-permute-start(f32[48,24,128]{2,1,0:T(8,128)S(1)} %collective-permute-done.3.got), channel_id=1, source_target_pairs={{0,32},{32,0},{64,96},{96,64},{128,160},{160,128},{192,224},{224,1... | collective-permute-start | bytes 1769480 | tf_op jit(solution)/shard_map/ppermute | solution.py:305
  19.6 3.6 %collective-permute-start.5 = (f32[48,24,128]{2,1,0:T(8,128)S(1)}, f32[48,24,128]{2,1,0:T(8,128)S(1)}, u32[]{:S(2)}, u32[]{:S(2)}) collective-permute-start(f32[48,24,128]{2,1,0:T(8,128)S(1)} %pad_maximum_fusion.1), channel_id=1, source_target_pairs={{0,1},{1,0},{2,3},{3,2},{4,5},{5,4},{6,7},{7,6},{8,9},{9,8},{10,11... | collective-permute-start | bytes 1769480 | tf_op jit(solution)/shard_map/ppermute | solution.py:314
  23.2 9.8 %collective-permute-start.6 = (f32[24,24,128]{2,1,0:T(8,128)S(1)}, f32[24,24,128]{2,1,0:T(8,128)S(1)}, u32[]{:S(2)}, u32[]{:S(2)}) collective-permute-start(f32[24,24,128]{2,1,0:T(8,128)S(1)} %slice.29), channel_id=1, source_target_pairs={{0,32},{32,0},{64,96},{96,64},{128,160},{160,128},{192,224},{224,1... | collective-permute-start | bytes 884744 | tf_op jit(solution)/shard_map/ppermute | solution.py:305
  43.9 1.3 %collective-permute-start.7 = (f32[1,128]{1,0:T(1,128)S(1)}, f32[1,128]{1,0:T(1,128)S(1)}, u32[]{:S(2)}, u32[]{:S(2)}) collective-permute-start(f32[1,128]{1,0:T(1,128)S(1)} %get-tuple-element.38), channel_id=1, source_target_pairs={{0,32},{32,0},{1,33},{33,1},{2,34},{34,2},{3,35},{35,3},{4,36},{36... | collective-permute-start | bytes 1544 | tf_op jit(solution)/shard_map/ppermute | solution.py:278

commit v4 on v2

--- a/solution.py
+++ b/solution.py
@@ -111,33 +111,46 @@
         lax.fori_loop(start, stop, body, 0, unroll=min(4, stop - start))
 
 
-def early_kernel(mid, wy, wx, wz, mid_lo, mid_hi, g8, g4, g2, g1):
-    def mid_body(i, carry):
-        at = pl.ds(2 * i, 2)
-        y_step((g8, g4, g2, g1), wy, [mid_lo[at], mid[at], mid_hi[at]], [2 * i] * 4)
-        return carry
-
-    lax.fori_loop(0, tile_x // 2, mid_body, 0, unroll=4)
+def by_parity(place, step, near_rim, wrap_rim):
+    for odd, rims in ((0, (wrap_rim, near_rim)), (1, (near_rim, wrap_rim))):
+
+        @pl.when(place[1] == odd)
+        def _(rims=rims):
+            step(*rims)
+
+
+def early_kernel(place, mid, wy, wx, wz, mid_near, mid_wrap, g8, g4, g2, g1):
+    def step(low, high):
+        def body(i, carry):
+            at = pl.ds(2 * i, 2)
+            y_step((g8, g4, g2, g1), wy, [low[at], mid[at], high[at]], [2 * i] * 4)
+            return carry
+
+        lax.fori_loop(0, tile_x // 2, body, 0, unroll=4)
+
+    by_parity(place, step, mid_near, mid_wrap)
 
 
 def late_kernel(
-    core_ref, wy, wx, wz, far, far_lo, far_hi, pair, pair_lo, pair_hi, g8, g4, g2, g1,
+    place, wy, wx, wz, far, far_near, far_wrap, pair, pair_near, pair_wrap, g8, g4, g2, g1,
     stats, peaks, f8, f4, f2, f1, mixed,
 ):
     own_fields, fields = (g8, g4, g2, g1), (f8, f4, f2, f1)
-    core = core_ref[0]
+    core = place[0]
     f8[pl.ds(2 * rim * pitch, 8 * pitch), :] = jnp.zeros((8 * pitch, depth), jnp.float32)
 
-    def pair_parts(plane):
-        at = pl.ds(plane, 2)
-        return [pair_lo[at], pair[at], pair_hi[at]]
-
-    def far_parts(plane):
-        at = pl.ds(plane, 2)
-        return [far_lo[at], far[at], far_hi[at]]
-
-    side_steps(fields, wy, pair_parts, core, [0] * 4)
-    side_steps(fields, wy, far_parts, 1 - core, near)
+    def side(tile, before, base):
+        def step(low, high):
+            def parts(plane):
+                at = pl.ds(plane, 2)
+                return [low[at], tile[at], high[at]]
+
+            side_steps(fields, wy, parts, before, base)
+
+        return step
+
+    by_parity(place, side(pair, core, [0] * 4), pair_near, pair_wrap)
+    by_parity(place, side(far, 1 - core, near), far_near, far_wrap)
 
     lane = lax.broadcasted_iota(jnp.int32, (1, depth), 1)
     peak_row = jnp.zeros((1, depth), jnp.float32)
@@ -167,7 +180,7 @@
                     mixed[first + k, at, depth : 2 * depth] = lo
             return carry
 
-        lax.fori_loop(0, tile_y // 2, x_body, 0, unroll=4)
+        lax.fori_loop(0, tile_y // 2, x_body, 0, unroll=8)
 
         def z_body(c, best, level=level):
             at = pl.ds(pl.multiple_of(c * z_rows, z_rows), z_rows)
@@ -225,18 +238,18 @@
     return [pl.BlockSpec(memory_space=pltpu.VMEM)] * n
 
 
-def early_call(volume, mid_lo, mid_hi, weights, interpret=False):
+def early_call(place, volume, mid_near, mid_wrap, weights, interpret=False):
     return pl.pallas_call(
         early_kernel,
         out_shape=[jax.ShapeDtypeStruct((tile_x * pitch, depth), jnp.float32)] * 4,
-        in_specs=vmem(6),
+        in_specs=[pl.BlockSpec(memory_space=pltpu.SMEM)] + vmem(6),
         out_specs=vmem(4),
         compiler_params=pltpu.CompilerParams(vmem_limit_bytes=16 * mib),
         interpret=interpret,
-    )(volume, *weights, mid_lo, mid_hi)
-
-
-def late_call(core, weights, pieces, early, interpret=False):
+    )(place, volume, *weights, mid_near, mid_wrap)
+
+
+def late_call(place, weights, pieces, early, interpret=False):
     return pl.pallas_call(
         late_kernel,
         out_shape=(
@@ -251,7 +264,7 @@
         + [pltpu.VMEM((6, rows, 2 * depth), jnp.bfloat16)],
         compiler_params=pltpu.CompilerParams(vmem_limit_bytes=24 * mib),
         interpret=interpret,
-    )(core, *weights, *pieces, *early)
+    )(place, *weights, *pieces, *early)
 
 
 def score_call(stats, peaks, interpret=False):
@@ -267,8 +280,7 @@
 
 
 def all_peaks(row):
-    row = jnp.maximum(row, lax.ppermute(row, "core", [(0, 1), (1, 0)]))
-    axes = ("zh", "x", "zl", "y")
+    axes = x_axes + y_axes
     peers = lax.axis_size(axes)
     spread = jnp.broadcast_to(row[None], (peers, 1, depth))
     return lax.all_to_all(spread, axes, 0, 0, tiled=True).reshape(peers, depth)
@@ -279,27 +291,32 @@
     pair_perm = [(i, i ^ 1) for i in range(n_x)]
     far_perm = [(i, i + 1) for i in range(1, n_x - 1, 2)]
     far_perm += [(j, i) for i, j in far_perm]
-    up = [(i, i + 1) for i in range(n_y - 1)]
-    down = [(j, i) for i, j in up]
-    tail, head = slice(tile_y - rim, tile_y), slice(0, rim)
-
-    core = lax.axis_index("core").reshape(1)
-    volume, core = lax.optimization_barrier((volume, core))
+    near_perm = [(i, i ^ 1) for i in range(n_y)]
+    wrap_perm = [(i, i + 1) for i in range(1, n_y - 1, 2)]
+    wrap_perm += [(j, i) for i, j in wrap_perm]
+
+    odd = lax.axis_index("y") & 1
+    place = jnp.stack([lax.axis_index("core"), odd]).astype(jnp.int32)
+    volume, place, is_odd, is_even = lax.optimization_barrier((volume, place, odd == 1, odd == 0))
+
+    def edge(tile, top):
+        return jnp.where(top, tile[:, tile_y - rim :], tile[:, :rim])
+
     far = lax.ppermute(volume, x_axes, far_perm)
-    mid_lo = lax.ppermute(volume[:, tail], y_axes, up)
-    mid_hi = lax.ppermute(volume[:, head], y_axes, down)
+    mid_wrap = lax.ppermute(edge(volume, is_odd), y_axes, wrap_perm)
+    mid_near = lax.ppermute(edge(volume, is_even), y_axes, near_perm)
     pair = lax.ppermute(volume, x_axes, pair_perm)
-    far_lo, far_hi = far[:, tail], far[:, head]
-    _, _, mid_lo, mid_hi = lax.optimization_barrier((far_lo, far_hi, mid_lo, mid_hi))
-    far_lo = lax.ppermute(far_lo, y_axes, up)
-    far_hi = lax.ppermute(far_hi, y_axes, down)
+    far_wrap, far_near = edge(far, is_odd), edge(far, is_even)
+    _, _, mid_wrap, mid_near = lax.optimization_barrier((far_wrap, far_near, mid_wrap, mid_near))
+    far_wrap = lax.ppermute(far_wrap, y_axes, wrap_perm)
+    far_near = lax.ppermute(far_near, y_axes, near_perm)
     weights = [jnp.asarray(w) for w in constants()]
-    early = early_call(volume, mid_lo, mid_hi, weights)
-    mid_lo, mid_hi, *early = lax.optimization_barrier((mid_lo, mid_hi, *early))
-    pair_lo = lax.ppermute(mid_lo, x_axes, pair_perm)
-    pair_hi = lax.ppermute(mid_hi, x_axes, pair_perm)
-    pieces = (far, far_lo, far_hi, pair, pair_lo, pair_hi)
-    stats, peaks = late_call(core, weights, pieces, early)
+    early = early_call(place, volume, mid_near, mid_wrap, weights)
+    mid_near, mid_wrap, *early = lax.optimization_barrier((mid_near, mid_wrap, *early))
+    pair_near = lax.ppermute(mid_near, x_axes, pair_perm)
+    pair_wrap = lax.ppermute(mid_wrap, x_axes, pair_perm)
+    pieces = (far, far_near, far_wrap, pair, pair_near, pair_wrap)
+    stats, peaks = late_call(place, weights, pieces, early)
     return score_call(stats, all_peaks(peaks))
 
 

time: 71.8 us -> 70.9 us (0.987)
  starting transfers between devices: 17.8 us -> 13.7 us
  waiting for transfers between devices: 6.45 us -> 8.1 us
  other arithmetic: 0.01 us -> 1.22 us
  local copies, waits for them, and re-layouts: 2.12 us -> 1.01 us
  Pallas kernels: 13.8 us -> 14.7 us
    ppermute x7 -> x6, starting transfers between devices: 11.3 us -> 7.23 us  [the longest x1 3.91 us: per_device(): far_near = lax.ppermute(far_near, y_axes, near_perm)]
    ppermute x1, waiting for transfers between devices: 3.35 us -> 6.6 us  [per_device(): far = lax.ppermute(volume, x_axes, far_perm)]
    ppermute x7 -> x6, waiting for transfers between devices: 3.09 us -> 1.49 us  [the longest x1 0.85 us: per_device(): far_near = lax.ppermute(far_near, y_axes, near_perm)]
    select_n x0 -> x2, other arithmetic: none -> 1.14 us  [edge(): return jnp.where(top, tile[:, tile_y - rim:], tile[:, :rim])]
    slice x2 -> x0, local copies, waits for them, and re-layouts: 1.14 us -> none  [the longest x1 1.1 us: per_device(): mid_hi = lax.ppermute(volume[:, head], y_axes, down)]
  transfers between devices with their start and end apart: 9 -> 8, of which waited for: 4 -> 4; matrix products, arithmetic and copies ran while one was open for 2% -> 2% of each run, Pallas kernels for 2% -> 2%
where the time goes in v4:
time: 70.9 us; the launch traced here: 70.7 us
  blocking collectives  31.8 us (45%)
  Pallas kernels  14.7 us (21%)
  starting transfers between devices  13.7 us (19%)
  waiting for transfers between devices  8.1 us (11%)
  other arithmetic  1.22 us (2%)
  local copies, waits for them, and re-layouts  1.01 us (1%)
    all_to_all x1, blocking collectives, all_peaks(): return lax.all_to_all(spread, axes, 0, 0, tiled=True).reshape(peers, depth)  31.8 us
    pallas_call x1, Pallas kernels, late_call(): pl.pallas_call(late_kernel, out_shape=(jax.ShapeDtypeStruct((12, rows, de...  10.6 us
    ppermute x1, waiting for transfers between devices, per_device(): far = lax.ppermute(volume, x_axes, far_perm)  6.6 us
    ppermute x1, starting transfers between devices, per_device(): far = lax.ppermute(volume, x_axes, far_perm)  6.41 us
    ppermute x1, starting transfers between devices, per_device(): far_near = lax.ppermute(far_near, y_axes, near_perm)  3.91 us
    pallas_call x1, Pallas kernels, score_call(): pl.pallas_call(score_kernel, out_shape=jax.ShapeDtypeStruct((tile_x, tile...  2.42 us
    pallas_call x1, Pallas kernels, early_call(): pl.pallas_call(early_kernel, out_shape=[jax.ShapeDtypeStruct((tile_x * pi...  1.68 us
  transfers between devices with their start and end apart: 8, of which 4 were waited for; matrix products, arithmetic and copies ran while one was open for 2% of the time, Pallas kernels for 2%

profile of v4, /device:TPU:1, one launch (start us, length us, event | category | flops | bytes accessed | tf_op | source)
XLA Modules:
  0.0 70.7 jit_solution(4973123011486967738)
XLA Ops:
  0.0 0.0 copy-start
  0.0 0.0 copy-start.2
  0.0 0.0 copy-start.1
  0.0 0.1 pad_add_fusion.place
  0.1 6.4 %collective-permute-start = (f32[24,32,128]{2,1,0:T(8,128)}, f32[24,32,128]{2,1,0:T(8,128)S(1)}, u32[]{:S(2)}, u32[]{:S(2)}) collective-permute-start(f32[24,32,128]{2,1,0:T(8,128)} %mid), channel_id=1, source_target_pairs={{32,64},{96,128},{160,192},{64,32},{128,96},{192,160},{33,65},{97,... | collective-permute-start | bytes 1179656 | tf_op jit(solution)/shard_map/ppermute | solution.py:305
  6.5 1.1 %slice_select_fusion.2 = (f32[24,24,128]{2,1,0:T(8,128)S(1)}, f32[24,24,128]{2,1,0:T(8,128)S(1)}) fusion(f32[24,32,128]{2,1,0:T(8,128)} %mid, pred[]{:T(512)S(6)} %eq.7, pred[]{:T(512)S(6)} %eq.6), kind=kLoop, calls=%fused_computation.2 | loop fusion | flops 147456 | bytes 1179650 | tf_op jit(solution)/shard_map/jit(_where)/select_n | solution.py:303
  7.6 1.4 %collective-permute-start.5 = (f32[24,24,128]{2,1,0:T(8,128)S(1)}, f32[24,24,128]{2,1,0:T(8,128)S(1)}, u32[]{:S(2)}, u32[]{:S(2)}) collective-permute-start(f32[24,24,128]{2,1,0:T(8,128)S(1)} %get-tuple-element.41), channel_id=1, source_target_pairs={{0,1},{1,0},{2,3},{3,2},{4,5},{5,4},{6,7},{7,6},{8,9},{9,8},{10,11... | collective-permute-start | bytes 884744 | tf_op jit(solution)/shard_map/ppermute | solution.py:307
  9.0 0.7 collective-permute-start.4
  9.7 0.1 collective-permute-start.3
  9.8 6.6 %collective-permute-done.far = f32[24,32,128]{2,1,0:T(8,128)S(1)} collective-permute-done((f32[24,32,128]{2,1,0:T(8,128)}, f32[24,32,128]{2,1,0:T(8,128)S(1)}, u32[]{:S(2)}, u32[]{:S(2)}) %collective-permute-start) | collective-permute-done | bytes 393248 | tf_op jit(solution)/shard_map/ppermute | solution.py:305
  16.4 0.7 collective-permute-start.2
  17.1 3.9 %collective-permute-start.1 = (f32[24,24,128]{2,1,0:T(8,128)S(1)}, f32[24,24,128]{2,1,0:T(8,128)S(1)}, u32[]{:S(2)}, u32[]{:S(2)}) collective-permute-start(f32[24,24,128]{2,1,0:T(8,128)S(1)} %get-tuple-element.44), channel_id=1, source_target_pairs={{0,1},{1,0},{2,3},{3,2},{4,5},{5,4},{6,7},{7,6},{8,9},{9,8},{10,11... | collective-permute-start | bytes 884744 | tf_op jit(solution)/shard_map/ppermute | solution.py:312
  21.0 0.0 collective-permute-done.5.mid_near
  21.0 0.0 collective-permute-done.4.mid_wrap
  21.0 0.0 copy-done
  21.0 0.0 copy-done.2
  21.0 0.0 copy-done.1
  21.1 0.0 copy-start.3
  21.1 0.9 %copy-done.3 = bf16[384,256]{1,0:T(8,128)(2,1)S(1)} copy-done((bf16[384,256]{1,0:T(8,128)(2,1)S(1)}, bf16[384,256]{1,0:T(8,128)(2,1)}, u32[]{:S(2)}) %copy-start.3) | copy-done | bytes 196632
  22.0 1.7 %shard_map.46 = (f32[2496,128]{1,0:T(8,128)S(1)}, f32[2496,128]{1,0:T(8,128)S(1)}, f32[2496,128]{1,0:T(8,128)S(1)}, f32[2496,128]{1,0:T(8,128)S(1)}) custom-call(s32[2]{0:T(128)S(1)} %pad_add_fusion.place, f32[24,32,128]{2,1,0:T(8,128)S(1)} %copy-done.1, bf16[384,256]{1,0:T(8,128)(2,1)S(1)} %copy-done.3, bf16[2,4,72,256]{3,2,1,0:T(8,128)(2,1)S(1)} %copy-done.2, ...), custom_call_target="tpu_custom_call" | custom-call | tf_op jit(solution)/shard_map/pallas_call | solution.py:242
  23.7 0.1 collective-permute-start.6
  23.8 0.5 collective-permute-start.7
  24.3 0.0 collective-permute-done.3.pair
  24.3 0.0 collective-permute-done.2.far_wrap
  24.3 0.9 %collective-permute-done.1.far_near = f32[24,24,128]{2,1,0:T(8,128)S(1)} collective-permute-done((f32[24,24,128]{2,1,0:T(8,128)S(1)}, f32[24,24,128]{2,1,0:T(8,128)S(1)}, u32[]{:S(2)}, u32[]{:S(2)}) %collective-permute-start.1) | collective-permute-done | bytes 294944 | tf_op jit(solution)/shard_map/ppermute | solution.py:312
  25.1 0.2 collective-permute-done.6.pair_near
  25.4 0.4 collective-permute-done.7.pair_wrap
  25.8 0.0 copy-done.4
  25.8 10.6 %shard_map.47 = (f32[12,768,128]{2,1,0:T(8,128)S(1)}, f32[1,128]{1,0:T(1,128)S(1)}) custom-call(s32[2]{0:T(128)S(1)} %pad_add_fusion.place, bf16[384,256]{1,0:T(8,128)(2,1)S(1)} %copy-done.4, bf16[2,4,72,256]{3,2,1,0:T(8,128)(2,1)S(1)} %copy-done.2, bf16[12,256,256]{2,1,0:T(8,128)(2,1)S(1)} %copy-done, f32[24,32,128]{2,1,0:T(8,128)S(1)} %collective-permute-done.far, ...), custom_call_target="tpu_custom_call" | custom-call | tf_op jit(solution)/shard_map/pallas_call | solution.py:253
  36.4 0.1 broadcast_in_dim.9
  36.5 31.8 %all_to_all.5 = f32[256,1,128]{2,1,0:T(1,128)S(1)} all-to-all(f32[256,1,128]{2,1,0:T(1,128)S(1)} %broadcast_in_dim.9), channel_id=1, replica_groups=mesh['zh'=4,'core'=2,'x'=4,'zl'=2,'y'=4] {'zh','core','x','zl','y'}, dimensions={0} | all-to-all | bytes 262144 | tf_op jit(solution)/shard_map/all_to_all | solution.py:286
  68.2 2.4 %shard_map.48 = f32[24,32,128]{2,1,0:T(8,128)} custom-call(f32[12,768,128]{2,1,0:T(8,128)S(1)} %get-tuple-element.39.stats, f32[256,128]{1,0:T(8,128)S(1)} %bitcast.4), custom_call_target="tpu_custom_call" | custom-call | tf_op jit(solution)/shard_map/pallas_call | solution.py:271
  (2 shorter events, 0.0 us)
Async XLA Ops:
  0.0 21.0 %copy-start = (bf16[12,256,256]{2,1,0:T(8,128)(2,1)S(1)}, bf16[12,256,256]{2,1,0:T(8,128)(2,1)}, u32[]{:S(2)}) copy-start(bf16[12,256,256]{2,1,0:T(8,128)(2,1)} %constant.22.clone.wz) | copy-start | bytes 4718596
  0.0 21.0 %copy-start.2 = (bf16[2,4,72,256]{3,2,1,0:T(8,128)(2,1)S(1)}, bf16[2,4,72,256]{3,2,1,0:T(8,128)(2,1)}, u32[]{:S(2)}) copy-start(bf16[2,4,72,256]{3,2,1,0:T(8,128)(2,1)} %constant.21.clone.wx) | copy-start | bytes 884740
  0.0 21.0 %copy-start.1 = (f32[24,32,128]{2,1,0:T(8,128)S(1)}, f32[24,32,128]{2,1,0:T(8,128)}, u32[]{:S(2)}) copy-start(f32[24,32,128]{2,1,0:T(8,128)} %mid) | copy-start | bytes 1179652
  0.1 16.3 %collective-permute-start = (f32[24,32,128]{2,1,0:T(8,128)}, f32[24,32,128]{2,1,0:T(8,128)S(1)}, u32[]{:S(2)}, u32[]{:S(2)}) collective-permute-start(f32[24,32,128]{2,1,0:T(8,128)} %mid), channel_id=1, source_target_pairs={{32,64},{96,128},{160,192},{64,32},{128,96},{192,160},{33,65},{97,... | collective-permute-start | bytes 1179656 | tf_op jit(solution)/shard_map/ppermute | solution.py:305
  7.6 13.4 %collective-permute-start.5 = (f32[24,24,128]{2,1,0:T(8,128)S(1)}, f32[24,24,128]{2,1,0:T(8,128)S(1)}, u32[]{:S(2)}, u32[]{:S(2)}) collective-permute-start(f32[24,24,128]{2,1,0:T(8,128)S(1)} %get-tuple-element.41), channel_id=1, source_target_pairs={{0,1},{1,0},{2,3},{3,2},{4,5},{5,4},{6,7},{7,6},{8,9},{9,8},{10,11... | collective-permute-start | bytes 884744 | tf_op jit(solution)/shard_map/ppermute | solution.py:307
  9.0 12.0 %collective-permute-start.4 = (f32[24,24,128]{2,1,0:T(8,128)S(1)}, f32[24,24,128]{2,1,0:T(8,128)S(1)}, u32[]{:S(2)}, u32[]{:S(2)}) collective-permute-start(f32[24,24,128]{2,1,0:T(8,128)S(1)} %get-tuple-element.42), channel_id=1, source_target_pairs={{1,2},{3,4},{5,6},{7,8},{9,10},{11,12},{13,14},{15,16},{17,18},{19... | collective-permute-start | bytes 884744 | tf_op jit(solution)/shard_map/ppermute | solution.py:306
  9.7 14.6 %collective-permute-start.3 = (f32[24,32,128]{2,1,0:T(8,128)}, f32[24,32,128]{2,1,0:T(8,128)S(1)}, u32[]{:S(2)}, u32[]{:S(2)}) collective-permute-start(f32[24,32,128]{2,1,0:T(8,128)} %mid), channel_id=1, source_target_pairs={{0,32},{32,0},{64,96},{96,64},{128,160},{160,128},{192,224},{224,1... | collective-permute-start | bytes 1179656 | tf_op jit(solution)/shard_map/ppermute | solution.py:308
  16.4 7.9 %collective-permute-start.2 = (f32[24,24,128]{2,1,0:T(8,128)S(1)}, f32[24,24,128]{2,1,0:T(8,128)S(1)}, u32[]{:S(2)}, u32[]{:S(2)}) collective-permute-start(f32[24,24,128]{2,1,0:T(8,128)S(1)} %get-tuple-element.43), channel_id=1, source_target_pairs={{1,2},{3,4},{5,6},{7,8},{9,10},{11,12},{13,14},{15,16},{17,18},{19... | collective-permute-start | bytes 884744 | tf_op jit(solution)/shard_map/ppermute | solution.py:311
  17.1 8.0 %collective-permute-start.1 = (f32[24,24,128]{2,1,0:T(8,128)S(1)}, f32[24,24,128]{2,1,0:T(8,128)S(1)}, u32[]{:S(2)}, u32[]{:S(2)}) collective-permute-start(f32[24,24,128]{2,1,0:T(8,128)S(1)} %get-tuple-element.44), channel_id=1, source_target_pairs={{0,1},{1,0},{2,3},{3,2},{4,5},{5,4},{6,7},{7,6},{8,9},{9,8},{10,11... | collective-permute-start | bytes 884744 | tf_op jit(solution)/shard_map/ppermute | solution.py:312
  21.1 0.9 %copy-start.3 = (bf16[384,256]{1,0:T(8,128)(2,1)S(1)}, bf16[384,256]{1,0:T(8,128)(2,1)}, u32[]{:S(2)}) copy-start(bf16[384,256]{1,0:T(8,128)(2,1)} %constant.20.clone.wy) | copy-start | bytes 589828
  22.0 3.8 %copy-start.4 = (bf16[384,256]{1,0:T(8,128)(2,1)S(1)}, bf16[384,256]{1,0:T(8,128)(2,1)}, u32[]{:S(2)}) copy-start(bf16[384,256]{1,0:T(8,128)(2,1)} %constant.20.clone.wy) | copy-start | bytes 589828
  23.7 1.7 %collective-permute-start.6 = (f32[24,24,128]{2,1,0:T(8,128)S(1)}, f32[24,24,128]{2,1,0:T(8,128)S(1)}, u32[]{:S(2)}, u32[]{:S(2)}) collective-permute-start(f32[24,24,128]{2,1,0:T(8,128)S(1)} %collective-permute-done.5.mid_near), channel_id=1, source_target_pairs={{0,32},{32,0},{64,96},{96,64},{128,160},{160,128},{192,224},{224,1... | collective-permute-start | bytes 884744 | tf_op jit(solution)/shard_map/ppermute | solution.py:316
  23.8 2.0 %collective-permute-start.7 = (f32[24,24,128]{2,1,0:T(8,128)S(1)}, f32[24,24,128]{2,1,0:T(8,128)S(1)}, u32[]{:S(2)}, u32[]{:S(2)}) collective-permute-start(f32[24,24,128]{2,1,0:T(8,128)S(1)} %collective-permute-done.4.mid_wrap), channel_id=1, source_target_pairs={{0,32},{32,0},{64,96},{96,64},{128,160},{160,128},{192,224},{224,1... | collective-permute-start | bytes 884744 | tf_op jit(solution)/shard_map/ppermute | solution.py:317

commit v5 on v4

--- a/solution.py
+++ b/solution.py
@@ -111,15 +111,15 @@
         lax.fori_loop(start, stop, body, 0, unroll=min(4, stop - start))
 
 
-def by_parity(place, step, near_rim, wrap_rim):
+def by_parity(odd_ref, step, near_rim, wrap_rim):
     for odd, rims in ((0, (wrap_rim, near_rim)), (1, (near_rim, wrap_rim))):
 
-        @pl.when(place[1] == odd)
+        @pl.when(odd_ref[0] == odd)
         def _(rims=rims):
             step(*rims)
 
 
-def early_kernel(place, mid, wy, wx, wz, mid_near, mid_wrap, g8, g4, g2, g1):
+def early_kernel(odd_ref, mid, wy, wx, wz, mid_near, mid_wrap, g8, g4, g2, g1):
     def step(low, high):
         def body(i, carry):
             at = pl.ds(2 * i, 2)
@@ -128,15 +128,15 @@
 
         lax.fori_loop(0, tile_x // 2, body, 0, unroll=4)
 
-    by_parity(place, step, mid_near, mid_wrap)
+    by_parity(odd_ref, step, mid_near, mid_wrap)
 
 
 def late_kernel(
-    place, wy, wx, wz, far, far_near, far_wrap, pair, pair_near, pair_wrap, g8, g4, g2, g1,
+    core_ref, odd_ref, wy, wx, wz, far, far_near, far_wrap, pair, pair_near, pair_wrap, g8, g4, g2, g1,
     stats, peaks, f8, f4, f2, f1, mixed,
 ):
     own_fields, fields = (g8, g4, g2, g1), (f8, f4, f2, f1)
-    core = place[0]
+    core = core_ref[0]
     f8[pl.ds(2 * rim * pitch, 8 * pitch), :] = jnp.zeros((8 * pitch, depth), jnp.float32)
 
     def side(tile, before, base):
@@ -149,8 +149,8 @@
 
         return step
 
-    by_parity(place, side(pair, core, [0] * 4), pair_near, pair_wrap)
-    by_parity(place, side(far, 1 - core, near), far_near, far_wrap)
+    by_parity(odd_ref, side(pair, core, [0] * 4), pair_near, pair_wrap)
+    by_parity(odd_ref, side(far, 1 - core, near), far_near, far_wrap)
 
     lane = lax.broadcasted_iota(jnp.int32, (1, depth), 1)
     peak_row = jnp.zeros((1, depth), jnp.float32)
@@ -180,7 +180,7 @@
                     mixed[first + k, at, depth : 2 * depth] = lo
             return carry
 
-        lax.fori_loop(0, tile_y // 2, x_body, 0, unroll=8)
+        lax.fori_loop(0, tile_y // 2, x_body, 0, unroll=16)
 
         def z_body(c, best, level=level):
             at = pl.ds(pl.multiple_of(c * z_rows, z_rows), z_rows)
@@ -201,7 +201,7 @@
             stats[3 * level + 2, at, :] = energy
             return jnp.maximum(best, jnp.max(energy.reshape(z_rows // 8, 8, depth), axis=0))
 
-        best = lax.fori_loop(0, rows // z_rows, z_body, jnp.zeros((8, depth), jnp.float32), unroll=2)
+        best = lax.fori_loop(0, rows // z_rows, z_body, jnp.zeros((8, depth), jnp.float32), unroll=4)
         peak_row = jnp.where(lane == level, jnp.max(best), peak_row)
     peaks[...] = peak_row
 
@@ -238,7 +238,7 @@
     return [pl.BlockSpec(memory_space=pltpu.VMEM)] * n
 
 
-def early_call(place, volume, mid_near, mid_wrap, weights, interpret=False):
+def early_call(odd, volume, mid_near, mid_wrap, weights, interpret=False):
     return pl.pallas_call(
         early_kernel,
         out_shape=[jax.ShapeDtypeStruct((tile_x * pitch, depth), jnp.float32)] * 4,
@@ -246,17 +246,17 @@
         out_specs=vmem(4),
         compiler_params=pltpu.CompilerParams(vmem_limit_bytes=16 * mib),
         interpret=interpret,
-    )(place, volume, *weights, mid_near, mid_wrap)
-
-
-def late_call(place, weights, pieces, early, interpret=False):
+    )(odd, volume, *weights, mid_near, mid_wrap)
+
+
+def late_call(core, odd, weights, pieces, early, interpret=False):
     return pl.pallas_call(
         late_kernel,
         out_shape=(
             jax.ShapeDtypeStruct((12, rows, depth), jnp.float32),
             jax.ShapeDtypeStruct((1, depth), jnp.float32),
         ),
-        in_specs=[pl.BlockSpec(memory_space=pltpu.SMEM)] + vmem(13),
+        in_specs=[pl.BlockSpec(memory_space=pltpu.SMEM)] * 2 + vmem(13),
         out_specs=tuple(vmem(2)),
         scratch_shapes=[
             pltpu.VMEM(((count - tile_x) * pitch, depth), jnp.float32) for count in planes
@@ -264,7 +264,7 @@
         + [pltpu.VMEM((6, rows, 2 * depth), jnp.bfloat16)],
         compiler_params=pltpu.CompilerParams(vmem_limit_bytes=24 * mib),
         interpret=interpret,
-    )(place, *weights, *pieces, *early)
+    )(core, odd, *weights, *pieces, *early)
 
 
 def score_call(stats, peaks, interpret=False):
@@ -296,8 +296,10 @@
     wrap_perm += [(j, i) for i, j in wrap_perm]
 
     odd = lax.axis_index("y") & 1
-    place = jnp.stack([lax.axis_index("core"), odd]).astype(jnp.int32)
-    volume, place, is_odd, is_even = lax.optimization_barrier((volume, place, odd == 1, odd == 0))
+    core = lax.axis_index("core")
+    volume, core, odd, is_odd, is_even = lax.optimization_barrier(
+        (volume, core.reshape(1), odd.reshape(1), odd == 1, odd == 0)
+    )
 
     def edge(tile, top):
         return jnp.where(top, tile[:, tile_y - rim :], tile[:, :rim])
@@ -311,12 +313,11 @@
     far_wrap = lax.ppermute(far_wrap, y_axes, wrap_perm)
     far_near = lax.ppermute(far_near, y_axes, near_perm)
     weights = [jnp.asarray(w) for w in constants()]
-    early = early_call(place, volume, mid_near, mid_wrap, weights)
-    mid_near, mid_wrap, *early = lax.optimization_barrier((mid_near, mid_wrap, *early))
+    early = early_call(odd, volume, mid_near, mid_wrap, weights)
     pair_near = lax.ppermute(mid_near, x_axes, pair_perm)
     pair_wrap = lax.ppermute(mid_wrap, x_axes, pair_perm)
     pieces = (far, far_near, far_wrap, pair, pair_near, pair_wrap)
-    stats, peaks = late_call(place, weights, pieces, early)
+    stats, peaks = late_call(core, odd, weights, pieces, early)
     return score_call(stats, all_peaks(peaks))
 
 

time: 70.9 us -> 68 us (0.959)
  Pallas kernels: 14.7 us -> 11.4 us
    pallas_call x1, Pallas kernels: 10.6 us -> 7.81 us  [late_call(): pl.pallas_call(late_kernel, out_shape=(jax.ShapeDtypeStruct((12, rows, de...]
  transfers between devices with their start and end apart: 8 -> 8, of which waited for: 4 -> 2; matrix products, arithmetic and copies ran while one was open for 2% -> 2% of each run, Pallas kernels for 2% -> 2%
where the time goes in v5:
time: 68 us; the launch traced here: 67.8 us
  blocking collectives  32.4 us (48%)
  starting transfers between devices  13.7 us (20%)
  Pallas kernels  11.4 us (17%)
  waiting for transfers between devices  8.11 us (12%)
  other arithmetic  1.14 us (2%)
  local copies, waits for them, and re-layouts  1.01 us (1%)
    all_to_all x1, blocking collectives, all_peaks(): return lax.all_to_all(spread, axes, 0, 0, tiled=True).reshape(peers, depth)  32.4 us
    pallas_call x1, Pallas kernels, late_call(): pl.pallas_call(late_kernel, out_shape=(jax.ShapeDtypeStruct((12, rows, de...  7.81 us
    ppermute x1, waiting for transfers between devices, per_device(): far = lax.ppermute(volume, x_axes, far_perm)  6.6 us
    ppermute x1, starting transfers between devices, per_device(): far = lax.ppermute(volume, x_axes, far_perm)  6.42 us
    ppermute x1, starting transfers between devices, per_device(): far_near = lax.ppermute(far_near, y_axes, near_perm)  3.91 us
    pallas_call x1, Pallas kernels, score_call(): pl.pallas_call(score_kernel, out_shape=jax.ShapeDtypeStruct((tile_x, tile...  2.4 us
    ppermute x1, waiting for transfers between devices, per_device(): far_near = lax.ppermute(far_near, y_axes, near_perm)  1.49 us
    ppermute x1, starting transfers between devices, per_device(): mid_near = lax.ppermute(edge(volume, is_even), y_axes, near_perm)  1.38 us
  transfers between devices with their start and end apart: 8, of which 2 were waited for; matrix products, arithmetic and copies ran while one was open for 2% of the time, Pallas kernels for 2%

profile of v5, /device:TPU:1, one launch (start us, length us, event | category | flops | bytes accessed | tf_op | source)
XLA Modules:
  0.0 67.8 jit_solution(4990839853274452730)
XLA Ops:
  0.0 0.0 copy-start
  0.0 0.0 copy-start.2
  0.0 0.0 copy-start.1
  0.0 6.4 %collective-permute-start = (f32[24,32,128]{2,1,0:T(8,128)}, f32[24,32,128]{2,1,0:T(8,128)S(1)}, u32[]{:S(2)}, u32[]{:S(2)}) collective-permute-start(f32[24,32,128]{2,1,0:T(8,128)} %mid), channel_id=1, source_target_pairs={{32,64},{96,128},{160,192},{64,32},{128,96},{192,160},{33,65},{97,... | collective-permute-start | bytes 1179656 | tf_op jit(solution)/shard_map/ppermute | solution.py:307
  6.4 1.1 %slice_select_fusion.2 = (f32[24,24,128]{2,1,0:T(8,128)S(1)}, f32[24,24,128]{2,1,0:T(8,128)S(1)}) fusion(f32[24,32,128]{2,1,0:T(8,128)} %mid, pred[]{:T(512)S(6)} %eq.7, pred[]{:T(512)S(6)} %eq.6), kind=kLoop, calls=%fused_computation.2 | loop fusion | flops 147456 | bytes 1179650 | tf_op jit(solution)/shard_map/jit(_where)/select_n | solution.py:305
  7.6 1.4 %collective-permute-start.5 = (f32[24,24,128]{2,1,0:T(8,128)S(1)}, f32[24,24,128]{2,1,0:T(8,128)S(1)}, u32[]{:S(2)}, u32[]{:S(2)}) collective-permute-start(f32[24,24,128]{2,1,0:T(8,128)S(1)} %get-tuple-element.31), channel_id=1, source_target_pairs={{0,1},{1,0},{2,3},{3,2},{4,5},{5,4},{6,7},{7,6},{8,9},{9,8},{10,11... | collective-permute-start | bytes 884744 | tf_op jit(solution)/shard_map/ppermute | solution.py:309
  8.9 0.7 collective-permute-start.4
  9.6 0.1 collective-permute-start.3
  9.7 6.6 %collective-permute-done.far = f32[24,32,128]{2,1,0:T(8,128)S(1)} collective-permute-done((f32[24,32,128]{2,1,0:T(8,128)}, f32[24,32,128]{2,1,0:T(8,128)S(1)}, u32[]{:S(2)}, u32[]{:S(2)}) %collective-permute-start) | collective-permute-done | bytes 393248 | tf_op jit(solution)/shard_map/ppermute | solution.py:307
  16.4 0.7 %collective-permute-start.2 = (f32[24,24,128]{2,1,0:T(8,128)S(1)}, f32[24,24,128]{2,1,0:T(8,128)S(1)}, u32[]{:S(2)}, u32[]{:S(2)}) collective-permute-start(f32[24,24,128]{2,1,0:T(8,128)S(1)} %get-tuple-element.33), channel_id=1, source_target_pairs={{1,2},{3,4},{5,6},{7,8},{9,10},{11,12},{13,14},{15,16},{17,18},{19... | collective-permute-start | bytes 884744 | tf_op jit(solution)/shard_map/ppermute | solution.py:313
  17.1 3.9 %collective-permute-start.1 = (f32[24,24,128]{2,1,0:T(8,128)S(1)}, f32[24,24,128]{2,1,0:T(8,128)S(1)}, u32[]{:S(2)}, u32[]{:S(2)}) collective-permute-start(f32[24,24,128]{2,1,0:T(8,128)S(1)} %get-tuple-element.34), channel_id=1, source_target_pairs={{0,1},{1,0},{2,3},{3,2},{4,5},{5,4},{6,7},{7,6},{8,9},{9,8},{10,11... | collective-permute-start | bytes 884744 | tf_op jit(solution)/shard_map/ppermute | solution.py:314
  21.0 0.0 collective-permute-done.5.mid_near
  21.0 0.0 collective-permute-done.4.mid_wrap
  21.0 0.0 collective-permute-start.6
  21.0 0.5 collective-permute-start.7
  21.5 0.0 copy-done
  21.5 0.0 copy-done.2
  21.5 0.0 copy-done.1
  21.5 0.0 copy-start.3
  21.5 0.9 %copy-done.3 = bf16[384,256]{1,0:T(8,128)(2,1)S(1)} copy-done((bf16[384,256]{1,0:T(8,128)(2,1)S(1)}, bf16[384,256]{1,0:T(8,128)(2,1)}, u32[]{:S(2)}) %copy-start.3) | copy-done | bytes 196632
  22.4 0.0 copy-start.4
  22.4 1.1 %shard_map.46 = (f32[2496,128]{1,0:T(8,128)S(1)}, f32[2496,128]{1,0:T(8,128)S(1)}, f32[2496,128]{1,0:T(8,128)S(1)}, f32[2496,128]{1,0:T(8,128)S(1)}) custom-call(s32[1]{0:T(128)} %bitcast.1.odd_ref, f32[24,32,128]{2,1,0:T(8,128)S(1)} %copy-done.1, bf16[384,256]{1,0:T(8,128)(2,1)S(1)} %copy-done.3, bf16[2,4,72,256]{3,2,1,0:T(8,128)(2,1)S(1)} %copy-done.2, ...), custom_call_target="tpu_custom_call" | custom-call | tf_op jit(solution)/shard_map/pallas_call | solution.py:242
  23.6 0.0 collective-permute-done.3.pair
  23.6 0.0 collective-permute-done.2.far_wrap
  23.6 1.5 %collective-permute-done.1.far_near = f32[24,24,128]{2,1,0:T(8,128)S(1)} collective-permute-done((f32[24,24,128]{2,1,0:T(8,128)S(1)}, f32[24,24,128]{2,1,0:T(8,128)S(1)}, u32[]{:S(2)}, u32[]{:S(2)}) %collective-permute-start.1) | collective-permute-done | bytes 294944 | tf_op jit(solution)/shard_map/ppermute | solution.py:314
  25.1 0.0 collective-permute-done.6.pair_near
  25.1 0.0 collective-permute-done.7.pair_wrap
  25.1 0.0 copy-done.4
  25.1 7.8 %shard_map.47 = (f32[12,768,128]{2,1,0:T(8,128)S(1)}, f32[1,128]{1,0:T(1,128)S(1)}) custom-call(s32[1]{0:T(128)} %bitcast.core_ref, s32[1]{0:T(128)} %bitcast.1.odd_ref, bf16[384,256]{1,0:T(8,128)(2,1)S(1)} %copy-done.4, bf16[2,4,72,256]{3,2,1,0:T(8,128)(2,1)S(1)} %copy-done.2, bf16[12,256,256]{2,1,0:T(8,128)(2,1)S(1)} %copy-done, ...), custom_call_target="tpu_custom_call" | custom-call | tf_op jit(solution)/shard_map/pallas_call | solution.py:253
  32.9 0.1 broadcast_in_dim.9
  33.0 32.4 %all_to_all.5 = f32[256,1,128]{2,1,0:T(1,128)S(1)} all-to-all(f32[256,1,128]{2,1,0:T(1,128)S(1)} %broadcast_in_dim.9), channel_id=1, replica_groups=mesh['zh'=4,'core'=2,'x'=4,'zl'=2,'y'=4] {'zh','core','x','zl','y'}, dimensions={0} | all-to-all | bytes 262144 | tf_op jit(solution)/shard_map/all_to_all | solution.py:286
  65.4 2.4 %shard_map.48 = f32[24,32,128]{2,1,0:T(8,128)} custom-call(f32[12,768,128]{2,1,0:T(8,128)S(1)} %get-tuple-element.29.stats, f32[256,128]{1,0:T(8,128)S(1)} %bitcast.4), custom_call_target="tpu_custom_call" | custom-call | tf_op jit(solution)/shard_map/pallas_call | solution.py:271
  (1 shorter events, 0.0 us)
Async XLA Ops:
  0.0 21.5 %copy-start = (bf16[12,256,256]{2,1,0:T(8,128)(2,1)S(1)}, bf16[12,256,256]{2,1,0:T(8,128)(2,1)}, u32[]{:S(2)}) copy-start(bf16[12,256,256]{2,1,0:T(8,128)(2,1)} %constant.22.clone.wz) | copy-start | bytes 4718596
  0.0 21.5 %copy-start.2 = (bf16[2,4,72,256]{3,2,1,0:T(8,128)(2,1)S(1)}, bf16[2,4,72,256]{3,2,1,0:T(8,128)(2,1)}, u32[]{:S(2)}) copy-start(bf16[2,4,72,256]{3,2,1,0:T(8,128)(2,1)} %constant.21.clone.wx) | copy-start | bytes 884740
  0.0 21.5 %copy-start.1 = (f32[24,32,128]{2,1,0:T(8,128)S(1)}, f32[24,32,128]{2,1,0:T(8,128)}, u32[]{:S(2)}) copy-start(f32[24,32,128]{2,1,0:T(8,128)} %mid) | copy-start | bytes 1179652
  0.0 16.3 %collective-permute-start = (f32[24,32,128]{2,1,0:T(8,128)}, f32[24,32,128]{2,1,0:T(8,128)S(1)}, u32[]{:S(2)}, u32[]{:S(2)}) collective-permute-start(f32[24,32,128]{2,1,0:T(8,128)} %mid), channel_id=1, source_target_pairs={{32,64},{96,128},{160,192},{64,32},{128,96},{192,160},{33,65},{97,... | collective-permute-start | bytes 1179656 | tf_op jit(solution)/shard_map/ppermute | solution.py:307
  7.6 13.4 %collective-permute-start.5 = (f32[24,24,128]{2,1,0:T(8,128)S(1)}, f32[24,24,128]{2,1,0:T(8,128)S(1)}, u32[]{:S(2)}, u32[]{:S(2)}) collective-permute-start(f32[24,24,128]{2,1,0:T(8,128)S(1)} %get-tuple-element.31), channel_id=1, source_target_pairs={{0,1},{1,0},{2,3},{3,2},{4,5},{5,4},{6,7},{7,6},{8,9},{9,8},{10,11... | collective-permute-start | bytes 884744 | tf_op jit(solution)/shard_map/ppermute | solution.py:309
  8.9 12.0 %collective-permute-start.4 = (f32[24,24,128]{2,1,0:T(8,128)S(1)}, f32[24,24,128]{2,1,0:T(8,128)S(1)}, u32[]{:S(2)}, u32[]{:S(2)}) collective-permute-start(f32[24,24,128]{2,1,0:T(8,128)S(1)} %get-tuple-element.32), channel_id=1, source_target_pairs={{1,2},{3,4},{5,6},{7,8},{9,10},{11,12},{13,14},{15,16},{17,18},{19... | collective-permute-start | bytes 884744 | tf_op jit(solution)/shard_map/ppermute | solution.py:308
  9.6 13.9 %collective-permute-start.3 = (f32[24,32,128]{2,1,0:T(8,128)}, f32[24,32,128]{2,1,0:T(8,128)S(1)}, u32[]{:S(2)}, u32[]{:S(2)}) collective-permute-start(f32[24,32,128]{2,1,0:T(8,128)} %mid), channel_id=1, source_target_pairs={{0,32},{32,0},{64,96},{96,64},{128,160},{160,128},{192,224},{224,1... | collective-permute-start | bytes 1179656 | tf_op jit(solution)/shard_map/ppermute | solution.py:310
  16.4 7.2 %collective-permute-start.2 = (f32[24,24,128]{2,1,0:T(8,128)S(1)}, f32[24,24,128]{2,1,0:T(8,128)S(1)}, u32[]{:S(2)}, u32[]{:S(2)}) collective-permute-start(f32[24,24,128]{2,1,0:T(8,128)S(1)} %get-tuple-element.33), channel_id=1, source_target_pairs={{1,2},{3,4},{5,6},{7,8},{9,10},{11,12},{13,14},{15,16},{17,18},{19... | collective-permute-start | bytes 884744 | tf_op jit(solution)/shard_map/ppermute | solution.py:313
  17.1 8.0 %collective-permute-start.1 = (f32[24,24,128]{2,1,0:T(8,128)S(1)}, f32[24,24,128]{2,1,0:T(8,128)S(1)}, u32[]{:S(2)}, u32[]{:S(2)}) collective-permute-start(f32[24,24,128]{2,1,0:T(8,128)S(1)} %get-tuple-element.34), channel_id=1, source_target_pairs={{0,1},{1,0},{2,3},{3,2},{4,5},{5,4},{6,7},{7,6},{8,9},{9,8},{10,11... | collective-permute-start | bytes 884744 | tf_op jit(solution)/shard_map/ppermute | solution.py:314
  21.0 4.1 %collective-permute-start.6 = (f32[24,24,128]{2,1,0:T(8,128)S(1)}, f32[24,24,128]{2,1,0:T(8,128)S(1)}, u32[]{:S(2)}, u32[]{:S(2)}) collective-permute-start(f32[24,24,128]{2,1,0:T(8,128)S(1)} %collective-permute-done.5.mid_near), channel_id=1, source_target_pairs={{0,32},{32,0},{64,96},{96,64},{128,160},{160,128},{192,224},{224,1... | collective-permute-start | bytes 884744 | tf_op jit(solution)/shard_map/ppermute | solution.py:317
  21.0 4.1 %collective-permute-start.7 = (f32[24,24,128]{2,1,0:T(8,128)S(1)}, f32[24,24,128]{2,1,0:T(8,128)S(1)}, u32[]{:S(2)}, u32[]{:S(2)}) collective-permute-start(f32[24,24,128]{2,1,0:T(8,128)S(1)} %collective-permute-done.4.mid_wrap), channel_id=1, source_target_pairs={{0,32},{32,0},{64,96},{96,64},{128,160},{160,128},{192,224},{224,1... | collective-permute-start | bytes 884744 | tf_op jit(solution)/shard_map/ppermute | solution.py:318
  21.5 0.9 %copy-start.3 = (bf16[384,256]{1,0:T(8,128)(2,1)S(1)}, bf16[384,256]{1,0:T(8,128)(2,1)}, u32[]{:S(2)}) copy-start(bf16[384,256]{1,0:T(8,128)(2,1)} %constant.20.clone.wy) | copy-start | bytes 589828
  22.4 2.7 %copy-start.4 = (bf16[384,256]{1,0:T(8,128)(2,1)S(1)}, bf16[384,256]{1,0:T(8,128)(2,1)}, u32[]{:S(2)}) copy-start(bf16[384,256]{1,0:T(8,128)(2,1)} %constant.20.clone.wy) | copy-start | bytes 589828

commit v6 on v5

--- a/solution.py
+++ b/solution.py
@@ -100,7 +100,7 @@
 
 
 def side_steps(fields, wy, parts, before, base):
-    for start, stop, levels in ((0, 2, 4), (2, 6, 3), (6, 10, 1), (10, 12, 1)):
+    for start, stop, levels in ((0, 2, 4), (2, 6, 3), (6, 12, 1)):
 
         def body(j, carry, levels=levels):
             plane = 2 * (j + before * (11 - 2 * j))
@@ -108,7 +108,7 @@
             y_step(fields, wy, parts(plane), slots)
             return carry
 
-        lax.fori_loop(start, stop, body, 0, unroll=min(4, stop - start))
+        lax.fori_loop(start, stop, body, 0, unroll=stop - start)
 
 
 def by_parity(odd_ref, step, near_rim, wrap_rim):
@@ -126,7 +126,7 @@
             y_step((g8, g4, g2, g1), wy, [low[at], mid[at], high[at]], [2 * i] * 4)
             return carry
 
-        lax.fori_loop(0, tile_x // 2, body, 0, unroll=4)
+        lax.fori_loop(0, tile_x // 2, body, 0, unroll=12)
 
     by_parity(odd_ref, step, mid_near, mid_wrap)
 
@@ -152,57 +152,61 @@
     by_parity(odd_ref, side(pair, core, [0] * 4), pair_near, pair_wrap)
     by_parity(odd_ref, side(far, 1 - core, near), far_near, far_wrap)
 
+    def x_step(level, yp):
+        own, field, count = own_fields[level], fields[level], planes[level]
+        at = pl.ds(48 * yp, 48)
+        for f, first, outs in ((0, 0, 3), (1, 3, 2), (2, 5, 1)):
+            pieces = [
+                [
+                    own[pl.ds(32 * f + 2 * yp + k, tile_x, stride=pitch), :],
+                    field[pl.ds(32 * f + 2 * yp + k, count - tile_x, stride=pitch), :],
+                ]
+                for k in range(2)
+            ]
+            pieces = [jnp.concatenate(piece, axis=0) for piece in pieces]
+            hi, lo = halves(jnp.concatenate(pieces, axis=1))
+            data = jnp.concatenate([hi, lo, hi], axis=0)
+            out = dot(wx[core, level, 0 : 24 * outs, 0 : 3 * count], data)
+            for k in range(outs):
+                u = out[24 * k : 24 * k + 24]
+                u = jnp.concatenate([u[:, :depth], u[:, depth:]], axis=0)
+                hi, lo = halves(u)
+                mixed[level, first + k, at, 0:depth] = hi
+                mixed[level, first + k, at, depth : 2 * depth] = lo
+
+    def z_step(level, c, best):
+        at = pl.ds(c * z_rows, z_rows)
+
+        def z_pass(order, chosen):
+            data = jnp.concatenate([mixed[level, p, at, :] for p in chosen], axis=0)
+            out = dot(data, wz[3 * level + order])
+            out = out[:, :depth] + out[:, depth:]
+            return [out[z_rows * k : z_rows * (k + 1)] for k in range(len(chosen))]
+
+        (zz,) = z_pass(2, (0,))
+        yz, xz = z_pass(1, (3, 1))
+        yy, xy, xx = z_pass(0, (5, 4, 2))
+        sq = xy * xy + xz * xz + yz * yz
+        stats[3 * level, at, :] = xx + yy + zz
+        stats[3 * level + 1, at, :] = xx * yy + (xx + yy) * zz - sq
+        energy = xx * xx + yy * yy + zz * zz + 2.0 * sq
+        stats[3 * level + 2, at, :] = energy
+        return jnp.maximum(best, jnp.max(energy.reshape(z_rows // 8, 8, depth), axis=0))
+
     lane = lax.broadcasted_iota(jnp.int32, (1, depth), 1)
     peak_row = jnp.zeros((1, depth), jnp.float32)
-    for level in range(4):
-        own, field = own_fields[level], fields[level]
-        count = planes[level]
-
-        def x_body(yp, carry, own=own, field=field, level=level, count=count):
-            at = pl.ds(pl.multiple_of(48 * yp, 48), 48)
-            for f, first, outs in ((0, 0, 3), (1, 3, 2), (2, 5, 1)):
-                pieces = [
-                    [
-                        own[pl.ds(32 * f + 2 * yp + k, tile_x, stride=pitch), :],
-                        field[pl.ds(32 * f + 2 * yp + k, count - tile_x, stride=pitch), :],
-                    ]
-                    for k in range(2)
-                ]
-                pieces = [jnp.concatenate(piece, axis=0) for piece in pieces]
-                hi, lo = halves(jnp.concatenate(pieces, axis=1))
-                data = jnp.concatenate([hi, lo, hi], axis=0)
-                out = dot(wx[core, level, 0 : 24 * outs, 0 : 3 * count], data)
-                for k in range(outs):
-                    u = out[24 * k : 24 * k + 24]
-                    u = jnp.concatenate([u[:, :depth], u[:, depth:]], axis=0)
-                    hi, lo = halves(u)
-                    mixed[first + k, at, 0:depth] = hi
-                    mixed[first + k, at, depth : 2 * depth] = lo
-            return carry
-
-        lax.fori_loop(0, tile_y // 2, x_body, 0, unroll=16)
-
-        def z_body(c, best, level=level):
-            at = pl.ds(pl.multiple_of(c * z_rows, z_rows), z_rows)
-
-            def z_pass(order, chosen):
-                data = jnp.concatenate([mixed[p, at, :] for p in chosen], axis=0)
-                out = dot(data, wz[3 * level + order])
-                out = out[:, :depth] + out[:, depth:]
-                return [out[z_rows * k : z_rows * (k + 1)] for k in range(len(chosen))]
-
-            (zz,) = z_pass(2, (0,))
-            yz, xz = z_pass(1, (3, 1))
-            yy, xy, xx = z_pass(0, (5, 4, 2))
-            sq = xy * xy + xz * xz + yz * yz
-            stats[3 * level, at, :] = xx + yy + zz
-            stats[3 * level + 1, at, :] = xx * yy + (xx + yy) * zz - sq
-            energy = xx * xx + yy * yy + zz * zz + 2.0 * sq
-            stats[3 * level + 2, at, :] = energy
-            return jnp.maximum(best, jnp.max(energy.reshape(z_rows // 8, 8, depth), axis=0))
-
-        best = lax.fori_loop(0, rows // z_rows, z_body, jnp.zeros((8, depth), jnp.float32), unroll=4)
-        peak_row = jnp.where(lane == level, jnp.max(best), peak_row)
+    blocks = rows // z_rows
+    steps = tile_y // 2 // blocks
+    for level in range(5):
+        best = jnp.zeros((8, depth), jnp.float32)
+        for c in range(blocks):
+            if level < 4:
+                for yp in range(steps * c, steps * (c + 1)):
+                    x_step(level, yp)
+            if level > 0:
+                best = z_step(level - 1, c, best)
+        if level > 0:
+            peak_row = jnp.where(lane == level - 1, jnp.max(best), peak_row)
     peaks[...] = peak_row
 
 
@@ -229,7 +233,7 @@
         flat[at, :] = 0.5 * best
         return carry
 
-    lax.fori_loop(0, rows // 24, body, 0, unroll=4)
+    lax.fori_loop(0, rows // 24, body, 0, unroll=32)
     for i in range(tile_x):
         throat[i] = flat[pl.ds(i, tile_y, stride=tile_x), :]
 
@@ -261,8 +265,8 @@
         scratch_shapes=[
             pltpu.VMEM(((count - tile_x) * pitch, depth), jnp.float32) for count in planes
         ]
-        + [pltpu.VMEM((6, rows, 2 * depth), jnp.bfloat16)],
-        compiler_params=pltpu.CompilerParams(vmem_limit_bytes=24 * mib),
+        + [pltpu.VMEM((4, 6, rows, 2 * depth), jnp.bfloat16)],
+        compiler_params=pltpu.CompilerParams(vmem_limit_bytes=28 * mib),
         interpret=interpret,
     )(core, odd, *weights, *pieces, *early)
 

time: 68 us -> 67.2 us (0.988)
  Pallas kernels: 11.4 us -> 10.2 us
  transfers between devices with their start and end apart: 8 -> 8, of which waited for: 2 -> 2; matrix products, arithmetic and copies ran while one was open for 2% -> 2% of each run, Pallas kernels for 2% -> 1%
where the time goes in v6:
time: 67.2 us; the launch traced here: 67 us
  blocking collectives  32.4 us (48%)
  starting transfers between devices  13.7 us (20%)
  Pallas kernels  10.2 us (15%)
  waiting for transfers between devices  8.46 us (13%)
  other arithmetic  1.14 us (2%)
  local copies, waits for them, and re-layouts  1.01 us (2%)
    all_to_all x1, blocking collectives, all_peaks(): return lax.all_to_all(spread, axes, 0, 0, tiled=True).reshape(peers, depth)  32.4 us
    pallas_call x1, Pallas kernels, late_call(): pl.pallas_call(late_kernel, out_shape=(jax.ShapeDtypeStruct((12, rows, de...  7.61 us
    ppermute x1, waiting for transfers between devices, per_device(): far = lax.ppermute(volume, x_axes, far_perm)  6.6 us
    ppermute x1, starting transfers between devices, per_device(): far = lax.ppermute(volume, x_axes, far_perm)  6.42 us
    ppermute x1, starting transfers between devices, per_device(): far_near = lax.ppermute(far_near, y_axes, near_perm)  3.91 us
    ppermute x1, waiting for transfers between devices, per_device(): far_near = lax.ppermute(far_near, y_axes, near_perm)  1.84 us
    pallas_call x1, Pallas kernels, score_call(): pl.pallas_call(score_kernel, out_shape=jax.ShapeDtypeStruct((tile_x, tile...  1.78 us
    ppermute x1, starting transfers between devices, per_device(): mid_near = lax.ppermute(edge(volume, is_even), y_axes, near_perm)  1.38 us
  transfers between devices with their start and end apart: 8, of which 2 were waited for; matrix products, arithmetic and copies ran while one was open for 2% of the time, Pallas kernels for 1%

profile of v6, /device:TPU:1, one launch (start us, length us, event | category | flops | bytes accessed | tf_op | source)
XLA Modules:
  0.0 67.0 jit_solution(10388568504744232573)
XLA Ops:
  0.0 0.0 copy-start
  0.0 0.0 copy-start.2
  0.0 0.0 copy-start.1
  0.0 6.4 %collective-permute-start = (f32[24,32,128]{2,1,0:T(8,128)}, f32[24,32,128]{2,1,0:T(8,128)S(1)}, u32[]{:S(2)}, u32[]{:S(2)}) collective-permute-start(f32[24,32,128]{2,1,0:T(8,128)} %mid), channel_id=1, source_target_pairs={{32,64},{96,128},{160,192},{64,32},{128,96},{192,160},{33,65},{97,... | collective-permute-start | bytes 1179656 | tf_op jit(solution)/shard_map/ppermute | solution.py:311
  6.4 1.1 %slice_select_fusion.2 = (f32[24,24,128]{2,1,0:T(8,128)S(1)}, f32[24,24,128]{2,1,0:T(8,128)S(1)}) fusion(f32[24,32,128]{2,1,0:T(8,128)} %mid, pred[]{:T(512)S(6)} %eq.7, pred[]{:T(512)S(6)} %eq.6), kind=kLoop, calls=%fused_computation.2 | loop fusion | flops 147456 | bytes 1179650 | tf_op jit(solution)/shard_map/jit(_where)/select_n | solution.py:309
  7.6 1.4 %collective-permute-start.5 = (f32[24,24,128]{2,1,0:T(8,128)S(1)}, f32[24,24,128]{2,1,0:T(8,128)S(1)}, u32[]{:S(2)}, u32[]{:S(2)}) collective-permute-start(f32[24,24,128]{2,1,0:T(8,128)S(1)} %get-tuple-element.31), channel_id=1, source_target_pairs={{0,1},{1,0},{2,3},{3,2},{4,5},{5,4},{6,7},{7,6},{8,9},{9,8},{10,11... | collective-permute-start | bytes 884744 | tf_op jit(solution)/shard_map/ppermute | solution.py:313
  8.9 0.7 collective-permute-start.4
  9.6 0.1 collective-permute-start.3
  9.7 6.6 %collective-permute-done.far = f32[24,32,128]{2,1,0:T(8,128)S(1)} collective-permute-done((f32[24,32,128]{2,1,0:T(8,128)}, f32[24,32,128]{2,1,0:T(8,128)S(1)}, u32[]{:S(2)}, u32[]{:S(2)}) %collective-permute-start) | collective-permute-done | bytes 393248 | tf_op jit(solution)/shard_map/ppermute | solution.py:311
  16.4 0.7 %collective-permute-start.2 = (f32[24,24,128]{2,1,0:T(8,128)S(1)}, f32[24,24,128]{2,1,0:T(8,128)S(1)}, u32[]{:S(2)}, u32[]{:S(2)}) collective-permute-start(f32[24,24,128]{2,1,0:T(8,128)S(1)} %get-tuple-element.33), channel_id=1, source_target_pairs={{1,2},{3,4},{5,6},{7,8},{9,10},{11,12},{13,14},{15,16},{17,18},{19... | collective-permute-start | bytes 884744 | tf_op jit(solution)/shard_map/ppermute | solution.py:317
  17.1 3.9 %collective-permute-start.1 = (f32[24,24,128]{2,1,0:T(8,128)S(1)}, f32[24,24,128]{2,1,0:T(8,128)S(1)}, u32[]{:S(2)}, u32[]{:S(2)}) collective-permute-start(f32[24,24,128]{2,1,0:T(8,128)S(1)} %get-tuple-element.34), channel_id=1, source_target_pairs={{0,1},{1,0},{2,3},{3,2},{4,5},{5,4},{6,7},{7,6},{8,9},{9,8},{10,11... | collective-permute-start | bytes 884744 | tf_op jit(solution)/shard_map/ppermute | solution.py:318
  21.0 0.0 collective-permute-done.5.mid_near
  21.0 0.0 collective-permute-done.4.mid_wrap
  21.0 0.0 collective-permute-start.6
  21.0 0.5 collective-permute-start.7
  21.5 0.0 copy-done
  21.5 0.0 copy-done.2
  21.5 0.0 copy-done.1
  21.5 0.0 copy-start.3
  21.5 0.9 %copy-done.3 = bf16[384,256]{1,0:T(8,128)(2,1)S(1)} copy-done((bf16[384,256]{1,0:T(8,128)(2,1)S(1)}, bf16[384,256]{1,0:T(8,128)(2,1)}, u32[]{:S(2)}) %copy-start.3) | copy-done | bytes 196632
  22.4 0.0 copy-start.4
  22.4 0.8 %shard_map.46 = (f32[2496,128]{1,0:T(8,128)S(1)}, f32[2496,128]{1,0:T(8,128)S(1)}, f32[2496,128]{1,0:T(8,128)S(1)}, f32[2496,128]{1,0:T(8,128)S(1)}) custom-call(s32[1]{0:T(128)} %bitcast.1.odd_ref, f32[24,32,128]{2,1,0:T(8,128)S(1)} %copy-done.1, bf16[384,256]{1,0:T(8,128)(2,1)S(1)} %copy-done.3, bf16[2,4,72,256]{3,2,1,0:T(8,128)(2,1)S(1)} %copy-done.2, ...), custom_call_target="tpu_custom_call" | custom-call | tf_op jit(solution)/shard_map/pallas_call | solution.py:246
  23.2 0.0 collective-permute-done.3.pair
  23.2 0.0 collective-permute-done.2.far_wrap
  23.2 1.8 %collective-permute-done.1.far_near = f32[24,24,128]{2,1,0:T(8,128)S(1)} collective-permute-done((f32[24,24,128]{2,1,0:T(8,128)S(1)}, f32[24,24,128]{2,1,0:T(8,128)S(1)}, u32[]{:S(2)}, u32[]{:S(2)}) %collective-permute-start.1) | collective-permute-done | bytes 294944 | tf_op jit(solution)/shard_map/ppermute | solution.py:318
  25.1 0.0 collective-permute-done.6.pair_near
  25.1 0.0 collective-permute-done.7.pair_wrap
  25.1 0.0 copy-done.4
  25.1 7.6 %shard_map.47 = (f32[12,768,128]{2,1,0:T(8,128)S(1)}, f32[1,128]{1,0:T(1,128)S(1)}) custom-call(s32[1]{0:T(128)} %bitcast.core_ref, s32[1]{0:T(128)} %bitcast.1.odd_ref, bf16[384,256]{1,0:T(8,128)(2,1)S(1)} %copy-done.4, bf16[2,4,72,256]{3,2,1,0:T(8,128)(2,1)S(1)} %copy-done.2, bf16[12,256,256]{2,1,0:T(8,128)(2,1)S(1)} %copy-done, ...), custom_call_target="tpu_custom_call" | custom-call | tf_op jit(solution)/shard_map/pallas_call | solution.py:257
  32.7 0.1 broadcast_in_dim.9
  32.8 32.4 %all_to_all.5 = f32[256,1,128]{2,1,0:T(1,128)S(1)} all-to-all(f32[256,1,128]{2,1,0:T(1,128)S(1)} %broadcast_in_dim.9), channel_id=1, replica_groups=mesh['zh'=4,'core'=2,'x'=4,'zl'=2,'y'=4] {'zh','core','x','zl','y'}, dimensions={0} | all-to-all | bytes 262144 | tf_op jit(solution)/shard_map/all_to_all | solution.py:290
  65.2 1.8 %shard_map.48 = f32[24,32,128]{2,1,0:T(8,128)} custom-call(f32[12,768,128]{2,1,0:T(8,128)S(1)} %get-tuple-element.29.stats, f32[256,128]{1,0:T(8,128)S(1)} %bitcast.4), custom_call_target="tpu_custom_call" | custom-call | tf_op jit(solution)/shard_map/pallas_call | solution.py:275
  (1 shorter events, 0.0 us)
Async XLA Ops:
  0.0 21.5 %copy-start = (bf16[12,256,256]{2,1,0:T(8,128)(2,1)S(1)}, bf16[12,256,256]{2,1,0:T(8,128)(2,1)}, u32[]{:S(2)}) copy-start(bf16[12,256,256]{2,1,0:T(8,128)(2,1)} %constant.22.clone.wz) | copy-start | bytes 4718596
  0.0 21.5 %copy-start.2 = (bf16[2,4,72,256]{3,2,1,0:T(8,128)(2,1)S(1)}, bf16[2,4,72,256]{3,2,1,0:T(8,128)(2,1)}, u32[]{:S(2)}) copy-start(bf16[2,4,72,256]{3,2,1,0:T(8,128)(2,1)} %constant.21.clone.wx) | copy-start | bytes 884740
  0.0 21.5 %copy-start.1 = (f32[24,32,128]{2,1,0:T(8,128)S(1)}, f32[24,32,128]{2,1,0:T(8,128)}, u32[]{:S(2)}) copy-start(f32[24,32,128]{2,1,0:T(8,128)} %mid) | copy-start | bytes 1179652
  0.0 16.3 %collective-permute-start = (f32[24,32,128]{2,1,0:T(8,128)}, f32[24,32,128]{2,1,0:T(8,128)S(1)}, u32[]{:S(2)}, u32[]{:S(2)}) collective-permute-start(f32[24,32,128]{2,1,0:T(8,128)} %mid), channel_id=1, source_target_pairs={{32,64},{96,128},{160,192},{64,32},{128,96},{192,160},{33,65},{97,... | collective-permute-start | bytes 1179656 | tf_op jit(solution)/shard_map/ppermute | solution.py:311
  7.6 13.4 %collective-permute-start.5 = (f32[24,24,128]{2,1,0:T(8,128)S(1)}, f32[24,24,128]{2,1,0:T(8,128)S(1)}, u32[]{:S(2)}, u32[]{:S(2)}) collective-permute-start(f32[24,24,128]{2,1,0:T(8,128)S(1)} %get-tuple-element.31), channel_id=1, source_target_pairs={{0,1},{1,0},{2,3},{3,2},{4,5},{5,4},{6,7},{7,6},{8,9},{9,8},{10,11... | collective-permute-start | bytes 884744 | tf_op jit(solution)/shard_map/ppermute | solution.py:313
  8.9 12.0 %collective-permute-start.4 = (f32[24,24,128]{2,1,0:T(8,128)S(1)}, f32[24,24,128]{2,1,0:T(8,128)S(1)}, u32[]{:S(2)}, u32[]{:S(2)}) collective-permute-start(f32[24,24,128]{2,1,0:T(8,128)S(1)} %get-tuple-element.32), channel_id=1, source_target_pairs={{1,2},{3,4},{5,6},{7,8},{9,10},{11,12},{13,14},{15,16},{17,18},{19... | collective-permute-start | bytes 884744 | tf_op jit(solution)/shard_map/ppermute | solution.py:312
  9.6 13.6 %collective-permute-start.3 = (f32[24,32,128]{2,1,0:T(8,128)}, f32[24,32,128]{2,1,0:T(8,128)S(1)}, u32[]{:S(2)}, u32[]{:S(2)}) collective-permute-start(f32[24,32,128]{2,1,0:T(8,128)} %mid), channel_id=1, source_target_pairs={{0,32},{32,0},{64,96},{96,64},{128,160},{160,128},{192,224},{224,1... | collective-permute-start | bytes 1179656 | tf_op jit(solution)/shard_map/ppermute | solution.py:314
  16.4 6.9 %collective-permute-start.2 = (f32[24,24,128]{2,1,0:T(8,128)S(1)}, f32[24,24,128]{2,1,0:T(8,128)S(1)}, u32[]{:S(2)}, u32[]{:S(2)}) collective-permute-start(f32[24,24,128]{2,1,0:T(8,128)S(1)} %get-tuple-element.33), channel_id=1, source_target_pairs={{1,2},{3,4},{5,6},{7,8},{9,10},{11,12},{13,14},{15,16},{17,18},{19... | collective-permute-start | bytes 884744 | tf_op jit(solution)/shard_map/ppermute | solution.py:317
  17.1 8.0 %collective-permute-start.1 = (f32[24,24,128]{2,1,0:T(8,128)S(1)}, f32[24,24,128]{2,1,0:T(8,128)S(1)}, u32[]{:S(2)}, u32[]{:S(2)}) collective-permute-start(f32[24,24,128]{2,1,0:T(8,128)S(1)} %get-tuple-element.34), channel_id=1, source_target_pairs={{0,1},{1,0},{2,3},{3,2},{4,5},{5,4},{6,7},{7,6},{8,9},{9,8},{10,11... | collective-permute-start | bytes 884744 | tf_op jit(solution)/shard_map/ppermute | solution.py:318
  21.0 4.1 %collective-permute-start.6 = (f32[24,24,128]{2,1,0:T(8,128)S(1)}, f32[24,24,128]{2,1,0:T(8,128)S(1)}, u32[]{:S(2)}, u32[]{:S(2)}) collective-permute-start(f32[24,24,128]{2,1,0:T(8,128)S(1)} %collective-permute-done.5.mid_near), channel_id=1, source_target_pairs={{0,32},{32,0},{64,96},{96,64},{128,160},{160,128},{192,224},{224,1... | collective-permute-start | bytes 884744 | tf_op jit(solution)/shard_map/ppermute | solution.py:321
  21.0 4.1 %collective-permute-start.7 = (f32[24,24,128]{2,1,0:T(8,128)S(1)}, f32[24,24,128]{2,1,0:T(8,128)S(1)}, u32[]{:S(2)}, u32[]{:S(2)}) collective-permute-start(f32[24,24,128]{2,1,0:T(8,128)S(1)} %collective-permute-done.4.mid_wrap), channel_id=1, source_target_pairs={{0,32},{32,0},{64,96},{96,64},{128,160},{160,128},{192,224},{224,1... | collective-permute-start | bytes 884744 | tf_op jit(solution)/shard_map/ppermute | solution.py:322
  21.5 0.9 %copy-start.3 = (bf16[384,256]{1,0:T(8,128)(2,1)S(1)}, bf16[384,256]{1,0:T(8,128)(2,1)}, u32[]{:S(2)}) copy-start(bf16[384,256]{1,0:T(8,128)(2,1)} %constant.20.clone.wy) | copy-start | bytes 589828
  22.4 2.7 %copy-start.4 = (bf16[384,256]{1,0:T(8,128)(2,1)S(1)}, bf16[384,256]{1,0:T(8,128)(2,1)}, u32[]{:S(2)}) copy-start(bf16[384,256]{1,0:T(8,128)(2,1)} %constant.20.clone.wy) | copy-start | bytes 589828

commit v7 on v6

--- a/solution.py
+++ b/solution.py
@@ -17,7 +17,7 @@
 near = (24, 12, 12, 4)
 planes = (80, 48, 48, 32)
 rows = tile_x * tile_y
-z_rows = 192
+z_rows = 96
 pitch = 104
 mib = 1024 * 1024
 log2_e = float(np.log2(np.e))

time: 67.2 us -> 67.4 us (level)
  no operation moved by 1% of the time
where the time goes in v7:
time: 67.4 us; the launch traced here: 67.2 us
  blocking collectives  32.4 us (48%)
  starting transfers between devices  13.7 us (20%)
  Pallas kernels  10.4 us (15%)
  waiting for transfers between devices  8.46 us (13%)
  other arithmetic  1.14 us (2%)
  local copies, waits for them, and re-layouts  1.01 us (1%)
    all_to_all x1, blocking collectives, all_peaks(): return lax.all_to_all(spread, axes, 0, 0, tiled=True).reshape(peers, depth)  32.4 us
    pallas_call x1, Pallas kernels, late_call(): pl.pallas_call(late_kernel, out_shape=(jax.ShapeDtypeStruct((12, rows, de...  7.82 us
    ppermute x1, waiting for transfers between devices, per_device(): far = lax.ppermute(volume, x_axes, far_perm)  6.6 us
    ppermute x1, starting transfers between devices, per_device(): far = lax.ppermute(volume, x_axes, far_perm)  6.42 us
    ppermute x1, starting transfers between devices, per_device(): far_near = lax.ppermute(far_near, y_axes, near_perm)  3.91 us
    ppermute x1, waiting for transfers between devices, per_device(): far_near = lax.ppermute(far_near, y_axes, near_perm)  1.84 us
    pallas_call x1, Pallas kernels, score_call(): pl.pallas_call(score_kernel, out_shape=jax.ShapeDtypeStruct((tile_x, tile...  1.78 us
    ppermute x1, starting transfers between devices, per_device(): mid_near = lax.ppermute(edge(volume, is_even), y_axes, near_perm)  1.38 us
  transfers between devices with their start and end apart: 8, of which 2 were waited for; matrix products, arithmetic and copies ran while one was open for 2% of the time, Pallas kernels for 1%

profile of v7, /device:TPU:1, one launch (start us, length us, event | category | flops | bytes accessed | tf_op | source)
XLA Modules:
  0.0 67.2 jit_solution(16439552572305790588)
XLA Ops:
  0.0 0.0 copy-start
  0.0 0.0 copy-start.2
  0.0 0.0 copy-start.1
  0.0 6.4 %collective-permute-start = (f32[24,32,128]{2,1,0:T(8,128)}, f32[24,32,128]{2,1,0:T(8,128)S(1)}, u32[]{:S(2)}, u32[]{:S(2)}) collective-permute-start(f32[24,32,128]{2,1,0:T(8,128)} %mid), channel_id=1, source_target_pairs={{32,64},{96,128},{160,192},{64,32},{128,96},{192,160},{33,65},{97,... | collective-permute-start | bytes 1179656 | tf_op jit(solution)/shard_map/ppermute | solution.py:311
  6.4 1.1 %slice_select_fusion.2 = (f32[24,24,128]{2,1,0:T(8,128)S(1)}, f32[24,24,128]{2,1,0:T(8,128)S(1)}) fusion(f32[24,32,128]{2,1,0:T(8,128)} %mid, pred[]{:T(512)S(6)} %eq.7, pred[]{:T(512)S(6)} %eq.6), kind=kLoop, calls=%fused_computation.2 | loop fusion | flops 147456 | bytes 1179650 | tf_op jit(solution)/shard_map/jit(_where)/select_n | solution.py:309
  7.6 1.4 %collective-permute-start.5 = (f32[24,24,128]{2,1,0:T(8,128)S(1)}, f32[24,24,128]{2,1,0:T(8,128)S(1)}, u32[]{:S(2)}, u32[]{:S(2)}) collective-permute-start(f32[24,24,128]{2,1,0:T(8,128)S(1)} %get-tuple-element.31), channel_id=1, source_target_pairs={{0,1},{1,0},{2,3},{3,2},{4,5},{5,4},{6,7},{7,6},{8,9},{9,8},{10,11... | collective-permute-start | bytes 884744 | tf_op jit(solution)/shard_map/ppermute | solution.py:313
  8.9 0.7 collective-permute-start.4
  9.6 0.1 collective-permute-start.3
  9.7 6.6 %collective-permute-done.far = f32[24,32,128]{2,1,0:T(8,128)S(1)} collective-permute-done((f32[24,32,128]{2,1,0:T(8,128)}, f32[24,32,128]{2,1,0:T(8,128)S(1)}, u32[]{:S(2)}, u32[]{:S(2)}) %collective-permute-start) | collective-permute-done | bytes 393248 | tf_op jit(solution)/shard_map/ppermute | solution.py:311
  16.4 0.7 %collective-permute-start.2 = (f32[24,24,128]{2,1,0:T(8,128)S(1)}, f32[24,24,128]{2,1,0:T(8,128)S(1)}, u32[]{:S(2)}, u32[]{:S(2)}) collective-permute-start(f32[24,24,128]{2,1,0:T(8,128)S(1)} %get-tuple-element.33), channel_id=1, source_target_pairs={{1,2},{3,4},{5,6},{7,8},{9,10},{11,12},{13,14},{15,16},{17,18},{19... | collective-permute-start | bytes 884744 | tf_op jit(solution)/shard_map/ppermute | solution.py:317
  17.1 3.9 %collective-permute-start.1 = (f32[24,24,128]{2,1,0:T(8,128)S(1)}, f32[24,24,128]{2,1,0:T(8,128)S(1)}, u32[]{:S(2)}, u32[]{:S(2)}) collective-permute-start(f32[24,24,128]{2,1,0:T(8,128)S(1)} %get-tuple-element.34), channel_id=1, source_target_pairs={{0,1},{1,0},{2,3},{3,2},{4,5},{5,4},{6,7},{7,6},{8,9},{9,8},{10,11... | collective-permute-start | bytes 884744 | tf_op jit(solution)/shard_map/ppermute | solution.py:318
  21.0 0.0 collective-permute-done.5.mid_near
  21.0 0.0 collective-permute-done.4.mid_wrap
  21.0 0.0 collective-permute-start.6
  21.0 0.5 collective-permute-start.7
  21.5 0.0 copy-done
  21.5 0.0 copy-done.2
  21.5 0.0 copy-done.1
  21.5 0.0 copy-start.3
  21.5 0.9 %copy-done.3 = bf16[384,256]{1,0:T(8,128)(2,1)S(1)} copy-done((bf16[384,256]{1,0:T(8,128)(2,1)S(1)}, bf16[384,256]{1,0:T(8,128)(2,1)}, u32[]{:S(2)}) %copy-start.3) | copy-done | bytes 196632
  22.4 0.0 copy-start.4
  22.4 0.8 %shard_map.46 = (f32[2496,128]{1,0:T(8,128)S(1)}, f32[2496,128]{1,0:T(8,128)S(1)}, f32[2496,128]{1,0:T(8,128)S(1)}, f32[2496,128]{1,0:T(8,128)S(1)}) custom-call(s32[1]{0:T(128)} %bitcast.1.odd_ref, f32[24,32,128]{2,1,0:T(8,128)S(1)} %copy-done.1, bf16[384,256]{1,0:T(8,128)(2,1)S(1)} %copy-done.3, bf16[2,4,72,256]{3,2,1,0:T(8,128)(2,1)S(1)} %copy-done.2, ...), custom_call_target="tpu_custom_call" | custom-call | tf_op jit(solution)/shard_map/pallas_call | solution.py:246
  23.2 0.0 collective-permute-done.3.pair
  23.2 0.0 collective-permute-done.2.far_wrap
  23.2 1.8 %collective-permute-done.1.far_near = f32[24,24,128]{2,1,0:T(8,128)S(1)} collective-permute-done((f32[24,24,128]{2,1,0:T(8,128)S(1)}, f32[24,24,128]{2,1,0:T(8,128)S(1)}, u32[]{:S(2)}, u32[]{:S(2)}) %collective-permute-start.1) | collective-permute-done | bytes 294944 | tf_op jit(solution)/shard_map/ppermute | solution.py:318
  25.1 0.0 collective-permute-done.6.pair_near
  25.1 0.0 collective-permute-done.7.pair_wrap
  25.1 0.0 copy-done.4
  25.1 7.8 %shard_map.47 = (f32[12,768,128]{2,1,0:T(8,128)S(1)}, f32[1,128]{1,0:T(1,128)S(1)}) custom-call(s32[1]{0:T(128)} %bitcast.core_ref, s32[1]{0:T(128)} %bitcast.1.odd_ref, bf16[384,256]{1,0:T(8,128)(2,1)S(1)} %copy-done.4, bf16[2,4,72,256]{3,2,1,0:T(8,128)(2,1)S(1)} %copy-done.2, bf16[12,256,256]{2,1,0:T(8,128)(2,1)S(1)} %copy-done, ...), custom_call_target="tpu_custom_call" | custom-call | tf_op jit(solution)/shard_map/pallas_call | solution.py:257
  32.9 0.1 broadcast_in_dim.9
  33.0 32.4 %all_to_all.5 = f32[256,1,128]{2,1,0:T(1,128)S(1)} all-to-all(f32[256,1,128]{2,1,0:T(1,128)S(1)} %broadcast_in_dim.9), channel_id=1, replica_groups=mesh['zh'=4,'core'=2,'x'=4,'zl'=2,'y'=4] {'zh','core','x','zl','y'}, dimensions={0} | all-to-all | bytes 262144 | tf_op jit(solution)/shard_map/all_to_all | solution.py:290
  65.4 1.8 %shard_map.48 = f32[24,32,128]{2,1,0:T(8,128)} custom-call(f32[12,768,128]{2,1,0:T(8,128)S(1)} %get-tuple-element.29.stats, f32[256,128]{1,0:T(8,128)S(1)} %bitcast.4), custom_call_target="tpu_custom_call" | custom-call | tf_op jit(solution)/shard_map/pallas_call | solution.py:275
  (1 shorter events, 0.0 us)
Async XLA Ops:
  0.0 21.5 %copy-start = (bf16[12,256,256]{2,1,0:T(8,128)(2,1)S(1)}, bf16[12,256,256]{2,1,0:T(8,128)(2,1)}, u32[]{:S(2)}) copy-start(bf16[12,256,256]{2,1,0:T(8,128)(2,1)} %constant.22.clone.wz) | copy-start | bytes 4718596
  0.0 21.5 %copy-start.2 = (bf16[2,4,72,256]{3,2,1,0:T(8,128)(2,1)S(1)}, bf16[2,4,72,256]{3,2,1,0:T(8,128)(2,1)}, u32[]{:S(2)}) copy-start(bf16[2,4,72,256]{3,2,1,0:T(8,128)(2,1)} %constant.21.clone.wx) | copy-start | bytes 884740
  0.0 21.5 %copy-start.1 = (f32[24,32,128]{2,1,0:T(8,128)S(1)}, f32[24,32,128]{2,1,0:T(8,128)}, u32[]{:S(2)}) copy-start(f32[24,32,128]{2,1,0:T(8,128)} %mid) | copy-start | bytes 1179652
  0.0 16.3 %collective-permute-start = (f32[24,32,128]{2,1,0:T(8,128)}, f32[24,32,128]{2,1,0:T(8,128)S(1)}, u32[]{:S(2)}, u32[]{:S(2)}) collective-permute-start(f32[24,32,128]{2,1,0:T(8,128)} %mid), channel_id=1, source_target_pairs={{32,64},{96,128},{160,192},{64,32},{128,96},{192,160},{33,65},{97,... | collective-permute-start | bytes 1179656 | tf_op jit(solution)/shard_map/ppermute | solution.py:311
  7.6 13.4 %collective-permute-start.5 = (f32[24,24,128]{2,1,0:T(8,128)S(1)}, f32[24,24,128]{2,1,0:T(8,128)S(1)}, u32[]{:S(2)}, u32[]{:S(2)}) collective-permute-start(f32[24,24,128]{2,1,0:T(8,128)S(1)} %get-tuple-element.31), channel_id=1, source_target_pairs={{0,1},{1,0},{2,3},{3,2},{4,5},{5,4},{6,7},{7,6},{8,9},{9,8},{10,11... | collective-permute-start | bytes 884744 | tf_op jit(solution)/shard_map/ppermute | solution.py:313
  8.9 12.0 %collective-permute-start.4 = (f32[24,24,128]{2,1,0:T(8,128)S(1)}, f32[24,24,128]{2,1,0:T(8,128)S(1)}, u32[]{:S(2)}, u32[]{:S(2)}) collective-permute-start(f32[24,24,128]{2,1,0:T(8,128)S(1)} %get-tuple-element.32), channel_id=1, source_target_pairs={{1,2},{3,4},{5,6},{7,8},{9,10},{11,12},{13,14},{15,16},{17,18},{19... | collective-permute-start | bytes 884744 | tf_op jit(solution)/shard_map/ppermute | solution.py:312
  9.6 13.6 %collective-permute-start.3 = (f32[24,32,128]{2,1,0:T(8,128)}, f32[24,32,128]{2,1,0:T(8,128)S(1)}, u32[]{:S(2)}, u32[]{:S(2)}) collective-permute-start(f32[24,32,128]{2,1,0:T(8,128)} %mid), channel_id=1, source_target_pairs={{0,32},{32,0},{64,96},{96,64},{128,160},{160,128},{192,224},{224,1... | collective-permute-start | bytes 1179656 | tf_op jit(solution)/shard_map/ppermute | solution.py:314
  16.4 6.9 %collective-permute-start.2 = (f32[24,24,128]{2,1,0:T(8,128)S(1)}, f32[24,24,128]{2,1,0:T(8,128)S(1)}, u32[]{:S(2)}, u32[]{:S(2)}) collective-permute-start(f32[24,24,128]{2,1,0:T(8,128)S(1)} %get-tuple-element.33), channel_id=1, source_target_pairs={{1,2},{3,4},{5,6},{7,8},{9,10},{11,12},{13,14},{15,16},{17,18},{19... | collective-permute-start | bytes 884744 | tf_op jit(solution)/shard_map/ppermute | solution.py:317
  17.1 8.0 %collective-permute-start.1 = (f32[24,24,128]{2,1,0:T(8,128)S(1)}, f32[24,24,128]{2,1,0:T(8,128)S(1)}, u32[]{:S(2)}, u32[]{:S(2)}) collective-permute-start(f32[24,24,128]{2,1,0:T(8,128)S(1)} %get-tuple-element.34), channel_id=1, source_target_pairs={{0,1},{1,0},{2,3},{3,2},{4,5},{5,4},{6,7},{7,6},{8,9},{9,8},{10,11... | collective-permute-start | bytes 884744 | tf_op jit(solution)/shard_map/ppermute | solution.py:318
  21.0 4.1 %collective-permute-start.6 = (f32[24,24,128]{2,1,0:T(8,128)S(1)}, f32[24,24,128]{2,1,0:T(8,128)S(1)}, u32[]{:S(2)}, u32[]{:S(2)}) collective-permute-start(f32[24,24,128]{2,1,0:T(8,128)S(1)} %collective-permute-done.5.mid_near), channel_id=1, source_target_pairs={{0,32},{32,0},{64,96},{96,64},{128,160},{160,128},{192,224},{224,1... | collective-permute-start | bytes 884744 | tf_op jit(solution)/shard_map/ppermute | solution.py:321
  21.0 4.1 %collective-permute-start.7 = (f32[24,24,128]{2,1,0:T(8,128)S(1)}, f32[24,24,128]{2,1,0:T(8,128)S(1)}, u32[]{:S(2)}, u32[]{:S(2)}) collective-permute-start(f32[24,24,128]{2,1,0:T(8,128)S(1)} %collective-permute-done.4.mid_wrap), channel_id=1, source_target_pairs={{0,32},{32,0},{64,96},{96,64},{128,160},{160,128},{192,224},{224,1... | collective-permute-start | bytes 884744 | tf_op jit(solution)/shard_map/ppermute | solution.py:322
  21.5 0.9 %copy-start.3 = (bf16[384,256]{1,0:T(8,128)(2,1)S(1)}, bf16[384,256]{1,0:T(8,128)(2,1)}, u32[]{:S(2)}) copy-start(bf16[384,256]{1,0:T(8,128)(2,1)} %constant.20.clone.wy) | copy-start | bytes 589828
  22.4 2.7 %copy-start.4 = (bf16[384,256]{1,0:T(8,128)(2,1)S(1)}, bf16[384,256]{1,0:T(8,128)(2,1)}, u32[]{:S(2)}) copy-start(bf16[384,256]{1,0:T(8,128)(2,1)} %constant.20.clone.wy) | copy-start | bytes 589828

commit v8 on v6

--- a/solution.py
+++ b/solution.py
@@ -197,16 +197,18 @@
     peak_row = jnp.zeros((1, depth), jnp.float32)
     blocks = rows // z_rows
     steps = tile_y // 2 // blocks
-    for level in range(5):
+    done = None
+    for level in (3, 2, 1, 0, None):
         best = jnp.zeros((8, depth), jnp.float32)
         for c in range(blocks):
-            if level < 4:
+            if level is not None:
                 for yp in range(steps * c, steps * (c + 1)):
                     x_step(level, yp)
-            if level > 0:
-                best = z_step(level - 1, c, best)
-        if level > 0:
-            peak_row = jnp.where(lane == level - 1, jnp.max(best), peak_row)
+            if done is not None:
+                best = z_step(done, c, best)
+        if done is not None:
+            peak_row = jnp.where(lane == done, jnp.max(best), peak_row)
+        done = level
     peaks[...] = peak_row
 
 

time: 67.2 us -> 67.2 us (level)
  no operation moved by 1% of the time
where the time goes in v8:
time: 67.2 us; the launch traced here: 67 us
  blocking collectives  32.4 us (48%)
  starting transfers between devices  13.7 us (20%)
  Pallas kernels  10.1 us (15%)
  waiting for transfers between devices  8.46 us (13%)
  other arithmetic  1.14 us (2%)
  local copies, waits for them, and re-layouts  1.01 us (2%)
    all_to_all x1, blocking collectives, all_peaks(): return lax.all_to_all(spread, axes, 0, 0, tiled=True).reshape(peers, depth)  32.4 us
    pallas_call x1, Pallas kernels, late_call(): pl.pallas_call(late_kernel, out_shape=(jax.ShapeDtypeStruct((12, rows, de...  7.59 us
    ppermute x1, waiting for transfers between devices, per_device(): far = lax.ppermute(volume, x_axes, far_perm)  6.6 us
    ppermute x1, starting transfers between devices, per_device(): far = lax.ppermute(volume, x_axes, far_perm)  6.42 us
    ppermute x1, starting transfers between devices, per_device(): far_near = lax.ppermute(far_near, y_axes, near_perm)  3.91 us
    ppermute x1, waiting for transfers between devices, per_device(): far_near = lax.ppermute(far_near, y_axes, near_perm)  1.84 us
    pallas_call x1, Pallas kernels, score_call(): pl.pallas_call(score_kernel, out_shape=jax.ShapeDtypeStruct((tile_x, tile...  1.78 us
    ppermute x1, starting transfers between devices, per_device(): mid_near = lax.ppermute(edge(volume, is_even), y_axes, near_perm)  1.38 us
  transfers between devices with their start and end apart: 8, of which 2 were waited for; matrix products, arithmetic and copies ran while one was open for 2% of the time, Pallas kernels for 1%

profile of v8, /device:TPU:1, one launch (start us, length us, event | category | flops | bytes accessed | tf_op | source)
XLA Modules:
  0.0 67.0 jit_solution(15342152259231391294)
XLA Ops:
  0.0 0.0 copy-start
  0.0 0.0 copy-start.2
  0.0 0.0 copy-start.1
  0.0 6.4 %collective-permute-start = (f32[24,32,128]{2,1,0:T(8,128)}, f32[24,32,128]{2,1,0:T(8,128)S(1)}, u32[]{:S(2)}, u32[]{:S(2)}) collective-permute-start(f32[24,32,128]{2,1,0:T(8,128)} %mid), channel_id=1, source_target_pairs={{32,64},{96,128},{160,192},{64,32},{128,96},{192,160},{33,65},{97,... | collective-permute-start | bytes 1179656 | tf_op jit(solution)/shard_map/ppermute | solution.py:313
  6.4 1.1 %slice_select_fusion.2 = (f32[24,24,128]{2,1,0:T(8,128)S(1)}, f32[24,24,128]{2,1,0:T(8,128)S(1)}) fusion(f32[24,32,128]{2,1,0:T(8,128)} %mid, pred[]{:T(512)S(6)} %eq.7, pred[]{:T(512)S(6)} %eq.6), kind=kLoop, calls=%fused_computation.2 | loop fusion | flops 147456 | bytes 1179650 | tf_op jit(solution)/shard_map/jit(_where)/select_n | solution.py:311
  7.6 1.4 %collective-permute-start.5 = (f32[24,24,128]{2,1,0:T(8,128)S(1)}, f32[24,24,128]{2,1,0:T(8,128)S(1)}, u32[]{:S(2)}, u32[]{:S(2)}) collective-permute-start(f32[24,24,128]{2,1,0:T(8,128)S(1)} %get-tuple-element.31), channel_id=1, source_target_pairs={{0,1},{1,0},{2,3},{3,2},{4,5},{5,4},{6,7},{7,6},{8,9},{9,8},{10,11... | collective-permute-start | bytes 884744 | tf_op jit(solution)/shard_map/ppermute | solution.py:315
  8.9 0.7 collective-permute-start.4
  9.6 0.1 collective-permute-start.3
  9.7 6.6 %collective-permute-done.far = f32[24,32,128]{2,1,0:T(8,128)S(1)} collective-permute-done((f32[24,32,128]{2,1,0:T(8,128)}, f32[24,32,128]{2,1,0:T(8,128)S(1)}, u32[]{:S(2)}, u32[]{:S(2)}) %collective-permute-start) | collective-permute-done | bytes 393248 | tf_op jit(solution)/shard_map/ppermute | solution.py:313
  16.4 0.7 %collective-permute-start.2 = (f32[24,24,128]{2,1,0:T(8,128)S(1)}, f32[24,24,128]{2,1,0:T(8,128)S(1)}, u32[]{:S(2)}, u32[]{:S(2)}) collective-permute-start(f32[24,24,128]{2,1,0:T(8,128)S(1)} %get-tuple-element.33), channel_id=1, source_target_pairs={{1,2},{3,4},{5,6},{7,8},{9,10},{11,12},{13,14},{15,16},{17,18},{19... | collective-permute-start | bytes 884744 | tf_op jit(solution)/shard_map/ppermute | solution.py:319
  17.1 3.9 %collective-permute-start.1 = (f32[24,24,128]{2,1,0:T(8,128)S(1)}, f32[24,24,128]{2,1,0:T(8,128)S(1)}, u32[]{:S(2)}, u32[]{:S(2)}) collective-permute-start(f32[24,24,128]{2,1,0:T(8,128)S(1)} %get-tuple-element.34), channel_id=1, source_target_pairs={{0,1},{1,0},{2,3},{3,2},{4,5},{5,4},{6,7},{7,6},{8,9},{9,8},{10,11... | collective-permute-start | bytes 884744 | tf_op jit(solution)/shard_map/ppermute | solution.py:320
  21.0 0.0 collective-permute-done.5.mid_near
  21.0 0.0 collective-permute-done.4.mid_wrap
  21.0 0.0 collective-permute-start.6
  21.0 0.5 collective-permute-start.7
  21.5 0.0 copy-done
  21.5 0.0 copy-done.2
  21.5 0.0 copy-done.1
  21.5 0.0 copy-start.3
  21.5 0.9 %copy-done.3 = bf16[384,256]{1,0:T(8,128)(2,1)S(1)} copy-done((bf16[384,256]{1,0:T(8,128)(2,1)S(1)}, bf16[384,256]{1,0:T(8,128)(2,1)}, u32[]{:S(2)}) %copy-start.3) | copy-done | bytes 196632
  22.4 0.0 copy-start.4
  22.4 0.8 %shard_map.46 = (f32[2496,128]{1,0:T(8,128)S(1)}, f32[2496,128]{1,0:T(8,128)S(1)}, f32[2496,128]{1,0:T(8,128)S(1)}, f32[2496,128]{1,0:T(8,128)S(1)}) custom-call(s32[1]{0:T(128)} %bitcast.1.odd_ref, f32[24,32,128]{2,1,0:T(8,128)S(1)} %copy-done.1, bf16[384,256]{1,0:T(8,128)(2,1)S(1)} %copy-done.3, bf16[2,4,72,256]{3,2,1,0:T(8,128)(2,1)S(1)} %copy-done.2, ...), custom_call_target="tpu_custom_call" | custom-call | tf_op jit(solution)/shard_map/pallas_call | solution.py:248
  23.2 0.0 collective-permute-done.3.pair
  23.2 0.0 collective-permute-done.2.far_wrap
  23.2 1.8 %collective-permute-done.1.far_near = f32[24,24,128]{2,1,0:T(8,128)S(1)} collective-permute-done((f32[24,24,128]{2,1,0:T(8,128)S(1)}, f32[24,24,128]{2,1,0:T(8,128)S(1)}, u32[]{:S(2)}, u32[]{:S(2)}) %collective-permute-start.1) | collective-permute-done | bytes 294944 | tf_op jit(solution)/shard_map/ppermute | solution.py:320
  25.1 0.0 collective-permute-done.6.pair_near
  25.1 0.0 collective-permute-done.7.pair_wrap
  25.1 0.0 copy-done.4
  25.1 7.6 %shard_map.47 = (f32[12,768,128]{2,1,0:T(8,128)S(1)}, f32[1,128]{1,0:T(1,128)S(1)}) custom-call(s32[1]{0:T(128)} %bitcast.core_ref, s32[1]{0:T(128)} %bitcast.1.odd_ref, bf16[384,256]{1,0:T(8,128)(2,1)S(1)} %copy-done.4, bf16[2,4,72,256]{3,2,1,0:T(8,128)(2,1)S(1)} %copy-done.2, bf16[12,256,256]{2,1,0:T(8,128)(2,1)S(1)} %copy-done, ...), custom_call_target="tpu_custom_call" | custom-call | tf_op jit(solution)/shard_map/pallas_call | solution.py:259
  32.7 0.1 broadcast_in_dim.9
  32.8 32.4 %all_to_all.5 = f32[256,1,128]{2,1,0:T(1,128)S(1)} all-to-all(f32[256,1,128]{2,1,0:T(1,128)S(1)} %broadcast_in_dim.9), channel_id=1, replica_groups=mesh['zh'=4,'core'=2,'x'=4,'zl'=2,'y'=4] {'zh','core','x','zl','y'}, dimensions={0} | all-to-all | bytes 262144 | tf_op jit(solution)/shard_map/all_to_all | solution.py:292
  65.2 1.8 %shard_map.48 = f32[24,32,128]{2,1,0:T(8,128)} custom-call(f32[12,768,128]{2,1,0:T(8,128)S(1)} %get-tuple-element.29.stats, f32[256,128]{1,0:T(8,128)S(1)} %bitcast.4), custom_call_target="tpu_custom_call" | custom-call | tf_op jit(solution)/shard_map/pallas_call | solution.py:277
  (1 shorter events, 0.0 us)
Async XLA Ops:
  0.0 21.5 %copy-start = (bf16[12,256,256]{2,1,0:T(8,128)(2,1)S(1)}, bf16[12,256,256]{2,1,0:T(8,128)(2,1)}, u32[]{:S(2)}) copy-start(bf16[12,256,256]{2,1,0:T(8,128)(2,1)} %constant.22.clone.wz) | copy-start | bytes 4718596
  0.0 21.5 %copy-start.2 = (bf16[2,4,72,256]{3,2,1,0:T(8,128)(2,1)S(1)}, bf16[2,4,72,256]{3,2,1,0:T(8,128)(2,1)}, u32[]{:S(2)}) copy-start(bf16[2,4,72,256]{3,2,1,0:T(8,128)(2,1)} %constant.21.clone.wx) | copy-start | bytes 884740
  0.0 21.5 %copy-start.1 = (f32[24,32,128]{2,1,0:T(8,128)S(1)}, f32[24,32,128]{2,1,0:T(8,128)}, u32[]{:S(2)}) copy-start(f32[24,32,128]{2,1,0:T(8,128)} %mid) | copy-start | bytes 1179652
  0.0 16.3 %collective-permute-start = (f32[24,32,128]{2,1,0:T(8,128)}, f32[24,32,128]{2,1,0:T(8,128)S(1)}, u32[]{:S(2)}, u32[]{:S(2)}) collective-permute-start(f32[24,32,128]{2,1,0:T(8,128)} %mid), channel_id=1, source_target_pairs={{32,64},{96,128},{160,192},{64,32},{128,96},{192,160},{33,65},{97,... | collective-permute-start | bytes 1179656 | tf_op jit(solution)/shard_map/ppermute | solution.py:313
  7.6 13.4 %collective-permute-start.5 = (f32[24,24,128]{2,1,0:T(8,128)S(1)}, f32[24,24,128]{2,1,0:T(8,128)S(1)}, u32[]{:S(2)}, u32[]{:S(2)}) collective-permute-start(f32[24,24,128]{2,1,0:T(8,128)S(1)} %get-tuple-element.31), channel_id=1, source_target_pairs={{0,1},{1,0},{2,3},{3,2},{4,5},{5,4},{6,7},{7,6},{8,9},{9,8},{10,11... | collective-permute-start | bytes 884744 | tf_op jit(solution)/shard_map/ppermute | solution.py:315
  8.9 12.0 %collective-permute-start.4 = (f32[24,24,128]{2,1,0:T(8,128)S(1)}, f32[24,24,128]{2,1,0:T(8,128)S(1)}, u32[]{:S(2)}, u32[]{:S(2)}) collective-permute-start(f32[24,24,128]{2,1,0:T(8,128)S(1)} %get-tuple-element.32), channel_id=1, source_target_pairs={{1,2},{3,4},{5,6},{7,8},{9,10},{11,12},{13,14},{15,16},{17,18},{19... | collective-permute-start | bytes 884744 | tf_op jit(solution)/shard_map/ppermute | solution.py:314
  9.6 13.6 %collective-permute-start.3 = (f32[24,32,128]{2,1,0:T(8,128)}, f32[24,32,128]{2,1,0:T(8,128)S(1)}, u32[]{:S(2)}, u32[]{:S(2)}) collective-permute-start(f32[24,32,128]{2,1,0:T(8,128)} %mid), channel_id=1, source_target_pairs={{0,32},{32,0},{64,96},{96,64},{128,160},{160,128},{192,224},{224,1... | collective-permute-start | bytes 1179656 | tf_op jit(solution)/shard_map/ppermute | solution.py:316
  16.4 6.9 %collective-permute-start.2 = (f32[24,24,128]{2,1,0:T(8,128)S(1)}, f32[24,24,128]{2,1,0:T(8,128)S(1)}, u32[]{:S(2)}, u32[]{:S(2)}) collective-permute-start(f32[24,24,128]{2,1,0:T(8,128)S(1)} %get-tuple-element.33), channel_id=1, source_target_pairs={{1,2},{3,4},{5,6},{7,8},{9,10},{11,12},{13,14},{15,16},{17,18},{19... | collective-permute-start | bytes 884744 | tf_op jit(solution)/shard_map/ppermute | solution.py:319
  17.1 8.0 %collective-permute-start.1 = (f32[24,24,128]{2,1,0:T(8,128)S(1)}, f32[24,24,128]{2,1,0:T(8,128)S(1)}, u32[]{:S(2)}, u32[]{:S(2)}) collective-permute-start(f32[24,24,128]{2,1,0:T(8,128)S(1)} %get-tuple-element.34), channel_id=1, source_target_pairs={{0,1},{1,0},{2,3},{3,2},{4,5},{5,4},{6,7},{7,6},{8,9},{9,8},{10,11... | collective-permute-start | bytes 884744 | tf_op jit(solution)/shard_map/ppermute | solution.py:320
  21.0 4.1 %collective-permute-start.6 = (f32[24,24,128]{2,1,0:T(8,128)S(1)}, f32[24,24,128]{2,1,0:T(8,128)S(1)}, u32[]{:S(2)}, u32[]{:S(2)}) collective-permute-start(f32[24,24,128]{2,1,0:T(8,128)S(1)} %collective-permute-done.5.mid_near), channel_id=1, source_target_pairs={{0,32},{32,0},{64,96},{96,64},{128,160},{160,128},{192,224},{224,1... | collective-permute-start | bytes 884744 | tf_op jit(solution)/shard_map/ppermute | solution.py:323
  21.0 4.1 %collective-permute-start.7 = (f32[24,24,128]{2,1,0:T(8,128)S(1)}, f32[24,24,128]{2,1,0:T(8,128)S(1)}, u32[]{:S(2)}, u32[]{:S(2)}) collective-permute-start(f32[24,24,128]{2,1,0:T(8,128)S(1)} %collective-permute-done.4.mid_wrap), channel_id=1, source_target_pairs={{0,32},{32,0},{64,96},{96,64},{128,160},{160,128},{192,224},{224,1... | collective-permute-start | bytes 884744 | tf_op jit(solution)/shard_map/ppermute | solution.py:324
  21.5 0.9 %copy-start.3 = (bf16[384,256]{1,0:T(8,128)(2,1)S(1)}, bf16[384,256]{1,0:T(8,128)(2,1)}, u32[]{:S(2)}) copy-start(bf16[384,256]{1,0:T(8,128)(2,1)} %constant.20.clone.wy) | copy-start | bytes 589828
  22.4 2.7 %copy-start.4 = (bf16[384,256]{1,0:T(8,128)(2,1)S(1)}, bf16[384,256]{1,0:T(8,128)(2,1)}, u32[]{:S(2)}) copy-start(bf16[384,256]{1,0:T(8,128)(2,1)} %constant.20.clone.wy) | copy-start | bytes 589828
